TPU v7x, 32 devices: a whole 2x2x4 slice. The times are simulated.
32 devices in a mesh: narrow: 8 (over z, core), wide: 4 (over y, x).
Axes of the slice: x: 2, y: 2, z: 4, core: 2. Of those that a mesh axis runs over, the one named last changes fastest.
Arguments:
- inputs: bfloat16 [1024, 8192], P('narrow', 'wide'), may hold values from -6 to 6
- gate_blocks: bfloat16 [112, 16, 128, 128], P('wide', 'narrow'), may hold values from -0.125 to 0.125
- up_blocks: bfloat16 [112, 16, 128, 128], P('wide', 'narrow'), may hold values from -0.125 to 0.125
- pattern: int32 [112, 16], P('wide'), may hold values from 0 to 63, as said below
- grad_hidden: bfloat16 [1024, 14336], P('narrow', 'wide'), may hold values from -0.59765625 to 0.59765625
Outputs:
- hidden: bfloat16 [1024, 14336], P('narrow', 'wide')
- grad_inputs: bfloat16 [1024, 8192], P('narrow', 'wide')
- grad_gate: bfloat16 [112, 16, 128, 128], P('wide', 'narrow')
- grad_up: bfloat16 [112, 16, 128, 128], P('wide', 'narrow')
Inputs may be any that keep to these rules, and one draw needn't show every extreme that they name: pattern[j, k] = b_j XOR m_k, with one offset b_j for each block column and 16 distinct masks m_k common to all block columns, so each block column lists 16 distinct block rows.
All inputs are finite; a program needn't handle non-finite values.
Results may differ from a plain program's by a relative error of at most 0.023.
Values may be sent and summed in bfloat16 or wider, within the bound.
No kernel may reach another device: no remote copies, remote signals or barrier semaphores. Data moves between devices by JAX's collectives and lax.ppermute only.
A program may use at most 192 MiB of HBM per device.

v0:
```python
import jax
import jax.numpy as jnp
from jax import lax
from jax.sharding import PartitionSpec as P


def silu_parts(gate_sum):
    sigmoid_value = jax.nn.sigmoid(gate_sum)
    return (gate_sum * sigmoid_value, sigmoid_value * (1.0 + gate_sum * (1.0 - sigmoid_value)))


def shards(inputs, gate_blocks, up_blocks, pattern, grad_hidden):
    tokens_here = inputs.shape[0]
    block_size = gate_blocks.shape[2]
    columns = gate_blocks.shape[0]
    full_inputs = lax.all_gather(inputs, "wide", axis=1, tiled=True)
    row_blocks = full_inputs.shape[1] // block_size
    input_blocks = full_inputs.reshape(tokens_here, row_blocks, block_size)

    def picks_for():
        return jnp.take(input_blocks, pattern, axis=1)

    gate_all, up_all = (
        lax.all_gather(gate_blocks, "narrow", axis=1, tiled=True),
        lax.all_gather(up_blocks, "narrow", axis=1, tiled=True),
    )
    pieces = (gate_all, up_all)
    picked = picks_for()
    gate_sum = jnp.einsum("tjkb,jkbc->tjc", picked, pieces[0], preferred_element_type=jnp.float32)
    up_sum = jnp.einsum("tjkb,jkbc->tjc", picked, pieces[1], preferred_element_type=jnp.float32)
    gate_sum, up_sum = (gate_sum, up_sum)
    activation, derivative = silu_parts(gate_sum)
    hidden = (activation * up_sum).astype(jnp.bfloat16)
    cotangent = grad_hidden.reshape(tokens_here, columns, block_size).astype(jnp.float32)
    d_gate = (cotangent * up_sum * derivative).astype(jnp.bfloat16)
    d_up = (cotangent * activation).astype(jnp.bfloat16)
    zero_inputs = jnp.zeros((tokens_here, row_blocks, block_size), jnp.float32)
    pieces = (gate_all, up_all)
    number_slots = pieces[0].shape[1]

    def one_slot(k, running):
        gate_slot = lax.dynamic_index_in_dim(pieces[0], k, 1, keepdims=False)
        up_slot = lax.dynamic_index_in_dim(pieces[1], k, 1, keepdims=False)
        contribution = jnp.einsum(
            "tjc,jbc->tjb", d_gate, gate_slot, preferred_element_type=jnp.float32
        )
        contribution = contribution + jnp.einsum(
            "tjc,jbc->tjb", d_up, up_slot, preferred_element_type=jnp.float32
        )
        targets = lax.dynamic_index_in_dim(pattern, k, 1, keepdims=False)
        return running.at[:, targets].add(contribution)

    partial_inputs = lax.fori_loop(0, number_slots, one_slot, zero_inputs)
    grad_inputs = lax.psum_scatter(
        partial_inputs.reshape(tokens_here, row_blocks * block_size).astype(jnp.bfloat16),
        "wide",
        scatter_dimension=1,
        tiled=True,
    )
    picked_all = picks_for()
    gate_terms = jnp.einsum(
        "tjkb,tjc->jkbc", picked_all, d_gate, preferred_element_type=jnp.float32
    )
    up_terms = jnp.einsum("tjkb,tjc->jkbc", picked_all, d_up, preferred_element_type=jnp.float32)
    grad_gate, grad_up = (
        lax.psum_scatter(
            gate_terms.astype(jnp.bfloat16), "narrow", scatter_dimension=1, tiled=True
        ).astype(jnp.float32),
        lax.psum_scatter(
            up_terms.astype(jnp.bfloat16), "narrow", scatter_dimension=1, tiled=True
        ).astype(jnp.float32),
    )
    return (
        hidden.reshape(tokens_here, columns * block_size),
        grad_inputs,
        grad_gate.astype(jnp.bfloat16),
        grad_up.astype(jnp.bfloat16),
    )


def solution(mesh):
    placed = (
        P("narrow", "wide"),
        P("wide", "narrow", None, None),
        P("wide", "narrow", None, None),
        P("wide", None),
        P("narrow", "wide"),
    )
    return jax.shard_map(
        shards,
        mesh=mesh,
        in_specs=placed,
        out_specs=(
            P("narrow", "wide"),
            P("narrow", "wide"),
            P("wide", "narrow", None, None),
            P("wide", "narrow", None, None),
        ),
        check_vma=False,
    )
```

profile of v0, /device:TPU:0, one launch (start us, length us, event | category | flops | bytes accessed | tf_op | source)
XLA Modules:
  0.0 966.7 jit_solution(5343642789117696766)
XLA Ops:
  7.2 2.2 copy.63
  9.5 3.8 copy.69
  13.4 2.4 copy.67
  17.7 30.8 %all-gather.4.cloned.1.call-done = bf16[128,8192]{0,1:T(8,128)(2,1)} async-done(((bf16[128,2048]{0,1:T(8,128)(2,1)}), bf16[128,8192]{0,1:T(8,128)(2,1)}) %all-gather.4.cloned.1.call-update) | async-done | bytes 2097168 | tf_op jit(solution)/shard_map/all_gather | solution.py:16
  48.5 3.2 copy.65
  51.7 13.4 %gather_fusion = bf16[448,128,128]{2,1,0:T(8,128)(2,1)} fusion(bf16[128,64,128]{2,0,1:T(8,128)(2,1)S(1)} %copy.65, s32[1024]{0:T(1024)S(1)} %pad_clamp_fusion), kind=kCustom, calls=%fused_computation.clone | custom fusion | bytes 29361920 | tf_op jit(solution)/shard_map/jit(_take)/gather | solution.py:21
  65.1 20.4 %copy.66 = bf16[28,16,128,128]{2,3,1,0:T(8,128)(2,1)} copy(bf16[28,16,128,128]{3,2,1,0:T(8,128)(2,1)} %bitcast.114) | data formatting | bytes 29360128 | tf_op jit(solution)/shard_map/jit(_take)/gather | solution.py:21
  85.5 99.1 %all-gather.8.cloned.1.call-done = bf16[28,16,128,128]{2,3,1,0:T(8,128)(2,1)} async-done(((bf16[28,2,128,128]{2,3,1,0:T(8,128)(2,1)}), bf16[28,16,128,128]{2,3,1,0:T(8,128)(2,1)}) %all-gather.8.cloned.1.call-update) | async-done | bytes 14680080 | tf_op jit(solution)/shard_map/all_gather | solution.py:25
  184.6 14.1 %fusion.14 = f32[28,128,128,1]{1,2,3,0:T(8,128)} fusion(bf16[28,16,128,128]{2,3,1,0:T(8,128)(2,1)} %all-gather.8.cloned.1.call-done, bf16[28,16,128,128]{2,3,1,0:T(8,128)(2,1)} %copy.66, pred[28,16]{1,0:T(8,128)(4,1)S(1)} %copy.62), kind=kOutput, calls=%fused_computation.19 | convolution fusion | flops 1886388224 | bytes 31195584 | tf_op jit(solution)/shard_map/tjkb,jkbc->tjc/dot_general | solution.py:30
  198.7 119.6 %all-gather.6.cloned.1.call-done = bf16[28,16,128,128]{2,3,1,0:T(8,128)(2,1)} async-done(((bf16[28,2,128,128]{2,3,1,0:T(8,128)(2,1)}), bf16[28,16,128,128]{2,3,1,0:T(8,128)(2,1)}) %all-gather.6.cloned.1.call-update) | async-done | bytes 14680080 | tf_op jit(solution)/shard_map/all_gather | solution.py:24
  318.4 13.7 %multiply_convert_fusion = (bf16[128,28,128]{0,2,1:T(8,128)(2,1)S(1)}, bf16[128,28,128]{0,2,1:T(8,128)(2,1)}, bf16[128,28,128]{0,2,1:T(8,128)(2,1)}) fusion(f32[128,28,128]{0,2,1:T(8,128)S(1)} %bitcast.116, f32[28,128,128,1]{1,2,3,0:T(8,128)} %fusion.14, bf16[28,16,128,128]{2,3,1,0:T(8,128)(2,1)} %all-gather.6.cloned.1.call-done, ...), kind=kOutput, calls=%fused_computation.43 | convolution fusion | flops 1893269504 | bytes 35783104 | tf_op jit(solution)/shard_map/tjkb,jkbc->tjc/dot_general | solution.py:29
  332.1 10.5 %fusion.16 = bf16[28,16,128,128]{3,2,1,0:T(8,128)(2,1)} fusion(bf16[28,16,128,128]{2,3,1,0:T(8,128)(2,1)} %copy.66, pred[28,16]{1,0:T(8,128)(4,1)S(1)} %copy.62, bf16[128,28,128]{0,2,1:T(8,128)(2,1)} %get-tuple-element.191), kind=kOutput, calls=%fused_computation.22 | convolution fusion | flops 1893728256 | bytes 30278080 | tf_op jit(solution)/shard_map/tjkb,tjc->jkbc/dot_general | solution.py:61
  342.6 10.3 %fusion.19 = bf16[28,16,128,128]{3,2,1,0:T(8,128)(2,1)} fusion(bf16[28,16,128,128]{2,3,1,0:T(8,128)(2,1)} %copy.66, pred[28,16]{1,0:T(8,128)(4,1)S(1)} %copy.62, bf16[128,28,128]{0,2,1:T(8,128)(2,1)S(1)} %get-tuple-element.190), kind=kOutput, calls=%fused_computation.23 | convolution fusion | flops 1893728256 | bytes 30278080 | tf_op jit(solution)/shard_map/tjkb,tjc->jkbc/dot_general | solution.py:64
  356.0 2.5 broadcast_in_dim.15
  358.5 217.4 %while.13 = (s32[]{:T(128)}, f32[128,64,128]{2,0,1:T(8,128)}, s32[28,16]{0,1:T(8,128)S(1)}, bf16[28,16,128,128]{2,3,1,0:T(8,128)(2,1)}, bf16[128,28,128]{2,0,1:T...) while((s32[]{:T(128)}, f32[128,64,128]{2,0,1:T(8,128)}, ...), condition=%wide.region_2.4_spmd, body=%wide.region_0.3_spmd.sunk | while | flops 235798624 | bytes 18350520 | solution.py:53
  358.6 2.0 fusion.55
  360.5 3.5 add_bitcast_fusion.2
  365.8 6.3 scatter_fusion
  372.1 2.0 fusion.55
  374.1 3.5 add_bitcast_fusion.2
  379.4 6.2 scatter_fusion
  385.6 2.0 fusion.55
  387.6 3.5 add_bitcast_fusion.2
  392.9 6.3 scatter_fusion
  399.2 2.0 fusion.55
  401.2 3.6 add_bitcast_fusion.2
  406.6 6.2 scatter_fusion
  414.7 3.5 add_bitcast_fusion.2
  420.0 6.2 scatter_fusion
  426.2 2.0 fusion.55
  428.2 3.5 add_bitcast_fusion.2
  433.5 6.3 scatter_fusion
  439.8 2.0 fusion.55
  441.8 3.5 add_bitcast_fusion.2
  447.1 6.3 scatter_fusion
  455.4 3.6 add_bitcast_fusion.2
  460.8 6.3 scatter_fusion
  469.1 3.5 add_bitcast_fusion.2
  474.3 6.3 scatter_fusion
  480.6 2.0 fusion.55
  482.6 3.8 add_bitcast_fusion.2
  488.2 6.3 scatter_fusion
  494.5 2.0 fusion.55
  496.5 3.5 add_bitcast_fusion.2
  501.8 6.3 scatter_fusion
  508.1 2.0 fusion.55
  510.1 3.5 add_bitcast_fusion.2
  515.4 6.3 scatter_fusion
  521.7 2.0 fusion.55
  523.6 3.6 add_bitcast_fusion.2
  529.0 6.3 scatter_fusion
  535.3 2.0 fusion.55
  537.3 3.5 add_bitcast_fusion.2
  542.6 6.3 scatter_fusion
  548.9 2.0 fusion.55
  550.9 3.5 add_bitcast_fusion.2
  556.2 6.3 scatter_fusion
  562.4 2.0 fusion.55
  564.4 3.5 add_bitcast_fusion.2
  569.7 6.3 scatter_fusion
  576.0 3.9 copy_bitcast_fusion
  582.5 338.9 %all-reduce.5.cloned.1.call-done = (bf16[28,16,128,128]{3,2,1,0:T(8,128)(2,1)}, bf16[28,16,128,128]{3,2,1,0:T(8,128)(2,1)}) async-done(((bf16[28,16,128,128]{3,2,1,0:T(8,128)(2,1)}, bf16[28,16,128,128]{3,2,1,0:T(8,128)(2,1)}), (bf16[28,16,128,128]{3,2,1,0:T(8,128)(2,1)}, bf16[28,16,128,128]{3,2,1,0:T(8,128)(2,1)})) %all-reduce.5.cloned.1.call-update) | async-done | bytes 29360144
  921.4 4.4 constant_dynamic-slice_fusion.1
  925.8 34.4 %reduce-scatter.8.cloned.1.call-done = bf16[128,2048]{1,0:T(8,128)(2,1)} async-done(((bf16[128,8192]{1,0:T(8,128)(2,1)}), bf16[128,2048]{1,0:T(8,128)(2,1)}) %reduce-scatter.8.cloned.1.call-update) | async-done | bytes 524304 | tf_op jit(solution)/shard_map/reduce_scatter | solution.py:54
  (70 shorter events, 42.1 us)
Async XLA Ops:
  7.2 6.2 copy-start
  7.2 41.3 %all-gather.4.cloned.1.call-start = ((), (), s32[]{:S(2)}) async-start(), calls=%async_computation.1 | async-start | bytes 2621440 | tf_op jit(solution)/shard_map/all_gather | solution.py:16
  9.4 175.2 %all-gather.8.cloned.1.call-start = ((), (), s32[]{:S(2)}) async-start(), calls=%async_computation.3 | async-start | bytes 16515072 | tf_op jit(solution)/shard_map/all_gather | solution.py:25
  13.3 2.6 copy-start.4
  13.3 4.1 copy-start.5
  13.3 305.0 %all-gather.6.cloned.1.call-start = ((), (), s32[]{:S(2)}) async-start(), calls=%async_computation.2 | async-start | bytes 16515072 | tf_op jit(solution)/shard_map/all_gather | solution.py:24
  15.8 905.6 %all-reduce.5.cloned.1.call-start = ((), (), s32[]{:S(2)}) async-start(), calls=%async_computation.5 | async-start | bytes 58720256
  85.5 232.8 %copy-start.1 = (f32[128,3584]{0,1:T(8,128)S(1)}, f32[128,3584]{0,1:T(8,128)}, u32[]{:S(2)}) copy-start(f32[128,3584]{0,1:T(8,128)} %copy.71) | copy-start | bytes 5505028
  352.9 1.2 copy-start.3
  353.0 607.2 %reduce-scatter.8.cloned.1.call-start = ((), (), s32[]{:S(2)}) async-start(), calls=%async_computation.4 | async-start | bytes 2621440 | tf_op jit(solution)/shard_map/reduce_scatter | solution.py:54
  576.0 3.9 copy-start.6
  576.0 5.2 copy-start.2
Sparse Core Ops, SparseCore 0:
  10.4 38.0 all-gather.3
  50.7 133.9 all-gather.7
  186.2 132.0 all-gather.5
  353.1 568.2 all-reduce.4
  924.8 35.3 reduce-scatter.7
where the time goes:
time: 971 us; the launch traced here: 967 us
  waiting for transfers between devices  623 us (64%)
  matrix products  137 us (14%)
  other arithmetic  104 us (11%)
  local copies, waits for them, and re-layouts  88.1 us (9%)
  between operations  14.5 us (1%)
    unnamed x6, waiting for transfers between devices  339 us
    all_gather x1, waiting for transfers between devices, shards(): lax.all_gather(gate_blocks, 'narrow', axis=1, tiled=True)  120 us
    scatter-add x16, other arithmetic, one_slot(): return running.at[:, targets].add(contribution)  100 us
    all_gather x1, waiting for transfers between devices, shards(): lax.all_gather(up_blocks, 'narrow', axis=1, tiled=True)  99.1 us
    dot_general x16, matrix products, one_slot(): jnp.einsum('tjc,jbc->tjb', d_up, up_slot, preferred_element_type=jnp.floa...  56.3 us
    reduce_scatter x1, waiting for transfers between devices, shards(): lax.psum_scatter(partial_inputs.reshape(tokens_here, row_blocks * block_s...  34.4 us
    gather x2, local copies, waits for them, and re-layouts, picks_for(): return jnp.take(input_blocks, pattern, axis=1)  33.8 us
    dot_general x16, matrix products, one_slot(): jnp.einsum('tjc,jbc->tjb', d_gate, gate_slot, preferred_element_type=jnp....  31.6 us
  transfers between devices with their start and end apart: 5, of which 5 were waited for; matrix products, arithmetic and copies ran while one was open for 30% of the time, Pallas kernels for 0%

commit v1 on v0

v1 whole, which is shorter than its diff:
```python
import functools

import jax
import jax.numpy as jnp
from jax import lax
from jax.experimental import pallas as pl
from jax.experimental.pallas import tpu as pltpu
from jax.sharding import PartitionSpec as P


def silu_parts(gate_sum):
    sigmoid_value = jax.nn.sigmoid(gate_sum)
    return (gate_sum * sigmoid_value, sigmoid_value * (1.0 + gate_sum * (1.0 - sigmoid_value)))


def gathered_weights(inputs, gate_blocks, up_blocks, pattern, grad_hidden):
    tokens_here = inputs.shape[0]
    block_size = gate_blocks.shape[2]
    columns = gate_blocks.shape[0]
    full_inputs = lax.all_gather(inputs, "wide", axis=1, tiled=True)
    row_blocks = full_inputs.shape[1] // block_size
    input_blocks = full_inputs.reshape(tokens_here, row_blocks, block_size)
    picked = jnp.take(input_blocks, pattern, axis=1)
    gate_all = lax.all_gather(gate_blocks, "narrow", axis=1, tiled=True)
    up_all = lax.all_gather(up_blocks, "narrow", axis=1, tiled=True)
    gate_sum = jnp.einsum("tjkb,jkbc->tjc", picked, gate_all, preferred_element_type=jnp.float32)
    up_sum = jnp.einsum("tjkb,jkbc->tjc", picked, up_all, preferred_element_type=jnp.float32)
    activation, derivative = silu_parts(gate_sum)
    hidden = (activation * up_sum).astype(jnp.bfloat16)
    cotangent = grad_hidden.reshape(tokens_here, columns, block_size).astype(jnp.float32)
    d_gate = (cotangent * up_sum * derivative).astype(jnp.bfloat16)
    d_up = (cotangent * activation).astype(jnp.bfloat16)
    zero_inputs = jnp.zeros((tokens_here, row_blocks, block_size), jnp.float32)

    def one_slot(k, running):
        gate_slot = lax.dynamic_index_in_dim(gate_all, k, 1, keepdims=False)
        up_slot = lax.dynamic_index_in_dim(up_all, k, 1, keepdims=False)
        contribution = jnp.einsum(
            "tjc,jbc->tjb", d_gate, gate_slot, preferred_element_type=jnp.float32
        )
        contribution = contribution + jnp.einsum(
            "tjc,jbc->tjb", d_up, up_slot, preferred_element_type=jnp.float32
        )
        targets = lax.dynamic_index_in_dim(pattern, k, 1, keepdims=False)
        return running.at[:, targets].add(contribution)

    partial_inputs = lax.fori_loop(0, gate_all.shape[1], one_slot, zero_inputs)
    grad_inputs = lax.psum_scatter(
        partial_inputs.reshape(tokens_here, row_blocks * block_size).astype(jnp.bfloat16),
        "wide",
        scatter_dimension=1,
        tiled=True,
    )
    gate_terms = jnp.einsum("tjkb,tjc->jkbc", picked, d_gate, preferred_element_type=jnp.float32)
    up_terms = jnp.einsum("tjkb,tjc->jkbc", picked, d_up, preferred_element_type=jnp.float32)
    grad_gate = lax.psum_scatter(
        gate_terms.astype(jnp.bfloat16), "narrow", scatter_dimension=1, tiled=True
    )
    grad_up = lax.psum_scatter(
        up_terms.astype(jnp.bfloat16), "narrow", scatter_dimension=1, tiled=True
    )
    return hidden.reshape(tokens_here, columns * block_size), grad_inputs, grad_gate, grad_up


def column_kernel(nz, nw, spd, places, *refs):
    refs = list(refs)

    def take(n):
        out = refs[:n]
        del refs[:n]
        return out

    x_in = take(nz * nw)
    w_in = take(nz * 2)
    gh_in = take(nz)
    hid_out = take(nz)
    dw_out = take(nz * 2)
    dx_out = take(nw)
    x_all, dx_all, x_col, w_col, d_col, sems = refs
    step = pl.program_id(0)
    tokens = x_in[0].shape[0]
    blk = w_in[0].shape[-1]
    slots = nz * 2 * spd

    @pl.when(step == 0)
    def _():
        copies = [
            pltpu.make_async_copy(
                x_in[r * nw + m], x_all.at[m, pl.ds(r * tokens, tokens)], sems.at[r * nw + m]
            )
            for r in range(nz)
            for m in range(nw)
        ]
        for c in copies:
            c.start()
        dx_all[...] = jnp.zeros_like(dx_all)
        for c in copies:
            c.wait()

    def place(q):
        return places[step, q, 0], pl.multiple_of(places[step, q, 1] * blk, blk)

    for q in range(slots):
        piece = w_in[q // spd]
        m, at = place(q)
        x_col[:, q * blk : (q + 1) * blk] = x_all[m, :, pl.ds(at, blk)]
        w_col[q * blk : (q + 1) * blk, :blk] = piece[0, 0, q % spd]
        w_col[q * blk : (q + 1) * blk, blk:] = piece[1, 0, q % spd]
    both = jnp.dot(x_col[...], w_col[...], preferred_element_type=jnp.float32)
    gate, up = both[:, :blk], both[:, blk:]
    activation, derivative = silu_parts(gate)
    hidden = (activation * up).astype(jnp.bfloat16)
    cotangent = jnp.concatenate([g[...] for g in gh_in], axis=0).astype(jnp.float32)
    d_col[:, :blk] = (cotangent * up * derivative).astype(jnp.bfloat16)
    d_col[:, blk:] = (cotangent * activation).astype(jnp.bfloat16)
    for r in range(nz):
        hid_out[r][...] = hidden[r * tokens : (r + 1) * tokens]
    for p in range(slots // 2):
        span = slice(2 * p * blk, (2 * p + 2) * blk)
        grads = lax.dot_general(
            x_col[:, span], d_col[...], (((0,), (0,)), ((), ())), preferred_element_type=jnp.float32
        ).astype(jnp.bfloat16)
        share = lax.dot_general(
            d_col[...], w_col[span], (((1,), (1,)), ((), ())), preferred_element_type=jnp.float32
        )
        for h in range(2):
            q = 2 * p + h
            rows = grads[h * blk : (h + 1) * blk]
            dw_out[q // spd][0, 0, q % spd] = rows[:, :blk]
            dw_out[q // spd][1, 0, q % spd] = rows[:, blk:]
            m, at = place(q)
            dx_all[m, :, pl.ds(at, blk)] += share[:, h * blk : (h + 1) * blk]

    @pl.when(step == pl.num_programs(0) - 1)
    def _():
        for m in range(nw):
            dx_out[m][...] = dx_all[m].astype(jnp.bfloat16)


def columns_call(nz, nw, places, x_parts, w_parts, gh_parts):
    tokens, features = x_parts[0].shape
    _, cols, spd, blk, _ = w_parts[0].shape
    rows = nz * tokens
    slots = nz * 2 * spd
    bf = jnp.bfloat16
    w_spec = pl.BlockSpec((2, 1, spd, blk, blk), lambda j, s: (0, j, 0, 0, 0))
    h_spec = pl.BlockSpec((tokens, blk), lambda j, s: (0, j))
    dx_spec = pl.BlockSpec((rows, features), lambda j, s: (0, 0), pipeline_mode=pl.Buffered(1))
    flops = 3 * 2 * rows * slots * blk * 2 * blk * cols
    return pl.pallas_call(
        functools.partial(column_kernel, nz, nw, spd),
        grid_spec=pltpu.PrefetchScalarGridSpec(
            num_scalar_prefetch=1,
            grid=(cols,),
            in_specs=[pl.BlockSpec(memory_space=pl.ANY)] * (nz * nw)
            + [w_spec] * (nz * 2)
            + [h_spec] * nz,
            out_specs=[h_spec] * nz + [w_spec] * (nz * 2) + [dx_spec] * nw,
            scratch_shapes=[
                pltpu.VMEM((nw, rows, features), bf),
                pltpu.VMEM((nw, rows, features), jnp.float32),
                pltpu.VMEM((rows, slots * blk), bf),
                pltpu.VMEM((slots * blk, 2 * blk), bf),
                pltpu.VMEM((rows, 2 * blk), bf),
                pltpu.SemaphoreType.DMA((nz * nw,)),
            ],
        ),
        out_shape=[jax.ShapeDtypeStruct((tokens, cols * blk), bf)] * nz
        + [jax.ShapeDtypeStruct(w_parts[0].shape, bf)] * (nz * 2)
        + [jax.ShapeDtypeStruct((rows, features), bf)] * nw,
        compiler_params=pltpu.CompilerParams(
            dimension_semantics=("arbitrary",), vmem_limit_bytes=58 * 1024 * 1024
        ),
        cost_estimate=pl.CostEstimate(flops=flops, bytes_accessed=40_000_000, transcendentals=0),
    )(places, *x_parts, *w_parts, *gh_parts)


def moved_tokens(narrow, nw, inputs, gate_blocks, up_blocks, pattern, grad_hidden):
    nz = narrow // 2
    tokens = inputs.shape[0]
    features = inputs.shape[1]
    all_cols, spd, blk, _ = gate_blocks.shape
    cols = all_cols // nz
    width = cols * blk
    me = lax.axis_index("narrow")
    z, core = me // 2, me % 2
    wide = lax.axis_index("wide")

    def along_z(a, s):
        return lax.ppermute(a, "narrow", [(i, (i + 2 * s) % narrow) for i in range(narrow)])

    def swap(a):
        return lax.ppermute(a, "narrow", [(i, i ^ 1) for i in range(narrow)])

    def over_wide(a, m):
        return lax.ppermute(a, "wide", [(i, i ^ m) for i in range(nw)])

    def ahead(r):
        return lax.rem(z + r, nz)

    mine = lax.dynamic_slice_in_dim(pattern, cols * z, cols, 0)
    slot_of = jnp.stack(
        [
            ((z - r + nz) % nz * 2 + (core ^ c)) * spd + i
            for r in range(nz)
            for c in range(2)
            for i in range(spd)
        ]
    )
    rows_of = jnp.take(mine, slot_of, axis=1)
    per_device = features // blk
    places = jnp.stack([(rows_of // per_device) ^ wide, rows_of % per_device], axis=-1)

    x_z = [inputs] + [along_z(inputs, r) for r in range(1, nz)]
    x_parts = []
    for r in range(nz):
        x_parts += [x_z[r]] + [over_wide(x_z[r], m) for m in range(1, nw)]

    w_parts = []
    for r in range(nz):
        piece = jnp.stack(
            [
                lax.dynamic_slice_in_dim(a, cols * ahead(r), cols, 0)
                for a in (gate_blocks, up_blocks)
            ]
        )
        if r:
            piece = along_z(piece, r)
        w_parts += [piece, swap(piece)]
    gh_parts = []
    for r in range(nz):
        piece = lax.dynamic_slice_in_dim(grad_hidden, width * ahead(r), width, 1)
        gh_parts.append(along_z(piece, r) if r else piece)

    outs = columns_call(nz, nw, places, x_parts, w_parts, gh_parts)
    hid, dw, dx = outs[:nz], outs[nz : 3 * nz], outs[3 * nz :]

    f32 = jnp.float32
    total = dx[0].astype(f32)
    for m in range(1, nw):
        total = total + over_wide(dx[m], m).astype(f32)
    total = total.astype(jnp.bfloat16).reshape(nz, tokens, features)
    back = total[0].astype(f32)
    for r in range(1, nz):
        back = back + along_z(total[r], nz - r).astype(f32)
    grad_inputs = back.astype(jnp.bfloat16)

    hidden = jnp.zeros((tokens, nz * width), jnp.bfloat16)
    grad_gate = jnp.zeros(gate_blocks.shape, jnp.bfloat16)
    grad_up = jnp.zeros(gate_blocks.shape, jnp.bfloat16)
    for r in range(nz):
        h = along_z(hid[r], nz - r) if r else hid[r]
        hidden = lax.dynamic_update_slice_in_dim(hidden, h, width * ahead(r), 1)
        both = (dw[2 * r].astype(f32) + swap(dw[2 * r + 1]).astype(f32)).astype(jnp.bfloat16)
        if r:
            both = along_z(both, nz - r)
        grad_gate = lax.dynamic_update_slice_in_dim(grad_gate, both[0], cols * ahead(r), 0)
        grad_up = lax.dynamic_update_slice_in_dim(grad_up, both[1], cols * ahead(r), 0)
    return hidden, grad_inputs, grad_gate, grad_up


def solution(mesh):
    narrow, nw = mesh.shape["narrow"], mesh.shape["wide"]

    def shards(inputs, gate_blocks, up_blocks, pattern, grad_hidden):
        columns = gate_blocks.shape[0]
        if narrow % 2 == 0 and columns % (narrow // 2) == 0 and nw & (nw - 1) == 0:
            return moved_tokens(
                narrow, nw, inputs, gate_blocks, up_blocks, pattern, grad_hidden
            )
        return gathered_weights(inputs, gate_blocks, up_blocks, pattern, grad_hidden)

    placed = (
        P("narrow", "wide"),
        P("wide", "narrow", None, None),
        P("wide", "narrow", None, None),
        P("wide", None),
        P("narrow", "wide"),
    )
    return jax.shard_map(
        shards,
        mesh=mesh,
        in_specs=placed,
        out_specs=(
            P("narrow", "wide"),
            P("narrow", "wide"),
            P("wide", "narrow", None, None),
            P("wide", "narrow", None, None),
        ),
        check_vma=False,
    )
```

time: 971 us -> 416 us (0.43)
  waiting for transfers between devices: 623 us -> 262 us
  matrix products: 137 us -> 0 us
  other arithmetic: 104 us -> 5.64 us
  starting transfers between devices: 0.2 us -> 98.3 us
  local copies, waits for them, and re-layouts: 88.1 us -> 11.3 us
  Pallas kernels: 0 us -> 37.4 us
  between operations: 14.5 us -> 1.29 us
    unnamed x6 -> x0, waiting for transfers between devices: 339 us -> none
    ppermute x0 -> x41, waiting for transfers between devices: none -> 262 us  [the longest x15 144 us: over_wide(): return lax.ppermute(a, 'wide', [(i, i ^ m) for i in range(nw)])]
    all_gather x3 -> x0, waiting for transfers between devices: 250 us -> none  [the longest x1 120 us: shards(): lax.all_gather(gate_blocks, 'narrow', axis=1, tiled=True)]
    dot_general x36 -> x0, matrix products: 137 us -> none  [the longest x16 56.3 us: one_slot(): jnp.einsum('tjc,jbc->tjb', d_up, up_slot, preferred_element_type=jnp.floa...]
    scatter-add x16 -> x0, other arithmetic: 100 us -> none  [one_slot(): return running.at[:, targets].add(contribution)]
    ppermute x0 -> x41, starting transfers between devices: none -> 98.3 us  [the longest x18 78 us: along_z(): lax.ppermute(a, 'narrow', [(i, (i + 2 * s) % narrow) for i in range(narro...]
    pallas_call x0 -> x1, Pallas kernels: none -> 37.4 us  [columns_call(): pl.pallas_call(functools.partial(column_kernel, nz, nw, spd), grid_spec=p...]
    reduce_scatter x1 -> x0, waiting for transfers between devices: 34.4 us -> none  [shards(): lax.psum_scatter(partial_inputs.reshape(tokens_here, row_blocks * block_s...]
  transfers between devices with their start and end apart: 5 -> 41, of which waited for: 5 -> 15; matrix products, arithmetic and copies ran while one was open for 30% -> 2% of each run, Pallas kernels for 0% -> 0%
where the time goes in v1:
time: 416 us
  waiting for transfers between devices  262 us (63%)
  starting transfers between devices  98.3 us (24%)
  Pallas kernels  37.4 us (9%)
  local copies, waits for them, and re-layouts  11.3 us (3%)
  other arithmetic  5.64 us (1%)
    ppermute x15, waiting for transfers between devices, over_wide(): return lax.ppermute(a, 'wide', [(i, i ^ m) for i in range(nw)])  144 us
    ppermute x18, waiting for transfers between devices, along_z(): lax.ppermute(a, 'narrow', [(i, (i + 2 * s) % narrow) for i in range(narro...  119 us
    ppermute x18, starting transfers between devices, along_z(): lax.ppermute(a, 'narrow', [(i, (i + 2 * s) % narrow) for i in range(narro...  78 us
    pallas_call x1, Pallas kernels, columns_call(): pl.pallas_call(functools.partial(column_kernel, nz, nw, spd), grid_spec=p...  37.4 us
    ppermute x15, starting transfers between devices, over_wide(): return lax.ppermute(a, 'wide', [(i, i ^ m) for i in range(nw)])  19.5 us
  transfers between devices with their start and end apart: 41, of which 15 were waited for; matrix products, arithmetic and copies ran while one was open for 2% of the time, Pallas kernels for 0%

profile of v1, /device:TPU:0, one launch (start us, length us, event | category | flops | bytes accessed | tf_op | source)
XLA Modules:
  0.0 416.1 jit_solution(9528466838960267266)
XLA Ops:
  0.7 2.2 constant_dynamic-slice_fusion
  2.9 3.0 collective-permute-start.22
  5.9 2.6 collective-permute-start.23
  8.5 0.3 collective-permute-start.7
  8.8 2.0 collective-permute-start.11
  10.9 2.0 dynamic-slice_bitcast_fusion
  12.8 1.7 collective-permute-done.22.refs_25_
  14.5 1.7 collective-permute-start
  16.3 18.6 %collective-permute-done.23.refs_26_ = bf16[128,896]{1,0:T(8,128)(2,1)} collective-permute-done((bf16[128,896]{1,0:T(8,128)(2,1)S(1)}, bf16[128,896]{1,0:T(8,128)(2,1)}, u32[]{:S(2)}, u32[]{:S(2)}) %collective-permute-start.23) | collective-permute-done | bytes 229408 | tf_op jit(solution)/shard_map/ppermute | solution.py:190
  34.9 13.9 %collective-permute-start.24 = (bf16[128,896]{1,0:T(8,128)(2,1)S(1)}, bf16[128,896]{1,0:T(8,128)(2,1)S(1)}, u32[]{:S(2)}, u32[]{:S(2)}) collective-permute-start(bf16[128,896]{1,0:T(8,128)(2,1)S(1)} %get-tuple-element.53), channel_id=1, source_target_pairs={{0,24},{4,28},{8,0},{12,4},{16,8},{20,12},{24,16},{28,20},{1,25},{... | collective-permute-start | bytes 688136 | tf_op jit(solution)/shard_map/ppermute | solution.py:190
  48.9 13.1 %collective-permute-done.24.refs_27_ = bf16[128,896]{1,0:T(8,128)(2,1)S(1)} collective-permute-done((bf16[128,896]{1,0:T(8,128)(2,1)S(1)}, bf16[128,896]{1,0:T(8,128)(2,1)S(1)}, u32[]{:S(2)}, u32[]{:S(2)}) %collective-permute-start.24) | collective-permute-done | bytes 229408 | tf_op jit(solution)/shard_map/ppermute | solution.py:190
  62.0 1.5 collective-permute-start.1
  63.7 1.2 collective-permute-start.20
  65.0 12.2 %collective-permute-start.18 = (bf16[2,7,2,128,128]{4,3,2,1,0:T(8,128)(2,1)S(1)}, bf16[2,7,2,128,128]{4,3,2,1,0:T(8,128)(2,1)S(1)}, u32[]{:S(2)}, u32[]{:S(2)}) collective-permute-start(bf16[2,7,2,128,128]{4,3,2,1,0:T(8,128)(2,1)S(1)} %pad_maximum_fusion.2), channel_id=1, source_target_pairs={{0,16},{4,20},{8,24},{12,28},{16,0},{20,4},{24,8},{28,12},{1,17},{... | collective-permute-start | bytes 2752520 | tf_op jit(solution)/shard_map/ppermute | solution.py:190
  77.2 35.4 %collective-permute-start.16 = (bf16[2,7,2,128,128]{4,3,2,1,0:T(8,128)(2,1)S(1)}, bf16[2,7,2,128,128]{4,3,2,1,0:T(8,128)(2,1)S(1)}, u32[]{:S(2)}, u32[]{:S(2)}) collective-permute-start(bf16[2,7,2,128,128]{4,3,2,1,0:T(8,128)(2,1)S(1)} %pad_maximum_fusion.1), channel_id=1, source_target_pairs={{0,8},{4,12},{8,16},{12,20},{16,24},{20,28},{24,0},{28,4},{1,9},{5... | collective-permute-start | bytes 2752520 | tf_op jit(solution)/shard_map/ppermute | solution.py:190
  112.7 2.5 collective-permute-start.2
  115.2 12.7 %collective-permute-done.2.refs_3_ = bf16[128,2048]{1,0:T(8,128)(2,1)S(1)} collective-permute-done((bf16[128,2048]{1,0:T(8,128)(2,1)S(1)}, bf16[128,2048]{1,0:T(8,128)(2,1)S(1)}, u32[]{:S(2)}, u32[]{:S(2)}) %collective-permute-start.2) | collective-permute-done | bytes 524320 | tf_op jit(solution)/shard_map/ppermute | solution.py:196
  127.9 2.4 collective-permute-start.10
  130.3 0.5 collective-permute-start.12
  130.9 25.1 %collective-permute-done.18.refs_20_ = bf16[2,7,2,128,128]{4,3,2,1,0:T(8,128)(2,1)S(1)} collective-permute-done((bf16[2,7,2,128,128]{4,3,2,1,0:T(8,128)(2,1)S(1)}, bf16[2,7,2,128,128]{4,3,2,1,0:T(8,128)(2,1)S(1)}, u32[]{:S(2)}, u32[]{:S(2)}) %collective-permute-start.18) | collective-permute-done | bytes 917536 | tf_op jit(solution)/shard_map/ppermute | solution.py:190
  156.0 0.5 collective-permute-start.13
  156.5 2.4 collective-permute-start.14
  158.9 0.6 collective-permute-start.4
  159.5 0.3 copy-done.15
  159.9 0.6 collective-permute-start.5
  160.5 0.8 copy-done.23
  161.3 2.1 collective-permute-start.6
  163.5 29.2 %collective-permute-done.13.refs_14_ = bf16[128,2048]{1,0:T(8,128)(2,1)} collective-permute-done((bf16[128,2048]{1,0:T(8,128)(2,1)}, bf16[128,2048]{1,0:T(8,128)(2,1)}, u32[]{:S(2)}, u32[]{:S(2)}) %collective-permute-start.13) | collective-permute-done | bytes 524320 | tf_op jit(solution)/shard_map/ppermute | solution.py:196
  192.7 0.5 collective-permute-start.19
  193.4 0.6 gather_fusion
  194.0 0.2 copy.16
  194.3 8.4 %collective-permute-done.5.refs_6_ = bf16[128,2048]{1,0:T(8,128)(2,1)} collective-permute-done((bf16[128,2048]{1,0:T(8,128)(2,1)}, bf16[128,2048]{1,0:T(8,128)(2,1)}, u32[]{:S(2)}, u32[]{:S(2)}) %collective-permute-start.5) | collective-permute-done | bytes 524320 | tf_op jit(solution)/shard_map/ppermute | solution.py:196
  202.7 1.5 collective-permute-start.8
  204.2 0.5 collective-permute-start.9
  204.8 0.7 pad_add_fusion.places
  205.5 10.0 %collective-permute-done.8.refs_9_ = bf16[128,2048]{1,0:T(8,128)(2,1)S(1)} collective-permute-done((bf16[128,2048]{1,0:T(8,128)(2,1)}, bf16[128,2048]{1,0:T(8,128)(2,1)S(1)}, u32[]{:S(2)}, u32[]{:S(2)}) %collective-permute-start.8) | collective-permute-done | bytes 524320 | tf_op jit(solution)/shard_map/ppermute | solution.py:196
  215.5 1.2 collective-permute-done.9.refs_10_
  216.8 0.7 copy-done.25
  217.5 37.4 %shard_map.84 = (bf16[128,896]{1,0:T(8,128)(2,1)}, bf16[128,896]{1,0:T(8,128)(2,1)}, bf16[128,896]{1,0:T(8,128)(2,1)}, bf16[128,896]{1,0:T(8,128)(2,1)}, bf16[2,...) custom-call(s32[7,16,2]{2,1,0:T(8,128)} %pad_add_fusion.places, ...), custom_call_target="tpu_custom_call" | custom-call | flops 11274289152 | bytes 40000000 | tf_op jit(solution)/shard_map/pallas_call | solution.py:150
  255.1 1.9 collective-permute-start.27
  257.1 7.4 %collective-permute-done.25 = bf16[128,896]{1,0:T(8,128)(2,1)S(1)} collective-permute-done((bf16[128,896]{1,0:T(8,128)(2,1)}, bf16[128,896]{1,0:T(8,128)(2,1)S(1)}, u32[]{:S(2)}, u32[]{:S(2)}) %collective-permute-start.25) | collective-permute-done | bytes 229408 | tf_op jit(solution)/shard_map/ppermute | solution.py:190
  264.5 0.5 collective-permute-start.28
  265.0 10.7 %collective-permute-done.26 = bf16[128,896]{1,0:T(8,128)(2,1)S(1)} collective-permute-done((bf16[128,896]{1,0:T(8,128)(2,1)}, bf16[128,896]{1,0:T(8,128)(2,1)S(1)}, u32[]{:S(2)}, u32[]{:S(2)}) %collective-permute-start.26) | collective-permute-done | bytes 229408 | tf_op jit(solution)/shard_map/ppermute | solution.py:190
  275.8 0.3 collective-permute-start.29
  276.1 1.7 collective-permute-start.30
  277.8 1.0 constant_dynamic-update-slice_fusion.3
  279.0 0.3 add_convert_fusion.4
  279.4 1.0 copy-done.16
  280.4 0.4 broadcast.176.clone.1
  280.9 0.4 broadcast.176.clone
  281.4 0.6 copy-done.10
  282.0 0.3 add_convert_fusion.1
  282.3 0.2 collective-permute-start.40
  282.6 0.4 add_convert_fusion.2
  283.0 1.8 collective-permute-start.38
  284.8 0.3 add_convert_fusion.3
  285.1 28.2 %collective-permute-done.28 = bf16[512,2048]{1,0:T(8,128)(2,1)S(1)} collective-permute-done((bf16[512,2048]{1,0:T(8,128)(2,1)}, bf16[512,2048]{1,0:T(8,128)(2,1)S(1)}, u32[]{:S(2)}, u32[]{:S(2)}) %collective-permute-start.28) | collective-permute-done | bytes 2097184 | tf_op jit(solution)/shard_map/ppermute | solution.py:196
  313.2 1.2 collective-permute-start.36
  314.4 53.9 %collective-permute-done.29 = bf16[512,2048]{1,0:T(8,128)(2,1)S(1)} collective-permute-done((bf16[512,2048]{1,0:T(8,128)(2,1)}, bf16[512,2048]{1,0:T(8,128)(2,1)S(1)}, u32[]{:S(2)}, u32[]{:S(2)}) %collective-permute-start.29) | collective-permute-done | bytes 2097184 | tf_op jit(solution)/shard_map/ppermute | solution.py:196
  368.3 2.0 add_convert_fusion
  370.6 1.9 collective-permute-start.33
  373.0 11.9 %collective-permute-done.31 = bf16[128,2048]{1,0:T(8,128)(2,1)S(1)} collective-permute-done((bf16[128,2048]{1,0:T(8,128)(2,1)S(1)}, bf16[128,2048]{1,0:T(8,128)(2,1)S(1)}, u32[]{:S(2)}, u32[]{:S(2)}) %collective-permute-start.31) | collective-permute-done | bytes 524320 | tf_op jit(solution)/shard_map/ppermute | solution.py:190
  384.9 30.1 %collective-permute-done.32 = bf16[128,2048]{1,0:T(8,128)(2,1)S(1)} collective-permute-done((bf16[128,2048]{1,0:T(8,128)(2,1)S(1)}, bf16[128,2048]{1,0:T(8,128)(2,1)S(1)}, u32[]{:S(2)}, u32[]{:S(2)}) %collective-permute-start.32) | collective-permute-done | bytes 524320 | tf_op jit(solution)/shard_map/ppermute | solution.py:190
  415.0 1.1 add_convert_fusion.5
  (110 shorter events, 2.3 us)
Async XLA Ops:
  0.6 192.7 %copy-start = (s32[28,16]{0,1:T(8,128)S(1)}, s32[28,16]{0,1:T(8,128)}, u32[]{:S(2)}) copy-start(s32[28,16]{0,1:T(8,128)} %param.8) | copy-start | bytes 5380
  0.6 10.2 %copy-start.5 = (bf16[28,2,128,128]{3,2,1,0:T(8,128)(2,1)S(1)}, bf16[28,2,128,128]{3,2,1,0:T(8,128)(2,1)}, u32[]{:S(2)}) copy-start(bf16[28,2,128,128]{3,2,1,0:T(8,128)(2,1)} %param.7) | copy-start | bytes 5505028
  2.9 11.6 %collective-permute-start.22 = (bf16[128,896]{1,0:T(8,128)(2,1)S(1)}, bf16[128,896]{1,0:T(8,128)(2,1)S(1)}, u32[]{:S(2)}, u32[]{:S(2)}) collective-permute-start(bf16[128,896]{1,0:T(8,128)(2,1)S(1)} %get-tuple-element.54), channel_id=1, source_target_pairs={{0,8},{4,12},{8,16},{12,20},{16,24},{20,28},{24,0},{28,4},{1,9},{5... | collective-permute-start | bytes 688136 | tf_op jit(solution)/shard_map/ppermute | solution.py:190
  5.9 28.9 %collective-permute-start.23 = (bf16[128,896]{1,0:T(8,128)(2,1)S(1)}, bf16[128,896]{1,0:T(8,128)(2,1)}, u32[]{:S(2)}, u32[]{:S(2)}) collective-permute-start(bf16[128,896]{1,0:T(8,128)(2,1)S(1)} %get-tuple-element.56), channel_id=1, source_target_pairs={{0,16},{4,20},{8,24},{12,28},{16,0},{20,4},{24,8},{28,12},{1,17},{... | collective-permute-start | bytes 688136 | tf_op jit(solution)/shard_map/ppermute | solution.py:190
  8.5 55.1 %collective-permute-start.7 = (bf16[128,2048]{1,0:T(8,128)(2,1)}, bf16[128,2048]{1,0:T(8,128)(2,1)}, u32[]{:S(2)}, u32[]{:S(2)}) collective-permute-start(bf16[128,2048]{1,0:T(8,128)(2,1)} %refs_0_.1), channel_id=1, source_target_pairs={{0,16},{4,20},{8,24},{12,28},{16,0},{20,4},{24,8},{28,12},{1,17},{... | collective-permute-start | bytes 1572872 | tf_op jit(solution)/shard_map/ppermute | solution.py:190
  8.8 56.1 %collective-permute-start.11 = (bf16[128,2048]{1,0:T(8,128)(2,1)}, bf16[128,2048]{1,0:T(8,128)(2,1)}, u32[]{:S(2)}, u32[]{:S(2)}) collective-permute-start(bf16[128,2048]{1,0:T(8,128)(2,1)} %refs_0_.1), channel_id=1, source_target_pairs={{0,24},{4,28},{8,0},{12,4},{16,8},{20,12},{24,16},{28,20},{1,25},{... | collective-permute-start | bytes 1572872 | tf_op jit(solution)/shard_map/ppermute | solution.py:190
  10.9 66.3 %collective-permute-start.3 = (bf16[128,2048]{1,0:T(8,128)(2,1)}, bf16[128,2048]{1,0:T(8,128)(2,1)}, u32[]{:S(2)}, u32[]{:S(2)}) collective-permute-start(bf16[128,2048]{1,0:T(8,128)(2,1)} %refs_0_.1), channel_id=1, source_target_pairs={{0,8},{4,12},{8,16},{12,20},{16,24},{20,28},{24,0},{28,4},{1,9},{5... | collective-permute-start | bytes 1572872 | tf_op jit(solution)/shard_map/ppermute | solution.py:190
  10.9 3.6 copy-start.18
  14.5 34.4 %copy-start.26 = (bf16[128,896]{1,0:T(8,128)(2,1)}, bf16[128,896]{1,0:T(8,128)(2,1)S(1)}, u32[]{:S(2)}) copy-start(bf16[128,896]{1,0:T(8,128)(2,1)S(1)} %collective-permute-done.22.refs_25_) | copy-start | bytes 688132
  14.5 98.1 %collective-permute-start = (bf16[128,2048]{1,0:T(8,128)(2,1)S(1)}, bf16[128,2048]{1,0:T(8,128)(2,1)S(1)}, u32[]{:S(2)}, u32[]{:S(2)}) collective-permute-start(bf16[128,2048]{1,0:T(8,128)(2,1)S(1)} %copy-done.18), channel_id=1, source_target_pairs={{0,1},{1,0},{2,3},{3,2},{4,5},{5,4},{6,7},{7,6},{8,9},{9,8},{10,11... | collective-permute-start | bytes 1572872 | tf_op jit(solution)/shard_map/ppermute | solution.py:196
  34.9 27.2 %collective-permute-start.24 = (bf16[128,896]{1,0:T(8,128)(2,1)S(1)}, bf16[128,896]{1,0:T(8,128)(2,1)S(1)}, u32[]{:S(2)}, u32[]{:S(2)}) collective-permute-start(bf16[128,896]{1,0:T(8,128)(2,1)S(1)} %get-tuple-element.53), channel_id=1, source_target_pairs={{0,24},{4,28},{8,0},{12,4},{16,8},{20,12},{24,16},{28,20},{1,25},{... | collective-permute-start | bytes 688136 | tf_op jit(solution)/shard_map/ppermute | solution.py:190
  62.0 2.9 copy-start.27
  62.0 50.6 %collective-permute-start.1 = (bf16[128,2048]{1,0:T(8,128)(2,1)S(1)}, bf16[128,2048]{1,0:T(8,128)(2,1)S(1)}, u32[]{:S(2)}, u32[]{:S(2)}) collective-permute-start(bf16[128,2048]{1,0:T(8,128)(2,1)S(1)} %copy-done.18), channel_id=1, source_target_pairs={{0,2},{1,3},{2,0},{3,1},{4,6},{5,7},{6,4},{7,5},{8,10},{9,11},{10,... | collective-permute-start | bytes 1572872 | tf_op jit(solution)/shard_map/ppermute | solution.py:196
  63.7 66.7 %collective-permute-start.20 = (bf16[2,7,2,128,128]{4,3,2,1,0:T(8,128)(2,1)S(1)}, bf16[2,7,2,128,128]{4,3,2,1,0:T(8,128)(2,1)S(1)}, u32[]{:S(2)}, u32[]{:S(2)}) collective-permute-start(bf16[2,7,2,128,128]{4,3,2,1,0:T(8,128)(2,1)S(1)} %pad_maximum_fusion.3), channel_id=1, source_target_pairs={{0,24},{4,28},{8,0},{12,4},{16,8},{20,12},{24,16},{28,20},{1,25},{... | collective-permute-start | bytes 2752520 | tf_op jit(solution)/shard_map/ppermute | solution.py:190
  65.0 151.8 %copy-start.6 = (bf16[2,7,2,128,128]{4,3,2,1,0:T(8,128)(2,1)}, bf16[2,7,2,128,128]{4,3,2,1,0:T(8,128)(2,1)S(1)}, u32[]{:S(2)}) copy-start(bf16[2,7,2,128,128]{4,3,2,1,0:T(8,128)(2,1)S(1)} %pad_maximum_fusion.refs_16_) | copy-start | bytes 2752516
  65.0 91.0 %collective-permute-start.18 = (bf16[2,7,2,128,128]{4,3,2,1,0:T(8,128)(2,1)S(1)}, bf16[2,7,2,128,128]{4,3,2,1,0:T(8,128)(2,1)S(1)}, u32[]{:S(2)}, u32[]{:S(2)}) collective-permute-start(bf16[2,7,2,128,128]{4,3,2,1,0:T(8,128)(2,1)S(1)} %pad_maximum_fusion.2), channel_id=1, source_target_pairs={{0,16},{4,20},{8,24},{12,28},{16,0},{20,4},{24,8},{28,12},{1,17},{... | collective-permute-start | bytes 2752520 | tf_op jit(solution)/shard_map/ppermute | solution.py:190
  77.2 79.3 %collective-permute-start.16 = (bf16[2,7,2,128,128]{4,3,2,1,0:T(8,128)(2,1)S(1)}, bf16[2,7,2,128,128]{4,3,2,1,0:T(8,128)(2,1)S(1)}, u32[]{:S(2)}, u32[]{:S(2)}) collective-permute-start(bf16[2,7,2,128,128]{4,3,2,1,0:T(8,128)(2,1)S(1)} %pad_maximum_fusion.1), channel_id=1, source_target_pairs={{0,8},{4,12},{8,16},{12,20},{16,24},{20,28},{24,0},{28,4},{1,9},{5... | collective-permute-start | bytes 2752520 | tf_op jit(solution)/shard_map/ppermute | solution.py:190
  112.6 47.2 %copy-start.19 = (bf16[128,2048]{1,0:T(8,128)(2,1)}, bf16[128,2048]{1,0:T(8,128)(2,1)S(1)}, u32[]{:S(2)}) copy-start(bf16[128,2048]{1,0:T(8,128)(2,1)S(1)} %collective-permute-done.refs_1_) | copy-start | bytes 1572868
  112.6 46.3 %collective-permute-start.15 = (bf16[2,7,2,128,128]{4,3,2,1,0:T(8,128)(2,1)S(1)}, bf16[2,7,2,128,128]{4,3,2,1,0:T(8,128)(2,1)S(1)}, u32[]{:S(2)}, u32[]{:S(2)}) collective-permute-start(bf16[2,7,2,128,128]{4,3,2,1,0:T(8,128)(2,1)S(1)} %pad_maximum_fusion.refs_16_), channel_id=1, source_target_pairs={{0,4},{4,0},{8,12},{12,8},{16,20},{20,16},{24,28},{28,24},{1,5},{5... | collective-permute-start | bytes 2752520 | tf_op jit(solution)/shard_map/ppermute | solution.py:193
  112.6 47.9 %copy-start.20 = (bf16[128,2048]{1,0:T(8,128)(2,1)}, bf16[128,2048]{1,0:T(8,128)(2,1)S(1)}, u32[]{:S(2)}) copy-start(bf16[128,2048]{1,0:T(8,128)(2,1)S(1)} %collective-permute-done.1.refs_2_) | copy-start | bytes 1572868
  112.7 15.2 %collective-permute-start.2 = (bf16[128,2048]{1,0:T(8,128)(2,1)S(1)}, bf16[128,2048]{1,0:T(8,128)(2,1)S(1)}, u32[]{:S(2)}, u32[]{:S(2)}) collective-permute-start(bf16[128,2048]{1,0:T(8,128)(2,1)S(1)} %copy-done.18), channel_id=1, source_target_pairs={{0,3},{1,2},{2,1},{3,0},{4,7},{5,6},{6,5},{7,4},{8,11},{9,10},{10,... | collective-permute-start | bytes 1572872 | tf_op jit(solution)/shard_map/ppermute | solution.py:196
  127.9 32.6 %copy-start.21 = (bf16[128,2048]{1,0:T(8,128)(2,1)}, bf16[128,2048]{1,0:T(8,128)(2,1)S(1)}, u32[]{:S(2)}) copy-start(bf16[128,2048]{1,0:T(8,128)(2,1)S(1)} %collective-permute-done.2.refs_3_) | copy-start | bytes 1572868
  127.9 32.0 %collective-permute-start.10 = (bf16[128,2048]{1,0:T(8,128)(2,1)}, bf16[128,2048]{1,0:T(8,128)(2,1)S(1)}, u32[]{:S(2)}, u32[]{:S(2)}) collective-permute-start(bf16[128,2048]{1,0:T(8,128)(2,1)} %collective-permute-done.7.refs_8_), channel_id=1, source_target_pairs={{0,3},{1,2},{2,1},{3,0},{4,7},{5,6},{6,5},{7,4},{8,11},{9,10},{10,... | collective-permute-start | bytes 1572872 | tf_op jit(solution)/shard_map/ppermute | solution.py:196
  130.3 86.4 %copy-start.12 = (bf16[2,7,2,128,128]{4,3,2,1,0:T(8,128)(2,1)}, bf16[2,7,2,128,128]{4,3,2,1,0:T(8,128)(2,1)S(1)}, u32[]{:S(2)}) copy-start(bf16[2,7,2,128,128]{4,3,2,1,0:T(8,128)(2,1)S(1)} %collective-permute-done.20.refs_22_) | copy-start | bytes 2752516
  130.3 30.2 %collective-permute-start.12 = (bf16[128,2048]{1,0:T(8,128)(2,1)}, bf16[128,2048]{1,0:T(8,128)(2,1)S(1)}, u32[]{:S(2)}, u32[]{:S(2)}) collective-permute-start(bf16[128,2048]{1,0:T(8,128)(2,1)} %collective-permute-done.11.refs_12_), channel_id=1, source_target_pairs={{0,1},{1,0},{2,3},{3,2},{4,5},{5,4},{6,7},{7,6},{8,9},{9,8},{10,11... | collective-permute-start | bytes 1572872 | tf_op jit(solution)/shard_map/ppermute | solution.py:196
  156.0 60.8 %copy-start.13 = (bf16[2,7,2,128,128]{4,3,2,1,0:T(8,128)(2,1)}, bf16[2,7,2,128,128]{4,3,2,1,0:T(8,128)(2,1)S(1)}, u32[]{:S(2)}) copy-start(bf16[2,7,2,128,128]{4,3,2,1,0:T(8,128)(2,1)S(1)} %collective-permute-done.18.refs_20_) | copy-start | bytes 2752516
  156.0 36.8 %collective-permute-start.13 = (bf16[128,2048]{1,0:T(8,128)(2,1)}, bf16[128,2048]{1,0:T(8,128)(2,1)}, u32[]{:S(2)}, u32[]{:S(2)}) collective-permute-start(bf16[128,2048]{1,0:T(8,128)(2,1)} %collective-permute-done.11.refs_12_), channel_id=1, source_target_pairs={{0,2},{1,3},{2,0},{3,1},{4,6},{5,7},{6,4},{7,5},{8,10},{9,11},{10,... | collective-permute-start | bytes 1572872 | tf_op jit(solution)/shard_map/ppermute | solution.py:196
  156.5 2.5 copy-start.14
  156.5 36.3 %collective-permute-start.14 = (bf16[128,2048]{1,0:T(8,128)(2,1)}, bf16[128,2048]{1,0:T(8,128)(2,1)}, u32[]{:S(2)}, u32[]{:S(2)}) collective-permute-start(bf16[128,2048]{1,0:T(8,128)(2,1)} %collective-permute-done.11.refs_12_), channel_id=1, source_target_pairs={{0,3},{1,2},{2,1},{3,0},{4,7},{5,6},{6,5},{7,4},{8,11},{9,10},{10,... | collective-permute-start | bytes 1572872 | tf_op jit(solution)/shard_map/ppermute | solution.py:196
  158.9 34.3 %collective-permute-start.4 = (bf16[128,2048]{1,0:T(8,128)(2,1)}, bf16[128,2048]{1,0:T(8,128)(2,1)}, u32[]{:S(2)}, u32[]{:S(2)}) collective-permute-start(bf16[128,2048]{1,0:T(8,128)(2,1)} %collective-permute-done.3.refs_4_), channel_id=1, source_target_pairs={{0,1},{1,0},{2,3},{3,2},{4,5},{5,4},{6,7},{7,6},{8,9},{9,8},{10,11... | collective-permute-start | bytes 1572872 | tf_op jit(solution)/shard_map/ppermute | solution.py:196
  159.9 56.9 %copy-start.22 = (bf16[128,2048]{1,0:T(8,128)(2,1)}, bf16[128,2048]{1,0:T(8,128)(2,1)S(1)}, u32[]{:S(2)}) copy-start(bf16[128,2048]{1,0:T(8,128)(2,1)S(1)} %collective-permute-done.10.refs_11_) | copy-start | bytes 1572868
  159.9 42.8 %collective-permute-start.5 = (bf16[128,2048]{1,0:T(8,128)(2,1)}, bf16[128,2048]{1,0:T(8,128)(2,1)}, u32[]{:S(2)}, u32[]{:S(2)}) collective-permute-start(bf16[128,2048]{1,0:T(8,128)(2,1)} %collective-permute-done.3.refs_4_), channel_id=1, source_target_pairs={{0,2},{1,3},{2,0},{3,1},{4,6},{5,7},{6,4},{7,5},{8,10},{9,11},{10,... | collective-permute-start | bytes 1572872 | tf_op jit(solution)/shard_map/ppermute | solution.py:196
  161.3 42.9 %collective-permute-start.6 = (bf16[128,2048]{1,0:T(8,128)(2,1)}, bf16[128,2048]{1,0:T(8,128)(2,1)}, u32[]{:S(2)}, u32[]{:S(2)}) collective-permute-start(bf16[128,2048]{1,0:T(8,128)(2,1)} %collective-permute-done.3.refs_4_), channel_id=1, source_target_pairs={{0,3},{1,2},{2,1},{3,0},{4,7},{5,6},{6,5},{7,4},{8,11},{9,10},{10,... | collective-permute-start | bytes 1572872 | tf_op jit(solution)/shard_map/ppermute | solution.py:196
  192.7 24.0 %collective-permute-start.21 = (bf16[2,7,2,128,128]{4,3,2,1,0:T(8,128)(2,1)S(1)}, bf16[2,7,2,128,128]{4,3,2,1,0:T(8,128)(2,1)}, u32[]{:S(2)}, u32[]{:S(2)}) collective-permute-start(bf16[2,7,2,128,128]{4,3,2,1,0:T(8,128)(2,1)S(1)} %collective-permute-done.20.refs_22_), channel_id=1, source_target_pairs={{0,4},{4,0},{8,12},{12,8},{16,20},{20,16},{24,28},{28,24},{1,5},{5... | collective-permute-start | bytes 2752520 | tf_op jit(solution)/shard_map/ppermute | solution.py:193
  192.7 24.0 %collective-permute-start.19 = (bf16[2,7,2,128,128]{4,3,2,1,0:T(8,128)(2,1)S(1)}, bf16[2,7,2,128,128]{4,3,2,1,0:T(8,128)(2,1)}, u32[]{:S(2)}, u32[]{:S(2)}) collective-permute-start(bf16[2,7,2,128,128]{4,3,2,1,0:T(8,128)(2,1)S(1)} %collective-permute-done.18.refs_20_), channel_id=1, source_target_pairs={{0,4},{4,0},{8,12},{12,8},{16,20},{20,16},{24,28},{28,24},{1,5},{5... | collective-permute-start | bytes 2752520 | tf_op jit(solution)/shard_map/ppermute | solution.py:193
  193.3 23.5 %collective-permute-start.17 = (bf16[2,7,2,128,128]{4,3,2,1,0:T(8,128)(2,1)}, bf16[2,7,2,128,128]{4,3,2,1,0:T(8,128)(2,1)}, u32[]{:S(2)}, u32[]{:S(2)}) collective-permute-start(bf16[2,7,2,128,128]{4,3,2,1,0:T(8,128)(2,1)} %copy-done.14), channel_id=1, source_target_pairs={{0,4},{4,0},{8,12},{12,8},{16,20},{20,16},{24,28},{28,24},{1,5},{5... | collective-permute-start | bytes 2752520 | tf_op jit(solution)/shard_map/ppermute | solution.py:193
  202.7 12.9 %collective-permute-start.8 = (bf16[128,2048]{1,0:T(8,128)(2,1)}, bf16[128,2048]{1,0:T(8,128)(2,1)S(1)}, u32[]{:S(2)}, u32[]{:S(2)}) collective-permute-start(bf16[128,2048]{1,0:T(8,128)(2,1)} %collective-permute-done.7.refs_8_), channel_id=1, source_target_pairs={{0,1},{1,0},{2,3},{3,2},{4,5},{5,4},{6,7},{7,6},{8,9},{9,8},{10,11... | collective-permute-start | bytes 1572872 | tf_op jit(solution)/shard_map/ppermute | solution.py:196
  204.2 12.6 %collective-permute-start.9 = (bf16[128,2048]{1,0:T(8,128)(2,1)}, bf16[128,2048]{1,0:T(8,128)(2,1)S(1)}, u32[]{:S(2)}, u32[]{:S(2)}) collective-permute-start(bf16[128,2048]{1,0:T(8,128)(2,1)} %collective-permute-done.7.refs_8_), channel_id=1, source_target_pairs={{0,2},{1,3},{2,0},{3,1},{4,6},{5,7},{6,4},{7,5},{8,10},{9,11},{10,... | collective-permute-start | bytes 1572872 | tf_op jit(solution)/shard_map/ppermute | solution.py:196
  215.5 1.3 copy-start.24
  254.9 24.1 %copy-start.17 = (bf16[2,7,2,128,128]{4,3,2,1,0:T(8,128)(2,1)S(1)}, bf16[2,7,2,128,128]{4,3,2,1,0:T(8,128)(2,1)}, u32[]{:S(2)}) copy-start(bf16[2,7,2,128,128]{4,3,2,1,0:T(8,128)(2,1)} %get-tuple-element.33) | copy-start | bytes 2752516
  254.9 24.1 %copy-start.11 = (bf16[2,7,2,128,128]{4,3,2,1,0:T(8,128)(2,1)S(1)}, bf16[2,7,2,128,128]{4,3,2,1,0:T(8,128)(2,1)}, u32[]{:S(2)}) copy-start(bf16[2,7,2,128,128]{4,3,2,1,0:T(8,128)(2,1)} %get-tuple-element.28) | copy-start | bytes 2752516
  254.9 24.0 %collective-permute-start.34 = (bf16[2,7,2,128,128]{4,3,2,1,0:T(8,128)(2,1)}, bf16[2,7,2,128,128]{4,3,2,1,0:T(8,128)(2,1)S(1)}, u32[]{:S(2)}, u32[]{:S(2)}) collective-permute-start(bf16[2,7,2,128,128]{4,3,2,1,0:T(8,128)(2,1)} %get-tuple-element.29), channel_id=1, source_target_pairs={{0,4},{4,0},{8,12},{12,8},{16,20},{20,16},{24,28},{28,24},{1,5},{5... | collective-permute-start | bytes 2752520 | tf_op jit(solution)/shard_map/ppermute | solution.py:193
  255.0 9.5 %collective-permute-start.25 = (bf16[128,896]{1,0:T(8,128)(2,1)}, bf16[128,896]{1,0:T(8,128)(2,1)S(1)}, u32[]{:S(2)}, u32[]{:S(2)}) collective-permute-start(bf16[128,896]{1,0:T(8,128)(2,1)} %get-tuple-element.21), channel_id=1, source_target_pairs={{0,24},{4,28},{8,0},{12,4},{16,8},{20,12},{24,16},{28,20},{1,25},{... | collective-permute-start | bytes 688136 | tf_op jit(solution)/shard_map/ppermute | solution.py:190
  255.1 20.7 %collective-permute-start.26 = (bf16[128,896]{1,0:T(8,128)(2,1)}, bf16[128,896]{1,0:T(8,128)(2,1)S(1)}, u32[]{:S(2)}, u32[]{:S(2)}) collective-permute-start(bf16[128,896]{1,0:T(8,128)(2,1)} %get-tuple-element.22), channel_id=1, source_target_pairs={{0,16},{4,20},{8,24},{12,28},{16,0},{20,4},{24,8},{28,12},{1,17},{... | collective-permute-start | bytes 688136 | tf_op jit(solution)/shard_map/ppermute | solution.py:190
  255.1 20.9 %collective-permute-start.27 = (bf16[128,896]{1,0:T(8,128)(2,1)}, bf16[128,896]{1,0:T(8,128)(2,1)S(1)}, u32[]{:S(2)}, u32[]{:S(2)}) collective-permute-start(bf16[128,896]{1,0:T(8,128)(2,1)} %get-tuple-element.23), channel_id=1, source_target_pairs={{0,8},{4,12},{8,16},{12,20},{16,24},{20,28},{24,0},{28,4},{1,9},{5... | collective-permute-start | bytes 688136 | tf_op jit(solution)/shard_map/ppermute | solution.py:190
  257.1 22.3 %collective-permute-start.39 = (bf16[2,7,2,128,128]{4,3,2,1,0:T(8,128)(2,1)}, bf16[2,7,2,128,128]{4,3,2,1,0:T(8,128)(2,1)S(1)}, u32[]{:S(2)}, u32[]{:S(2)}) collective-permute-start(bf16[2,7,2,128,128]{4,3,2,1,0:T(8,128)(2,1)} %get-tuple-element.35), channel_id=1, source_target_pairs={{0,4},{4,0},{8,12},{12,8},{16,20},{20,16},{24,28},{28,24},{1,5},{5... | collective-permute-start | bytes 2752520 | tf_op jit(solution)/shard_map/ppermute | solution.py:193
  264.5 48.8 %collective-permute-start.28 = (bf16[512,2048]{1,0:T(8,128)(2,1)}, bf16[512,2048]{1,0:T(8,128)(2,1)S(1)}, u32[]{:S(2)}, u32[]{:S(2)}) collective-permute-start(bf16[512,2048]{1,0:T(8,128)(2,1)} %get-tuple-element.25), channel_id=1, source_target_pairs={{0,1},{1,0},{2,3},{3,2},{4,5},{5,4},{6,7},{7,6},{8,9},{9,8},{10,11... | collective-permute-start | bytes 6291464 | tf_op jit(solution)/shard_map/ppermute | solution.py:196
  275.8 92.5 %collective-permute-start.29 = (bf16[512,2048]{1,0:T(8,128)(2,1)}, bf16[512,2048]{1,0:T(8,128)(2,1)S(1)}, u32[]{:S(2)}, u32[]{:S(2)}) collective-permute-start(bf16[512,2048]{1,0:T(8,128)(2,1)} %get-tuple-element.26), channel_id=1, source_target_pairs={{0,2},{1,3},{2,0},{3,1},{4,6},{5,7},{6,4},{7,5},{8,10},{9,11},{10,... | collective-permute-start | bytes 6291464 | tf_op jit(solution)/shard_map/ppermute | solution.py:196
  276.1 92.2 %collective-permute-start.30 = (bf16[512,2048]{1,0:T(8,128)(2,1)}, bf16[512,2048]{1,0:T(8,128)(2,1)S(1)}, u32[]{:S(2)}, u32[]{:S(2)}) collective-permute-start(bf16[512,2048]{1,0:T(8,128)(2,1)} %get-tuple-element.27), channel_id=1, source_target_pairs={{0,3},{1,2},{2,1},{3,0},{4,7},{5,6},{6,5},{7,4},{8,11},{9,10},{10,... | collective-permute-start | bytes 6291464 | tf_op jit(solution)/shard_map/ppermute | solution.py:196
  278.8 1.5 copy-start.16
  278.9 1.9 copy-start.7
  279.0 3.4 collective-permute-start.37
  280.4 2.6 collective-permute-start.35
  282.3 2.5 copy-start.8
  282.3 90.5 %collective-permute-start.40 = (bf16[2,7,2,128,128]{4,3,2,1,0:T(8,128)(2,1)S(1)}, bf16[2,7,2,128,128]{4,3,2,1,0:T(8,128)(2,1)S(1)}, u32[]{:S(2)}, u32[]{:S(2)}) collective-permute-start(bf16[2,7,2,128,128]{4,3,2,1,0:T(8,128)(2,1)S(1)} %add_convert_fusion.1), channel_id=1, source_target_pairs={{0,8},{4,12},{8,16},{12,20},{16,24},{20,28},{24,0},{28,4},{1,9},{5... | collective-permute-start | bytes 2752520 | tf_op jit(solution)/shard_map/ppermute | solution.py:190
  283.0 85.3 %copy-start.2 = (bf16[512,2048]{1,0:T(8,128)(2,1)S(1)}, bf16[512,2048]{1,0:T(8,128)(2,1)}, u32[]{:S(2)}) copy-start(bf16[512,2048]{1,0:T(8,128)(2,1)} %get-tuple-element.24) | copy-start | bytes 6291460
  283.0 89.7 %collective-permute-start.38 = (bf16[2,7,2,128,128]{4,3,2,1,0:T(8,128)(2,1)S(1)}, bf16[2,7,2,128,128]{4,3,2,1,0:T(8,128)(2,1)S(1)}, u32[]{:S(2)}, u32[]{:S(2)}) collective-permute-start(bf16[2,7,2,128,128]{4,3,2,1,0:T(8,128)(2,1)S(1)} %add_convert_fusion.2), channel_id=1, source_target_pairs={{0,16},{4,20},{8,24},{12,28},{16,0},{20,4},{24,8},{28,12},{1,17},{... | collective-permute-start | bytes 2752520 | tf_op jit(solution)/shard_map/ppermute | solution.py:190
  313.2 57.4 %collective-permute-start.36 = (bf16[2,7,2,128,128]{4,3,2,1,0:T(8,128)(2,1)S(1)}, bf16[2,7,2,128,128]{4,3,2,1,0:T(8,128)(2,1)S(1)}, u32[]{:S(2)}, u32[]{:S(2)}) collective-permute-start(bf16[2,7,2,128,128]{4,3,2,1,0:T(8,128)(2,1)S(1)} %add_convert_fusion.3), channel_id=1, source_target_pairs={{0,24},{4,28},{8,0},{12,4},{16,8},{20,12},{24,16},{28,20},{1,25},{... | collective-permute-start | bytes 2752520 | tf_op jit(solution)/shard_map/ppermute | solution.py:190
  370.5 14.4 %collective-permute-start.31 = (bf16[128,2048]{1,0:T(8,128)(2,1)S(1)}, bf16[128,2048]{1,0:T(8,128)(2,1)S(1)}, u32[]{:S(2)}, u32[]{:S(2)}) collective-permute-start(bf16[128,2048]{1,0:T(8,128)(2,1)S(1)} %get-tuple-element.36), channel_id=1, source_target_pairs={{0,24},{4,28},{8,0},{12,4},{16,8},{20,12},{24,16},{28,20},{1,25},{... | collective-permute-start | bytes 1572872 | tf_op jit(solution)/shard_map/ppermute | solution.py:190
  370.5 44.4 %collective-permute-start.32 = (bf16[128,2048]{1,0:T(8,128)(2,1)S(1)}, bf16[128,2048]{1,0:T(8,128)(2,1)S(1)}, u32[]{:S(2)}, u32[]{:S(2)}) collective-permute-start(bf16[128,2048]{1,0:T(8,128)(2,1)S(1)} %get-tuple-element.38), channel_id=1, source_target_pairs={{0,16},{4,20},{8,24},{12,28},{16,0},{20,4},{24,8},{28,12},{1,17},{... | collective-permute-start | bytes 1572872 | tf_op jit(solution)/shard_map/ppermute | solution.py:190
  370.6 44.3 %collective-permute-start.33 = (bf16[128,2048]{1,0:T(8,128)(2,1)S(1)}, bf16[128,2048]{1,0:T(8,128)(2,1)S(1)}, u32[]{:S(2)}, u32[]{:S(2)}) collective-permute-start(bf16[128,2048]{1,0:T(8,128)(2,1)S(1)} %get-tuple-element.37), channel_id=1, source_target_pairs={{0,8},{4,12},{8,16},{12,20},{16,24},{20,28},{24,0},{28,4},{1,9},{5... | collective-permute-start | bytes 1572872 | tf_op jit(solution)/shard_map/ppermute | solution.py:190
  372.8 43.3 %copy-start.1 = (s32[28,16]{0,1:T(8,128)S(1)}, s32[28,16]{0,1:T(8,128)}, u32[]{:S(2)}) copy-start(s32[28,16]{0,1:T(8,128)} %param.8) | copy-start | bytes 5380
  373.0 43.1 %copy-start.3 = (bf16[28,2,128,128]{3,2,1,0:T(8,128)(2,1)}, bf16[28,2,128,128]{3,2,1,0:T(8,128)(2,1)S(1)}, u32[]{:S(2)}) copy-start(bf16[28,2,128,128]{3,2,1,0:T(8,128)(2,1)S(1)} %get-tuple-element.47) | copy-start | bytes 5505028
  373.0 43.1 %copy-start.4 = (bf16[28,2,128,128]{3,2,1,0:T(8,128)(2,1)}, bf16[28,2,128,128]{3,2,1,0:T(8,128)(2,1)S(1)}, u32[]{:S(2)}) copy-start(bf16[28,2,128,128]{3,2,1,0:T(8,128)(2,1)S(1)} %get-tuple-element.48) | copy-start | bytes 5505028
  (5 other events, 4.9 us)

commit v2 on v0

v2 whole, which is shorter than its diff:
```python
import functools

import jax
import jax.numpy as jnp
from jax import lax
from jax.experimental import pallas as pl
from jax.experimental.pallas import tpu as pltpu
from jax.sharding import PartitionSpec as P


def silu_parts(gate_sum):
    sigmoid_value = jax.nn.sigmoid(gate_sum)
    return (gate_sum * sigmoid_value, sigmoid_value * (1.0 + gate_sum * (1.0 - sigmoid_value)))


def gathered_weights(inputs, gate_blocks, up_blocks, pattern, grad_hidden):
    tokens_here = inputs.shape[0]
    block_size = gate_blocks.shape[2]
    columns = gate_blocks.shape[0]
    full_inputs = lax.all_gather(inputs, "wide", axis=1, tiled=True)
    row_blocks = full_inputs.shape[1] // block_size
    input_blocks = full_inputs.reshape(tokens_here, row_blocks, block_size)
    picked = jnp.take(input_blocks, pattern, axis=1)
    gate_all = lax.all_gather(gate_blocks, "narrow", axis=1, tiled=True)
    up_all = lax.all_gather(up_blocks, "narrow", axis=1, tiled=True)
    gate_sum = jnp.einsum("tjkb,jkbc->tjc", picked, gate_all, preferred_element_type=jnp.float32)
    up_sum = jnp.einsum("tjkb,jkbc->tjc", picked, up_all, preferred_element_type=jnp.float32)
    activation, derivative = silu_parts(gate_sum)
    hidden = (activation * up_sum).astype(jnp.bfloat16)
    cotangent = grad_hidden.reshape(tokens_here, columns, block_size).astype(jnp.float32)
    d_gate = (cotangent * up_sum * derivative).astype(jnp.bfloat16)
    d_up = (cotangent * activation).astype(jnp.bfloat16)
    zero_inputs = jnp.zeros((tokens_here, row_blocks, block_size), jnp.float32)

    def one_slot(k, running):
        gate_slot = lax.dynamic_index_in_dim(gate_all, k, 1, keepdims=False)
        up_slot = lax.dynamic_index_in_dim(up_all, k, 1, keepdims=False)
        contribution = jnp.einsum(
            "tjc,jbc->tjb", d_gate, gate_slot, preferred_element_type=jnp.float32
        )
        contribution = contribution + jnp.einsum(
            "tjc,jbc->tjb", d_up, up_slot, preferred_element_type=jnp.float32
        )
        targets = lax.dynamic_index_in_dim(pattern, k, 1, keepdims=False)
        return running.at[:, targets].add(contribution)

    partial_inputs = lax.fori_loop(0, gate_all.shape[1], one_slot, zero_inputs)
    grad_inputs = lax.psum_scatter(
        partial_inputs.reshape(tokens_here, row_blocks * block_size).astype(jnp.bfloat16),
        "wide",
        scatter_dimension=1,
        tiled=True,
    )
    gate_terms = jnp.einsum("tjkb,tjc->jkbc", picked, d_gate, preferred_element_type=jnp.float32)
    up_terms = jnp.einsum("tjkb,tjc->jkbc", picked, d_up, preferred_element_type=jnp.float32)
    grad_gate = lax.psum_scatter(
        gate_terms.astype(jnp.bfloat16), "narrow", scatter_dimension=1, tiled=True
    )
    grad_up = lax.psum_scatter(
        up_terms.astype(jnp.bfloat16), "narrow", scatter_dimension=1, tiled=True
    )
    return hidden.reshape(tokens_here, columns * block_size), grad_inputs, grad_gate, grad_up


BF16, F32 = jnp.bfloat16, jnp.float32
CHUNKS = 2


ANY = pl.BlockSpec(memory_space=pl.ANY)


def taker(refs):
    refs = list(refs)

    def take(n):
        out = refs[:n]
        del refs[:n]
        return out

    return take


def place_of(places, step, q, blk):
    return places[step, q, 0], pl.multiple_of(places[step, q, 1] * blk, blk)


def forward_kernel(nz, nw, spd, unread, layout, places, *refs):
    take = taker(refs)
    x_in = take(len(layout))
    w_own, w_other = take(nz), take(nz)
    take(unread)
    (g_own, g_other, d_out) = take(nz), take(1)[0], take(1)[0]
    x_all, x_col, w_col, sems = take(4)
    step = pl.program_id(0)
    tokens = d_out.shape[1] // nz
    blk = d_out.shape[-1] // 2
    slots = nz * 2 * spd

    @pl.when(step == 0)
    def _():
        copies = []
        for source, pieces in zip(x_in, layout):
            for at, m, rows, n in pieces:
                target = x_all.at[m, pl.ds(rows, n)]
                sem = sems.at[len(copies)]
                copies.append(pltpu.make_async_copy(source.at[pl.ds(at, n)], target, sem))
        for c in copies:
            c.start()
        for c in copies:
            c.wait()

    for q in range(slots):
        r, i = q // (2 * spd), q % spd
        piece = (w_other if q // spd % 2 else w_own)[r]
        m, at = place_of(places, step, q, blk)
        x_col[:, q * blk : (q + 1) * blk] = x_all[m, :, pl.ds(at, blk)]
        w_col[q * blk : (q + 1) * blk, :blk] = piece[i, 0]
        w_col[q * blk : (q + 1) * blk, blk:] = piece[spd + i, 0]
    both = jnp.dot(x_col[...], w_col[...], preferred_element_type=F32)
    gate, up = both[:, :blk], both[:, blk:]
    activation, derivative = silu_parts(gate)
    hidden = (activation * up).astype(BF16)
    cotangent = jnp.concatenate([w[2 * spd, 0] for w in w_own], axis=0).astype(F32)
    d_out[0, :, :blk] = (cotangent * up * derivative).astype(BF16)
    d_out[0, :, blk:] = (cotangent * activation).astype(BF16)
    for r in range(nz):
        g_own[r][2 * spd, 0] = hidden[r * tokens : (r + 1) * tokens]
        g_other[r, 2 * spd, 0] = jnp.zeros((tokens, blk), BF16)
    for p in range(slots // 2):
        grads = lax.dot_general(
            x_col[:, 2 * p * blk : (2 * p + 2) * blk],
            d_out[0],
            (((0,), (0,)), ((), ())),
            preferred_element_type=F32,
        ).astype(BF16)
        for h in range(2):
            q = 2 * p + h
            r, i = q // (2 * spd), q % spd
            rows = grads[h * blk : (h + 1) * blk]
            target = g_other.at[r] if q // spd % 2 else g_own[r]
            target[i, 0] = rows[:, :blk]
            target[spd + i, 0] = rows[:, blk:]


def forward_call(lo, nw, tokens, places, layout, x_parts, w_own, w_other, earlier):
    nz, features = len(w_own), x_parts[0].shape[1]
    parts, cols, blk, _ = w_own[1].shape
    spd = parts // 2
    rows, slots = nz * tokens, nz * 2 * spd
    own = pl.BlockSpec((parts, 1, blk, blk), lambda j, s: (0, j, 0, 0))
    own0 = pl.BlockSpec((parts, 1, blk, blk), lambda j, s: (0, j + lo, 0, 0))
    other = pl.BlockSpec((2 * spd, 1, blk, blk), lambda j, s: (0, j, 0, 0))
    other0 = pl.BlockSpec((2 * spd, 1, blk, blk), lambda j, s: (0, j + lo, 0, 0))
    every = pl.BlockSpec((nz, parts, 1, blk, blk), lambda j, s: (0, 0, j, 0, 0))
    d_spec = pl.BlockSpec((1, rows, 2 * blk), lambda j, s: (j, 0, 0))
    outs = pl.pallas_call(
        functools.partial(forward_kernel, nz, nw, spd, len(earlier), layout),
        grid_spec=pltpu.PrefetchScalarGridSpec(
            num_scalar_prefetch=1,
            grid=(cols,),
            in_specs=[ANY] * len(x_parts)
            + [own0]
            + [own] * (nz - 1)
            + [other0]
            + [other] * (nz - 1)
            + [ANY] * len(earlier),
            out_specs=[own] * nz + [every, d_spec],
            scratch_shapes=[
                pltpu.VMEM((nw, rows, features), BF16),
                pltpu.VMEM((rows, slots * blk), BF16),
                pltpu.VMEM((slots * blk, 2 * blk), BF16),
                pltpu.SemaphoreType.DMA((sum(len(p) for p in layout),)),
            ],
        ),
        out_shape=[jax.ShapeDtypeStruct(w_own[1].shape, BF16)] * nz
        + [
            jax.ShapeDtypeStruct((nz, *w_own[1].shape), BF16),
            jax.ShapeDtypeStruct((cols, rows, 2 * blk), BF16),
        ],
        compiler_params=pltpu.CompilerParams(
            dimension_semantics=("arbitrary",), vmem_limit_bytes=28 * 1024 * 1024
        ),
        cost_estimate=pl.CostEstimate(
            flops=8 * rows * slots * blk * blk * cols,
            bytes_accessed=10_000_000 + cols * 2_500_000,
            transcendentals=0,
        ),
    )(places, *x_parts, *w_own, *w_other, *earlier)
    return outs[:nz], outs[nz], outs[nz + 1]


OUT_HALVES = ((0, (2, 3)), (1, (1, 3)), (0, (0, 1)), (1, (0, 2)))


def inputs_kernel(nz, spd, counts, groups, unread, places, *refs):
    take = taker(refs)
    chunks = [(take(nz), take(nz), take(1)[0]) for _ in counts]
    take(unread)
    dx_out = [take(len(OUT_HALVES)) for _ in groups]
    dx_all, w_col = take(2)
    step = pl.program_id(0)
    tokens = dx_all.shape[1] // nz
    blk = w_col.shape[-1] // 2
    slots = nz * 2 * spd

    @pl.when(step == 0)
    def _():
        dx_all[...] = jnp.zeros_like(dx_all)

    start = 0
    for count, (w_own, w_other, d_in) in zip(counts, chunks):

        @pl.when((step >= start) & (step < start + count))
        def _(w_own=w_own, w_other=w_other, d_in=d_in):
            for q in range(slots):
                r, i = q // (2 * spd), q % spd
                piece = (w_other if q // spd % 2 else w_own)[r]
                w_col[q * blk : (q + 1) * blk, :blk] = piece[i, 0]
                w_col[q * blk : (q + 1) * blk, blk:] = piece[spd + i, 0]
            for p in range(slots // 2):
                share = lax.dot_general(
                    d_in[0],
                    w_col[2 * p * blk : (2 * p + 2) * blk],
                    (((1,), (1,)), ((), ())),
                    preferred_element_type=F32,
                )
                for h in range(2):
                    m, at = place_of(places, step, 2 * p + h, blk)
                    dx_all[m, :, pl.ds(at, blk)] += share[:, h * blk : (h + 1) * blk]

        start += count

    @pl.when(step == pl.num_programs(0) - 1)
    def _():
        half = tokens // 2
        for group, out in zip(groups, dx_out):
            for ref, (h, ms) in zip(out, OUT_HALVES):
                for i, m in enumerate(ms):
                    for k, r in enumerate(group):
                        rows = dx_all[m, r * tokens + h * half : r * tokens + (h + 1) * half]
                        ref[i, k * half : (k + 1) * half] = rows.astype(BF16)


def inputs_call(places, nw, tokens, features, chunks, groups, earlier):
    nz = len(chunks[0][0])
    parts, _, blk, _ = chunks[0][0][0].shape
    spd = parts // 2
    rows, slots = nz * tokens, nz * 2 * spd
    counts = tuple(c[0][1].shape[1] for c in chunks)
    in_specs, operands, start = [], [], 0
    for count, (w_own, w_other, d) in zip(counts, chunks):

        def at(j, start=start, count=count):
            return jnp.clip(j - start, 0, count - 1)

        block = pl.BlockSpec((2 * spd, 1, blk, blk), lambda j, s, at=at: (0, at(j), 0, 0))
        block0 = pl.BlockSpec(
            (2 * spd, 1, blk, blk), lambda j, s, at=at, start=start: (0, at(j) + start, 0, 0)
        )
        in_specs += ([block0] + [block] * (nz - 1)) * 2
        in_specs += [pl.BlockSpec((1, rows, 2 * blk), lambda j, s, at=at: (at(j), 0, 0))]
        operands += [*w_own, *w_other, d]
        start += count
    in_specs += [ANY] * len(earlier)
    operands += earlier
    shapes = [(2, len(g) * tokens // 2, features) for g in groups for _ in OUT_HALVES]
    outs = pl.pallas_call(
        functools.partial(inputs_kernel, nz, spd, counts, groups, len(earlier)),
        grid_spec=pltpu.PrefetchScalarGridSpec(
            num_scalar_prefetch=1,
            grid=(start,),
            in_specs=in_specs,
            out_specs=[
                pl.BlockSpec(s, lambda j, s_: (0, 0, 0), pipeline_mode=pl.Buffered(1)) for s in shapes
            ],
            scratch_shapes=[
                pltpu.VMEM((nw, rows, features), F32),
                pltpu.VMEM((slots * blk, 2 * blk), BF16),
            ],
        ),
        out_shape=[jax.ShapeDtypeStruct(s, BF16) for s in shapes],
        compiler_params=pltpu.CompilerParams(
            dimension_semantics=("arbitrary",), vmem_limit_bytes=40 * 1024 * 1024
        ),
        cost_estimate=pl.CostEstimate(
            flops=4 * rows * slots * blk * blk * start,
            bytes_accessed=20_000_000,
            transcendentals=0,
        ),
    )(places, *operands)
    n = len(OUT_HALVES)
    return [outs[g * n : (g + 1) * n] for g in range(len(groups))]


def hold(values, *earlier):
    n = len(values)
    return pl.pallas_call(
        lambda *refs: None,
        in_specs=[ANY] * (n + len(earlier)),
        out_specs=[ANY] * n,
        out_shape=[jax.ShapeDtypeStruct(v.shape, v.dtype) for v in values],
        input_output_aliases={i: i for i in range(n)},
    )(*values, *earlier)


VMEM = pl.BlockSpec(memory_space=pltpu.VMEM)
SMEM = pl.BlockSpec(memory_space=pltpu.SMEM)


def message_blocks(nz, cols, spd, blk, bounds, where):
    for k, (r, lo, hi) in enumerate(bounds):
        first = lax.rem(where[0] + r, nz) * cols + lo
        for j in range(hi - lo):
            yield k, j, first + j, pl.ds(pl.multiple_of((first + j) * blk, blk), blk)


def pack_kernel(nz, cols, spd, bounds, where, gate, up, cot, *outs):
    for k, j, col, at in message_blocks(nz, cols, spd, gate.shape[-1], bounds, where):
        for i in range(spd):
            outs[k][i, j] = gate[col, i]
            outs[k][spd + i, j] = up[col, i]
        outs[k][2 * spd, j] = cot[:, at]


def pack_call(nz, bounds, where, gate, up, cot):
    all_cols, spd, blk, _ = gate.shape
    cols = all_cols // nz
    return pl.pallas_call(
        functools.partial(pack_kernel, nz, cols, spd, bounds),
        in_specs=[SMEM] + [VMEM] * 3,
        out_specs=[VMEM] * len(bounds),
        out_shape=[
            jax.ShapeDtypeStruct((2 * spd + 1, hi - lo, blk, blk), BF16) for _, lo, hi in bounds
        ],
        compiler_params=pltpu.CompilerParams(vmem_limit_bytes=20 * 1024 * 1024),
        cost_estimate=pl.CostEstimate(flops=0, bytes_accessed=10_000_000, transcendentals=0),
    )(where, gate, up, cot)


def unpack_kernel(nz, cols, spd, bounds, where, *refs):
    parts = refs[: len(bounds)]
    hidden, gate, up = refs[len(bounds) :]
    for k, j, col, at in message_blocks(nz, cols, spd, gate.shape[-1], bounds, where):
        for i in range(spd):
            gate[col, i] = parts[k][i, j]
            up[col, i] = parts[k][spd + i, j]
        hidden[:, at] = parts[k][2 * spd, j]


def unpack_call(nz, bounds, where, parts, hidden, gate):
    all_cols, spd, blk, _ = gate.shape
    cols = all_cols // nz
    return pl.pallas_call(
        functools.partial(unpack_kernel, nz, cols, spd, bounds),
        in_specs=[SMEM] + [VMEM] * len(bounds),
        out_specs=[VMEM] * 3,
        out_shape=[jax.ShapeDtypeStruct(a.shape, BF16) for a in (hidden, gate, gate)],
        compiler_params=pltpu.CompilerParams(vmem_limit_bytes=20 * 1024 * 1024),
        cost_estimate=pl.CostEstimate(flops=0, bytes_accessed=10_000_000, transcendentals=0),
    )(where, *parts)


def moved_tokens(narrow, nw, inputs, gate_blocks, up_blocks, pattern, grad_hidden):
    nz = narrow // 2
    tokens, features = inputs.shape
    all_cols, spd, blk, _ = gate_blocks.shape
    cols = all_cols // nz
    me = lax.axis_index("narrow")
    z, core = me // 2, me % 2
    wide = lax.axis_index("wide")
    shifts = sorted(range(1, nz), key=lambda r: -min(r, nz - r))

    def along_z(a, s):
        with jax.named_scope(f"along_z{s}"):
            return lax.ppermute(a, "narrow", [(i, (i + 2 * s) % narrow) for i in range(narrow)])

    def swap(a):
        with jax.named_scope("swap"):
            return lax.ppermute(a, "narrow", [(i, i ^ 1) for i in range(narrow)])

    def over_wide(a, m):
        with jax.named_scope(f"wide{m}"):
            return lax.ppermute(a, "wide", [(i, i ^ m) for i in range(nw)])

    where = z.reshape(1).astype(jnp.int32)
    mine = lax.dynamic_slice_in_dim(pattern, cols * z, cols, 0)
    slot_of = jnp.stack(
        [
            ((z - r + nz) % nz * 2 + (core ^ c)) * spd + i
            for r in range(nz)
            for c in range(2)
            for i in range(spd)
        ]
    )
    rows_of = jnp.take(mine, slot_of, axis=1)
    per_device = features // blk
    places = jnp.stack([(rows_of // per_device) ^ wide, rows_of % per_device], axis=-1)

    edges = [cols * k // CHUNKS for k in range(CHUNKS, -1, -1)]
    edges = [cols - e for e in edges]
    chunks = list(zip(edges[:-1], edges[1:]))
    bounds = [(0, 0, cols)] + [(r, lo, hi) for lo, hi in chunks for r in shifts]
    own, *messages = pack_call(nz, bounds, where, gate_blocks, up_blocks, grad_hidden)

    half = tokens // 2
    x_z = {r: along_z(inputs, r) for r in reversed(shifts)}
    x_parts, layout = [], []
    for group in ([0], list(range(1, nz))):
        pieces = [inputs if r == 0 else x_z[r] for r in group]
        a, b = (
            jnp.concatenate([p[h * half : (h + 1) * half] for p in pieces], axis=0)
            for h in range(2)
        )
        if x_parts:
            a, b = hold([a, b], *x_parts[-2:], *messages[:1])
        n = len(group) * half
        ax, by = over_wide(a, 1), over_wide(b, 2)
        far_a = over_wide(jnp.concatenate([a, ax], axis=0), 2)
        far_b = over_wide(jnp.concatenate([b, by], axis=0), 1)
        x_parts += [a, b, ax, by, far_a, far_b]
        for h, ms in ((0, (0,)), (1, (0,)), (0, (1,)), (1, (2,)), (0, (2, 3)), (1, (1, 3))):
            layout.append(
                tuple(
                    (i * n + k * half, m, r * tokens + h * half, half)
                    for i, m in enumerate(ms)
                    for k, r in enumerate(group)
                )
            )

    earlier = [x_z[r] for r in shifts]
    weights, other = [], None
    for lo, hi in chunks:
        now, messages = messages[: nz - 1], messages[nz - 1 :]
        now = [hold([a], e)[0] for a, e in zip(now, earlier)]
        now = earlier = [along_z(a, r) for a, r in zip(now, shifts)]
        if other is None:
            other = swap(*hold([own], *now))
        in_order = [now[shifts.index(r)] for r in range(1, nz)]
        weights.append(([own] + in_order, [other] + [swap(a) for a in in_order]))

    order = [*shifts, 0]
    groups = [order[: (nz + 1) // 2], order[(nz + 1) // 2 :]]
    columns, sent, parts, back, sums = [], [], [], [], []
    for k, ((lo, hi), (w_own, w_other)) in enumerate(zip(chunks, weights)):
        g_own, g_other, d = forward_call(
            lo, nw, tokens, places[lo:hi], tuple(layout), x_parts, w_own, w_other, sums
        )
        columns.append((w_own, w_other, d))
        if k + 1 < len(chunks):
            beside = weights[k + 1][0][1:]
        else:
            dx = inputs_call(places, nw, tokens, features, columns, groups, [])
            beside = [dx[0][0], *(sent[-1] if sent else [])]
        g_other = swap(*hold([g_other], *beside))
        sums = [(g_own[r].astype(F32) + g_other[r].astype(F32)).astype(BF16) for r in [0, *shifts]]
        now = sums[1:]
        if sent:
            now = [hold([a], e)[0] for a, e in zip(now, sent[-1])]
        sent.append([along_z(a, nz - r) for a, r in zip(now, shifts)])
        parts += [sums[0], *sent[-1]]
        back += [(r, lo, hi) for r in [0, *shifts]]
    hidden, grad_gate, grad_up = unpack_call(nz, back, where, parts, grad_hidden, gate_blocks)

    total, earlier = 0, sent[0]
    step = [a for a, r in zip(sent[-1], shifts) if 2 * r != nz]
    for group, (to_y, to_x, keep_a, keep_b) in zip(groups, dx):
        to_y, to_x = hold([to_y, to_x], *earlier)
        to_y, to_x = over_wide(to_y, 2), over_wide(to_x, 1)
        near_a, pass_a = (keep_a[i].astype(F32) + to_y[i].astype(F32) for i in range(2))
        near_b, pass_b = (keep_b[i].astype(F32) + to_x[i].astype(F32) for i in range(2))
        pass_a, pass_b = hold([pass_a.astype(BF16), pass_b.astype(BF16)], *step)
        step = sent[-1]
        earlier = [pass_a, pass_b]
        pass_a, pass_b = over_wide(pass_a, 1), over_wide(pass_b, 2)
        halves = near_a + pass_a.astype(F32), near_b + pass_b.astype(F32)
        shares = []
        for i, r in enumerate(group):
            shares.append(jnp.concatenate([a[i * half : (i + 1) * half] for a in halves], axis=0))
        away = [i for i, r in enumerate(group) if r]
        ready = [shares[i].astype(BF16) for i in away]
        ready = [hold([a], sent[-1][shifts.index(group[i])])[0] for a, i in zip(ready, away)]
        for i, a in zip(away, ready):
            shares[i] = along_z(a, nz - group[i]).astype(F32)
        total = total + sum(shares)
    return hidden, total.astype(BF16), grad_gate, grad_up


def solution(mesh):
    narrow, nw = mesh.shape["narrow"], mesh.shape["wide"]

    def shards(inputs, gate_blocks, up_blocks, pattern, grad_hidden):
        columns = gate_blocks.shape[0]
        if narrow % 2 == 0 and columns % (narrow // 2) == 0 and nw == 4:
            return moved_tokens(
                narrow, nw, inputs, gate_blocks, up_blocks, pattern, grad_hidden
            )
        return gathered_weights(inputs, gate_blocks, up_blocks, pattern, grad_hidden)

    placed = (
        P("narrow", "wide"),
        P("wide", "narrow", None, None),
        P("wide", "narrow", None, None),
        P("wide", None),
        P("narrow", "wide"),
    )
    return jax.shard_map(
        shards,
        mesh=mesh,
        in_specs=placed,
        out_specs=(
            P("narrow", "wide"),
            P("narrow", "wide"),
            P("wide", "narrow", None, None),
            P("wide", "narrow", None, None),
        ),
        check_vma=False,
    )
```

time: 971 us -> 355 us (0.37)
  the two profiles are of different devices: /device:TPU:0 before, /device:TPU:21 now
where the time goes in v2:
time: 355 us; the launch traced here: 354 us
  waiting for transfers between devices  157 us (44%)
  starting transfers between devices  68.3 us (19%)
  Pallas kernels  51.4 us (14%)
  local copies, waits for them, and re-layouts  45.4 us (13%)
  other arithmetic  30.2 us (9%)
    ppermute x18, waiting for transfers between devices, along_z(): lax.ppermute(a, 'narrow', [(i, (i + 2 * s) % narrow) for i in range(narro...  89.9 us
    ppermute x16, waiting for transfers between devices, over_wide(): return lax.ppermute(a, 'wide', [(i, i ^ m) for i in range(nw)])  61.4 us
    unnamed x185, local copies, waits for them, and re-layouts  39.3 us
    ppermute x9, starting transfers between devices, swap(): return lax.ppermute(a, 'narrow', [(i, i ^ 1) for i in range(narrow)])  32.1 us
    pallas_call x2, Pallas kernels, forward_call(): pl.pallas_call(functools.partial(forward_kernel, nz, nw, spd, len(earlier...  29.7 us
    ppermute x18, starting transfers between devices, along_z(): lax.ppermute(a, 'narrow', [(i, (i + 2 * s) % narrow) for i in range(narro...  25.8 us
    pallas_call x1, Pallas kernels, inputs_call(): pl.pallas_call(functools.partial(inputs_kernel, nz, spd, counts, groups,...  18.7 us
    ppermute x16, starting transfers between devices, over_wide(): return lax.ppermute(a, 'wide', [(i, i ^ m) for i in range(nw)])  10.3 us
  transfers between devices with their start and end apart: 43, of which 19 were waited for; matrix products, arithmetic and copies ran while one was open for 10% of the time, Pallas kernels for 15%

profile of v2, /device:TPU:21, one launch (start us, length us, event | category | flops | bytes accessed | tf_op | source)
XLA Modules:
  0.0 354.1 jit_solution(1074987392772168989)
XLA Ops:
  0.6 1.1 fusion.27
  1.7 1.3 collective-permute-start
  3.4 1.3 collective-permute-start.4
  4.7 1.9 collective-permute-start.5
  6.6 1.5 copy-done.42
  8.1 1.5 copy-done.43
  9.6 1.2 copy-done.56
  15.3 1.2 collective-permute-start.2
  17.5 1.1 fusion.26
  18.6 8.6 %collective-permute-done.4.refs_1_ = bf16[128,2048]{1,0:T(8,128)(2,1)} collective-permute-done((bf16[128,2048]{1,0:T(8,128)(2,1)}, bf16[128,2048]{1,0:T(8,128)(2,1)}, u32[]{:S(2)}, u32[]{:S(2)}) %collective-permute-start.4) | collective-permute-done | bytes 524320 | tf_op jit(solution)/shard_map/along_z1/ppermute | solution.py:375
  27.2 1.1 fusion.24
  28.3 19.2 %collective-permute-done.5.refs_1_ = bf16[128,2048]{1,0:T(8,128)(2,1)} collective-permute-done((bf16[128,2048]{1,0:T(8,128)(2,1)}, bf16[128,2048]{1,0:T(8,128)(2,1)}, u32[]{:S(2)}, u32[]{:S(2)}) %collective-permute-start.5) | collective-permute-done | bytes 524320 | tf_op jit(solution)/shard_map/along_z2/ppermute | solution.py:375
  47.5 1.1 fusion.25
  48.5 1.2 pad_maximum_fusion.2
  51.2 5.4 %collective-permute-start.11 = (bf16[5,4,128,128]{3,2,1,0:T(8,128)(2,1)}, bf16[5,4,128,128]{3,2,1,0:T(8,128)(2,1)}, u32[]{:S(2)}, u32[]{:S(2)}) collective-permute-start(bf16[5,4,128,128]{3,2,1,0:T(8,128)(2,1)} %shard_map.86), channel_id=1, source_target_pairs={{0,8},{4,12},{8,16},{12,20},{16,24},{20,28},{24,0},{28,4},{1,9},{5... | collective-permute-start | bytes 1966088 | tf_op jit(solution)/shard_map/along_z1/ppermute | solution.py:375
  56.7 2.1 collective-permute-start.12
  58.7 9.5 %collective-permute-done.8.refs_9_ = bf16[192,2048]{1,0:T(8,128)(2,1)S(1)} collective-permute-done((bf16[192,2048]{1,0:T(8,128)(2,1)}, bf16[192,2048]{1,0:T(8,128)(2,1)S(1)}, u32[]{:S(2)}, u32[]{:S(2)}) %collective-permute-start.8) | collective-permute-done | bytes 786464 | tf_op jit(solution)/shard_map/wide2/ppermute | solution.py:383
  68.2 1.3 pad_maximum_fusion.1
  69.8 2.4 pad_maximum_fusion
  72.9 27.7 %collective-permute-start.15 = (bf16[5,4,128,128]{3,2,1,0:T(8,128)(2,1)}, bf16[5,4,128,128]{3,2,1,0:T(8,128)(2,1)}, u32[]{:S(2)}, u32[]{:S(2)}) collective-permute-start(bf16[5,4,128,128]{3,2,1,0:T(8,128)(2,1)} %collective-permute-done.11.refs_2_.refs_13_.refs_1_), channel_id=1, source_target_pairs={{0,4},{4,0},{8,12},{12,8},{16,20},{20,16},{24,28},{28,24},{1,5},{5... | collective-permute-start | bytes 1966088 | tf_op jit(solution)/shard_map/swap/ppermute | solution.py:379
  101.7 11.6 %collective-permute-done.12.refs_1_.refs_14_.refs_2_ = bf16[5,4,128,128]{3,2,1,0:T(8,128)(2,1)} collective-permute-done((bf16[5,4,128,128]{3,2,1,0:T(8,128)(2,1)}, bf16[5,4,128,128]{3,2,1,0:T(8,128)(2,1)}, u32[]{:S(2)}, u32[]{:S(2)}) %collective-permute-start.12) | collective-permute-done | bytes 655392 | tf_op jit(solution)/shard_map/along_z2/ppermute | solution.py:375
  116.1 1.6 add_select_fusion
  119.2 4.9 %collective-permute-start.19 = (bf16[5,3,128,128]{3,2,1,0:T(8,128)(2,1)}, bf16[5,3,128,128]{3,2,1,0:T(8,128)(2,1)}, u32[]{:S(2)}, u32[]{:S(2)}) collective-permute-start(bf16[5,3,128,128]{3,2,1,0:T(8,128)(2,1)} %shard_map.92), channel_id=1, source_target_pairs={{0,16},{4,20},{8,24},{12,28},{16,0},{20,4},{24,8},{28,12},{1,17},{... | collective-permute-start | bytes 1474568 | tf_op jit(solution)/shard_map/along_z2/ppermute | solution.py:375
  130.9 16.1 %shard_map.90 = (bf16[5,4,128,128]{3,2,1,0:T(8,128)(2,1)S(1)}, bf16[5,4,128,128]{3,2,1,0:T(8,128)(2,1)S(1)}, bf16[5,4,128,128]{3,2,1,0:T(8,128)(2,1)S(1)}, bf16[...) custom-call(s32[4,16,2]{2,1,0:T(8,128)S(1)} %fusion.18.places, ...), custom_call_target="tpu_custom_call" | custom-call | flops 4294967296 | bytes 20000000 | tf_op jit(solution)/shard_map/pallas_call | solution.py:156
  147.0 1.5 copy-done.23
  153.7 7.6 %collective-permute-done.19.refs_2_.refs_14_.refs_11_ = bf16[5,3,128,128]{3,2,1,0:T(8,128)(2,1)} collective-permute-done((bf16[5,3,128,128]{3,2,1,0:T(8,128)(2,1)}, bf16[5,3,128,128]{3,2,1,0:T(8,128)(2,1)}, u32[]{:S(2)}, u32[]{:S(2)}) %collective-permute-start.19) | collective-permute-done | bytes 491552 | tf_op jit(solution)/shard_map/along_z2/ppermute | solution.py:375
  161.3 1.3 collective-permute-start.21
  164.2 3.2 collective-permute-done.21
  167.5 2.7 fusion
  170.2 3.2 collective-permute-start.22
  173.4 1.5 collective-permute-start.24
  175.1 13.5 %shard_map.95 = (bf16[5,3,128,128]{3,2,1,0:T(8,128)(2,1)S(1)}, bf16[5,3,128,128]{3,2,1,0:T(8,128)(2,1)S(1)}, bf16[5,3,128,128]{3,2,1,0:T(8,128)(2,1)S(1)}, bf16[...) custom-call(s32[3,16,2]{2,1,0:T(8,128)S(1)} %fusion.20.places, ...), custom_call_target="tpu_custom_call" | custom-call | flops 3221225472 | bytes 17500000 | tf_op jit(solution)/shard_map/pallas_call | solution.py:156
  191.7 1.3 copy-done.41
  193.0 18.7 %shard_map.96 = (bf16[2,128,2048]{2,1,0:T(8,128)(2,1)S(1)}, bf16[2,128,2048]{2,1,0:T(8,128)(2,1)S(1)}, bf16[2,128,2048]{2,1,0:T(8,128)(2,1)S(1)}, bf16[2,128,204...) custom-call(s32[7,16,2]{2,1,0:T(8,128)S(1)} %pad_add_fusion.places, ...), custom_call_target="tpu_custom_call" | custom-call | flops 3758096384 | bytes 20000000 | tf_op jit(solution)/shard_map/pallas_call | solution.py:267
  212.7 1.1 copy-done.50
  215.7 1.0 copy-done.55
  216.8 11.8 %collective-permute-done.23.refs_3_.refs_1_.refs_2_ = bf16[5,4,128,128]{3,2,1,0:T(8,128)(2,1)S(1)} collective-permute-done((bf16[5,4,128,128]{3,2,1,0:T(8,128)(2,1)S(1)}, bf16[5,4,128,128]{3,2,1,0:T(8,128)(2,1)S(1)}, u32[]{:S(2)}, u32[]{:S(2)}) %collective-permute-start.23) | collective-permute-done | bytes 655392 | tf_op jit(solution)/shard_map/along_z3/ppermute | solution.py:375
  228.6 2.1 collective-permute-done.24.refs_4_.refs_1_.refs_3_
  232.1 1.3 collective-permute-start.33
  233.5 2.5 collective-permute-done.28
  236.1 3.3 fusion.8
  239.4 1.5 collective-permute-start.30
  240.8 16.5 %collective-permute-done.33 = bf16[2,128,2048]{2,1,0:T(8,128)(2,1)} collective-permute-done((bf16[2,128,2048]{2,1,0:T(8,128)(2,1)}, bf16[2,128,2048]{2,1,0:T(8,128)(2,1)}, u32[]{:S(2)}, u32[]{:S(2)}) %collective-permute-start.33) | collective-permute-done | bytes 1048608 | tf_op jit(solution)/shard_map/wide1/ppermute | solution.py:383
  257.3 2.0 fusion.13.refs_1_
  259.3 2.0 fusion.12.refs_0_
  262.8 1.2 collective-permute-start.34
  265.2 1.4 collective-permute-start.38
  266.6 9.2 %collective-permute-done.34 = bf16[128,2048]{1,0:T(8,128)(2,1)} collective-permute-done((bf16[128,2048]{1,0:T(8,128)(2,1)}, bf16[128,2048]{1,0:T(8,128)(2,1)}, u32[]{:S(2)}, u32[]{:S(2)}) %collective-permute-start.34) | collective-permute-done | bytes 524320 | tf_op jit(solution)/shard_map/wide1/ppermute | solution.py:383
  275.8 1.4 fusion.7
  277.3 1.6 fusion.6
  278.9 19.3 %collective-permute-done.39 = bf16[2,128,2048]{2,1,0:T(8,128)(2,1)S(1)} collective-permute-done((bf16[2,128,2048]{2,1,0:T(8,128)(2,1)}, bf16[2,128,2048]{2,1,0:T(8,128)(2,1)S(1)}, u32[]{:S(2)}, u32[]{:S(2)}) %collective-permute-start.39) | collective-permute-done | bytes 1048608 | tf_op jit(solution)/shard_map/wide1/ppermute | solution.py:383
  298.2 1.1 fusion.15.refs_1_
  299.3 1.1 fusion.14.refs_0_
  301.2 1.2 collective-permute-start.40
  305.1 1.5 collective-permute-start.37
  306.5 6.7 %collective-permute-done.40 = bf16[128,2048]{1,0:T(8,128)(2,1)S(1)} collective-permute-done((bf16[128,2048]{1,0:T(8,128)(2,1)}, bf16[128,2048]{1,0:T(8,128)(2,1)S(1)}, u32[]{:S(2)}, u32[]{:S(2)}) %collective-permute-start.40) | collective-permute-done | bytes 524320 | tf_op jit(solution)/shard_map/wide1/ppermute | solution.py:383
  313.3 1.2 bitcast_add_fusion.1
  314.8 1.4 bitcast_add_fusion
  318.6 1.1 copy-done.15
  320.7 2.6 shard_map.101
  323.3 4.3 %collective-permute-done.36 = bf16[128,2048]{1,0:T(8,128)(2,1)} collective-permute-done((bf16[128,2048]{1,0:T(8,128)(2,1)}, bf16[128,2048]{1,0:T(8,128)(2,1)}, u32[]{:S(2)}, u32[]{:S(2)}) %collective-permute-start.36) | collective-permute-done | bytes 524320 | tf_op jit(solution)/shard_map/along_z2/ppermute | solution.py:375
  327.7 21.3 %collective-permute-done.37 = bf16[128,2048]{1,0:T(8,128)(2,1)} collective-permute-done((bf16[128,2048]{1,0:T(8,128)(2,1)}, bf16[128,2048]{1,0:T(8,128)(2,1)}, u32[]{:S(2)}, u32[]{:S(2)}) %collective-permute-start.37) | collective-permute-done | bytes 524320 | tf_op jit(solution)/shard_map/along_z3/ppermute | solution.py:375
  348.9 2.9 collective-permute-done.42
  351.8 2.3 fusion.5
  (275 shorter events, 44.6 us)
Async XLA Ops:
  0.6 113.9 %copy-start = (s32[28,16]{0,1:T(8,128)S(1)}, s32[28,16]{0,1:T(8,128)}, u32[]{:S(2)}) copy-start(s32[28,16]{0,1:T(8,128)} %param.8) | copy-start | bytes 5380
  1.7 12.7 %copy-start.28 = (bf16[64,2048]{1,0:T(8,128)(2,1)}, bf16[64,2048]{1,0:T(8,128)(2,1)S(1)}, u32[]{:S(2)}) copy-start(bf16[64,2048]{1,0:T(8,128)(2,1)S(1)} %get-tuple-element.103.refs_0_) | copy-start | bytes 786436
  1.7 14.8 %copy-start.25 = (bf16[64,2048]{1,0:T(8,128)(2,1)}, bf16[64,2048]{1,0:T(8,128)(2,1)S(1)}, u32[]{:S(2)}) copy-start(bf16[64,2048]{1,0:T(8,128)(2,1)S(1)} %get-tuple-element.102.refs_1_) | copy-start | bytes 786436
  1.7 12.7 %collective-permute-start = (bf16[64,2048]{1,0:T(8,128)(2,1)S(1)}, bf16[64,2048]{1,0:T(8,128)(2,1)S(1)}, u32[]{:S(2)}, u32[]{:S(2)}) collective-permute-start(bf16[64,2048]{1,0:T(8,128)(2,1)S(1)} %get-tuple-element.103.refs_0_), channel_id=1, source_target_pairs={{0,1},{1,0},{2,3},{3,2},{4,5},{5,4},{6,7},{7,6},{8,9},{9,8},{10,11... | collective-permute-start | bytes 786440 | tf_op jit(solution)/shard_map/wide1/ppermute | solution.py:383
  3.0 14.5 %collective-permute-start.6 = (bf16[128,2048]{1,0:T(8,128)(2,1)}, bf16[128,2048]{1,0:T(8,128)(2,1)}, u32[]{:S(2)}, u32[]{:S(2)}) collective-permute-start(bf16[128,2048]{1,0:T(8,128)(2,1)} %param.5), channel_id=1, source_target_pairs={{0,24},{4,28},{8,0},{12,4},{16,8},{20,12},{24,16},{28,20},{1,25},{... | collective-permute-start | bytes 1572872 | tf_op jit(solution)/shard_map/along_z3/ppermute | solution.py:375
  3.2 13.3 %collective-permute-start.1 = (bf16[64,2048]{1,0:T(8,128)(2,1)S(1)}, bf16[64,2048]{1,0:T(8,128)(2,1)S(1)}, u32[]{:S(2)}, u32[]{:S(2)}) collective-permute-start(bf16[64,2048]{1,0:T(8,128)(2,1)S(1)} %get-tuple-element.102.refs_1_), channel_id=1, source_target_pairs={{0,2},{1,3},{2,0},{3,1},{4,6},{5,7},{6,4},{7,5},{8,10},{9,11},{10,... | collective-permute-start | bytes 786440 | tf_op jit(solution)/shard_map/wide2/ppermute | solution.py:383
  3.4 23.8 %collective-permute-start.4 = (bf16[128,2048]{1,0:T(8,128)(2,1)}, bf16[128,2048]{1,0:T(8,128)(2,1)}, u32[]{:S(2)}, u32[]{:S(2)}) collective-permute-start(bf16[128,2048]{1,0:T(8,128)(2,1)} %param.5), channel_id=1, source_target_pairs={{0,8},{4,12},{8,16},{12,20},{16,24},{20,28},{24,0},{28,4},{1,9},{5... | collective-permute-start | bytes 1572872 | tf_op jit(solution)/shard_map/along_z1/ppermute | solution.py:375
  4.7 42.8 %collective-permute-start.5 = (bf16[128,2048]{1,0:T(8,128)(2,1)}, bf16[128,2048]{1,0:T(8,128)(2,1)}, u32[]{:S(2)}, u32[]{:S(2)}) collective-permute-start(bf16[128,2048]{1,0:T(8,128)(2,1)} %param.5), channel_id=1, source_target_pairs={{0,16},{4,20},{8,24},{12,28},{16,0},{20,4},{24,8},{28,12},{1,17},{... | collective-permute-start | bytes 1572872 | tf_op jit(solution)/shard_map/along_z2/ppermute | solution.py:375
  14.4 35.4 %copy-start.57 = (bf16[5,4,128,128]{3,2,1,0:T(8,128)(2,1)}, bf16[5,4,128,128]{3,2,1,0:T(8,128)(2,1)S(1)}, u32[]{:S(2)}) copy-start(bf16[5,4,128,128]{3,2,1,0:T(8,128)(2,1)S(1)} %get-tuple-element.49.refs_0_) | copy-start | bytes 1966084
  14.4 35.4 %copy-start.24 = (bf16[5,4,128,128]{3,2,1,0:T(8,128)(2,1)}, bf16[5,4,128,128]{3,2,1,0:T(8,128)(2,1)S(1)}, u32[]{:S(2)}) copy-start(bf16[5,4,128,128]{3,2,1,0:T(8,128)(2,1)S(1)} %get-tuple-element.44.refs_4_.refs_0_) | copy-start | bytes 1966084
  14.4 110.5 %copy-start.16 = (bf16[5,7,128,128]{3,2,1,0:T(8,128)(2,1)}, bf16[5,7,128,128]{3,2,1,0:T(8,128)(2,1)S(1)}, u32[]{:S(2)}) copy-start(bf16[5,7,128,128]{3,2,1,0:T(8,128)(2,1)S(1)} %get-tuple-element.47.refs_12_.refs_0_.refs_9_) | copy-start | bytes 3440644
  15.3 34.5 %collective-permute-start.2 = (bf16[128,2048]{1,0:T(8,128)(2,1)S(1)}, bf16[128,2048]{1,0:T(8,128)(2,1)S(1)}, u32[]{:S(2)}, u32[]{:S(2)}) collective-permute-start(bf16[128,2048]{1,0:T(8,128)(2,1)S(1)} %pad_maximum_fusion.4), channel_id=1, source_target_pairs={{0,2},{1,3},{2,0},{3,1},{4,6},{5,7},{6,4},{7,5},{8,10},{9,11},{10,... | collective-permute-start | bytes 1572872 | tf_op jit(solution)/shard_map/wide2/ppermute | solution.py:383
  17.3 32.5 %collective-permute-start.3 = (bf16[128,2048]{1,0:T(8,128)(2,1)S(1)}, bf16[128,2048]{1,0:T(8,128)(2,1)S(1)}, u32[]{:S(2)}, u32[]{:S(2)}) collective-permute-start(bf16[128,2048]{1,0:T(8,128)(2,1)S(1)} %pad_maximum_fusion.5), channel_id=1, source_target_pairs={{0,1},{1,0},{2,3},{3,2},{4,5},{5,4},{6,7},{7,6},{8,9},{9,8},{10,11... | collective-permute-start | bytes 1572872 | tf_op jit(solution)/shard_map/wide1/ppermute | solution.py:383
  50.8 17.5 %collective-permute-start.8 = (bf16[192,2048]{1,0:T(8,128)(2,1)}, bf16[192,2048]{1,0:T(8,128)(2,1)S(1)}, u32[]{:S(2)}, u32[]{:S(2)}) collective-permute-start(bf16[192,2048]{1,0:T(8,128)(2,1)} %get-tuple-element.46.refs_7_), channel_id=1, source_target_pairs={{0,2},{1,3},{2,0},{3,1},{4,6},{5,7},{6,4},{7,5},{8,10},{9,11},{10,... | collective-permute-start | bytes 2359304 | tf_op jit(solution)/shard_map/wide2/ppermute | solution.py:383
  51.0 18.8 %collective-permute-start.7 = (bf16[192,2048]{1,0:T(8,128)(2,1)}, bf16[192,2048]{1,0:T(8,128)(2,1)}, u32[]{:S(2)}, u32[]{:S(2)}) collective-permute-start(bf16[192,2048]{1,0:T(8,128)(2,1)} %get-tuple-element.45.refs_6_), channel_id=1, source_target_pairs={{0,1},{1,0},{2,3},{3,2},{4,5},{5,4},{6,7},{7,6},{8,9},{9,8},{10,11... | collective-permute-start | bytes 2359304 | tf_op jit(solution)/shard_map/wide1/ppermute | solution.py:383
  51.2 21.7 %collective-permute-start.11 = (bf16[5,4,128,128]{3,2,1,0:T(8,128)(2,1)}, bf16[5,4,128,128]{3,2,1,0:T(8,128)(2,1)}, u32[]{:S(2)}, u32[]{:S(2)}) collective-permute-start(bf16[5,4,128,128]{3,2,1,0:T(8,128)(2,1)} %shard_map.86), channel_id=1, source_target_pairs={{0,8},{4,12},{8,16},{12,20},{16,24},{20,28},{24,0},{28,4},{1,9},{5... | collective-permute-start | bytes 1966088 | tf_op jit(solution)/shard_map/along_z1/ppermute | solution.py:375
  56.7 11.6 %copy-start.3 = (bf16[192,2048]{1,0:T(8,128)(2,1)S(1)}, bf16[192,2048]{1,0:T(8,128)(2,1)}, u32[]{:S(2)}) copy-start(bf16[192,2048]{1,0:T(8,128)(2,1)} %get-tuple-element.46.refs_7_) | copy-start | bytes 2359300
  56.7 45.1 %collective-permute-start.13 = (bf16[5,4,128,128]{3,2,1,0:T(8,128)(2,1)}, bf16[5,4,128,128]{3,2,1,0:T(8,128)(2,1)}, u32[]{:S(2)}, u32[]{:S(2)}) collective-permute-start(bf16[5,4,128,128]{3,2,1,0:T(8,128)(2,1)} %shard_map.88), channel_id=1, source_target_pairs={{0,24},{4,28},{8,0},{12,4},{16,8},{20,12},{24,16},{28,20},{1,25},{... | collective-permute-start | bytes 1966088 | tf_op jit(solution)/shard_map/along_z3/ppermute | solution.py:375
  56.7 13.2 %copy-start.2 = (bf16[192,2048]{1,0:T(8,128)(2,1)S(1)}, bf16[192,2048]{1,0:T(8,128)(2,1)}, u32[]{:S(2)}) copy-start(bf16[192,2048]{1,0:T(8,128)(2,1)} %get-tuple-element.45.refs_6_) | copy-start | bytes 2359300
  56.7 56.6 %collective-permute-start.12 = (bf16[5,4,128,128]{3,2,1,0:T(8,128)(2,1)}, bf16[5,4,128,128]{3,2,1,0:T(8,128)(2,1)}, u32[]{:S(2)}, u32[]{:S(2)}) collective-permute-start(bf16[5,4,128,128]{3,2,1,0:T(8,128)(2,1)} %shard_map.87), channel_id=1, source_target_pairs={{0,16},{4,20},{8,24},{12,28},{16,0},{20,4},{24,8},{28,12},{1,17},{... | collective-permute-start | bytes 1966088 | tf_op jit(solution)/shard_map/along_z2/ppermute | solution.py:375
  68.2 56.7 %copy-start.21 = (bf16[192,2048]{1,0:T(8,128)(2,1)}, bf16[192,2048]{1,0:T(8,128)(2,1)S(1)}, u32[]{:S(2)}) copy-start(bf16[192,2048]{1,0:T(8,128)(2,1)S(1)} %collective-permute-done.8.refs_9_) | copy-start | bytes 2359300
  69.6 55.4 %collective-permute-start.10 = (bf16[384,2048]{1,0:T(8,128)(2,1)}, bf16[384,2048]{1,0:T(8,128)(2,1)}, u32[]{:S(2)}, u32[]{:S(2)}) collective-permute-start(bf16[384,2048]{1,0:T(8,128)(2,1)} %pad_maximum_fusion.1), channel_id=1, source_target_pairs={{0,1},{1,0},{2,3},{3,2},{4,5},{5,4},{6,7},{7,6},{8,9},{9,8},{10,11... | collective-permute-start | bytes 4718600 | tf_op jit(solution)/shard_map/wide1/ppermute | solution.py:383
  72.3 52.7 %collective-permute-start.9 = (bf16[384,2048]{1,0:T(8,128)(2,1)}, bf16[384,2048]{1,0:T(8,128)(2,1)}, u32[]{:S(2)}, u32[]{:S(2)}) collective-permute-start(bf16[384,2048]{1,0:T(8,128)(2,1)} %pad_maximum_fusion), channel_id=1, source_target_pairs={{0,2},{1,3},{2,0},{3,1},{4,6},{5,7},{6,4},{7,5},{8,10},{9,11},{10,... | collective-permute-start | bytes 4718600 | tf_op jit(solution)/shard_map/wide2/ppermute | solution.py:383
  72.9 41.0 %collective-permute-start.15 = (bf16[5,4,128,128]{3,2,1,0:T(8,128)(2,1)}, bf16[5,4,128,128]{3,2,1,0:T(8,128)(2,1)}, u32[]{:S(2)}, u32[]{:S(2)}) collective-permute-start(bf16[5,4,128,128]{3,2,1,0:T(8,128)(2,1)} %collective-permute-done.11.refs_2_.refs_13_.refs_1_), channel_id=1, source_target_pairs={{0,4},{4,0},{8,12},{12,8},{16,20},{20,16},{24,28},{28,24},{1,5},{5... | collective-permute-start | bytes 1966088 | tf_op jit(solution)/shard_map/swap/ppermute | solution.py:379
  113.3 5.9 %collective-permute-start.14 = (bf16[5,7,128,128]{3,2,1,0:T(8,128)(2,1)}, bf16[5,7,128,128]{3,2,1,0:T(8,128)(2,1)}, u32[]{:S(2)}, u32[]{:S(2)}) collective-permute-start(bf16[5,7,128,128]{3,2,1,0:T(8,128)(2,1)} %shard_map.89), channel_id=1, source_target_pairs={{0,4},{4,0},{8,12},{12,8},{16,20},{20,16},{24,28},{28,24},{1,5},{5... | collective-permute-start | bytes 3440648 | tf_op jit(solution)/shard_map/swap/ppermute | solution.py:379
  113.9 3.8 %collective-permute-start.17 = (bf16[5,4,128,128]{3,2,1,0:T(8,128)(2,1)}, bf16[5,4,128,128]{3,2,1,0:T(8,128)(2,1)}, u32[]{:S(2)}, u32[]{:S(2)}) collective-permute-start(bf16[5,4,128,128]{3,2,1,0:T(8,128)(2,1)} %collective-permute-done.13.refs_3_.refs_15_.refs_1_), channel_id=1, source_target_pairs={{0,4},{4,0},{8,12},{12,8},{16,20},{20,16},{24,28},{28,24},{1,5},{5... | collective-permute-start | bytes 1966088 | tf_op jit(solution)/shard_map/swap/ppermute | solution.py:379
  114.0 4.4 %collective-permute-start.16 = (bf16[5,4,128,128]{3,2,1,0:T(8,128)(2,1)}, bf16[5,4,128,128]{3,2,1,0:T(8,128)(2,1)}, u32[]{:S(2)}, u32[]{:S(2)}) collective-permute-start(bf16[5,4,128,128]{3,2,1,0:T(8,128)(2,1)} %collective-permute-done.12.refs_1_.refs_14_.refs_2_), channel_id=1, source_target_pairs={{0,4},{4,0},{8,12},{12,8},{16,20},{20,16},{24,28},{28,24},{1,5},{5... | collective-permute-start | bytes 1966088 | tf_op jit(solution)/shard_map/swap/ppermute | solution.py:379
  117.7 35.2 %collective-permute-start.18 = (bf16[5,3,128,128]{3,2,1,0:T(8,128)(2,1)}, bf16[5,3,128,128]{3,2,1,0:T(8,128)(2,1)S(1)}, u32[]{:S(2)}, u32[]{:S(2)}) collective-permute-start(bf16[5,3,128,128]{3,2,1,0:T(8,128)(2,1)} %shard_map.91), channel_id=1, source_target_pairs={{0,8},{4,12},{8,16},{12,20},{16,24},{20,28},{24,0},{28,4},{1,9},{5... | collective-permute-start | bytes 1474568 | tf_op jit(solution)/shard_map/along_z1/ppermute | solution.py:375
  118.4 35.3 %collective-permute-start.20 = (bf16[5,3,128,128]{3,2,1,0:T(8,128)(2,1)}, bf16[5,3,128,128]{3,2,1,0:T(8,128)(2,1)}, u32[]{:S(2)}, u32[]{:S(2)}) collective-permute-start(bf16[5,3,128,128]{3,2,1,0:T(8,128)(2,1)} %shard_map.93), channel_id=1, source_target_pairs={{0,24},{4,28},{8,0},{12,4},{16,8},{20,12},{24,16},{28,20},{1,25},{... | collective-permute-start | bytes 1474568 | tf_op jit(solution)/shard_map/along_z3/ppermute | solution.py:375
  119.2 42.1 %collective-permute-start.19 = (bf16[5,3,128,128]{3,2,1,0:T(8,128)(2,1)}, bf16[5,3,128,128]{3,2,1,0:T(8,128)(2,1)}, u32[]{:S(2)}, u32[]{:S(2)}) collective-permute-start(bf16[5,3,128,128]{3,2,1,0:T(8,128)(2,1)} %shard_map.92), channel_id=1, source_target_pairs={{0,16},{4,20},{8,24},{12,28},{16,0},{20,4},{24,8},{28,12},{1,17},{... | collective-permute-start | bytes 1474568 | tf_op jit(solution)/shard_map/along_z2/ppermute | solution.py:375
  161.3 6.1 %collective-permute-start.21 = (bf16[4,5,4,128,128]{4,3,2,1,0:T(8,128)(2,1)}, bf16[4,5,4,128,128]{4,3,2,1,0:T(8,128)(2,1)S(1)}, u32[]{:S(2)}, u32[]{:S(2)}) collective-permute-start(bf16[4,5,4,128,128]{4,3,2,1,0:T(8,128)(2,1)} %shard_map.94), channel_id=1, source_target_pairs={{0,4},{4,0},{8,12},{12,8},{16,20},{20,16},{24,28},{28,24},{1,5},{5... | collective-permute-start | bytes 7864328 | tf_op jit(solution)/shard_map/swap/ppermute | solution.py:379
  162.7 10.7 %collective-permute-start.25 = (bf16[5,3,128,128]{3,2,1,0:T(8,128)(2,1)S(1)}, bf16[5,3,128,128]{3,2,1,0:T(8,128)(2,1)S(1)}, u32[]{:S(2)}, u32[]{:S(2)}) collective-permute-start(bf16[5,3,128,128]{3,2,1,0:T(8,128)(2,1)S(1)} %copy-done.39), channel_id=1, source_target_pairs={{0,4},{4,0},{8,12},{12,8},{16,20},{20,16},{24,28},{28,24},{1,5},{5... | collective-permute-start | bytes 1474568 | tf_op jit(solution)/shard_map/swap/ppermute | solution.py:379
  163.6 11.4 %collective-permute-start.27 = (bf16[5,3,128,128]{3,2,1,0:T(8,128)(2,1)}, bf16[5,3,128,128]{3,2,1,0:T(8,128)(2,1)S(1)}, u32[]{:S(2)}, u32[]{:S(2)}) collective-permute-start(bf16[5,3,128,128]{3,2,1,0:T(8,128)(2,1)} %collective-permute-done.20.refs_3_.refs_15_.refs_12_), channel_id=1, source_target_pairs={{0,4},{4,0},{8,12},{12,8},{16,20},{20,16},{24,28},{28,24},{1,5},{5... | collective-permute-start | bytes 1474568 | tf_op jit(solution)/shard_map/swap/ppermute | solution.py:379
  163.6 11.4 %collective-permute-start.26 = (bf16[5,3,128,128]{3,2,1,0:T(8,128)(2,1)}, bf16[5,3,128,128]{3,2,1,0:T(8,128)(2,1)S(1)}, u32[]{:S(2)}, u32[]{:S(2)}) collective-permute-start(bf16[5,3,128,128]{3,2,1,0:T(8,128)(2,1)} %collective-permute-done.19.refs_2_.refs_14_.refs_11_), channel_id=1, source_target_pairs={{0,4},{4,0},{8,12},{12,8},{16,20},{20,16},{24,28},{28,24},{1,5},{5... | collective-permute-start | bytes 1474568 | tf_op jit(solution)/shard_map/swap/ppermute | solution.py:379
  170.2 18.4 %copy-start.14 = (bf16[5,4,128,128]{3,2,1,0:T(8,128)(2,1)}, bf16[5,4,128,128]{3,2,1,0:T(8,128)(2,1)S(1)}, u32[]{:S(2)}) copy-start(bf16[5,4,128,128]{3,2,1,0:T(8,128)(2,1)S(1)} %get-tuple-element.87.refs_20_.refs_0_) | copy-start | bytes 1966084
  170.2 46.5 %collective-permute-start.22 = (bf16[5,4,128,128]{3,2,1,0:T(8,128)(2,1)S(1)}, bf16[5,4,128,128]{3,2,1,0:T(8,128)(2,1)S(1)}, u32[]{:S(2)}, u32[]{:S(2)}) collective-permute-start(bf16[5,4,128,128]{3,2,1,0:T(8,128)(2,1)S(1)} %get-tuple-element.86.refs_21_), channel_id=1, source_target_pairs={{0,16},{4,20},{8,24},{12,28},{16,0},{20,4},{24,8},{28,12},{1,17},{... | collective-permute-start | bytes 1966088 | tf_op jit(solution)/shard_map/along_z2/ppermute | solution.py:375
  173.4 55.1 %collective-permute-start.23 = (bf16[5,4,128,128]{3,2,1,0:T(8,128)(2,1)S(1)}, bf16[5,4,128,128]{3,2,1,0:T(8,128)(2,1)S(1)}, u32[]{:S(2)}, u32[]{:S(2)}) collective-permute-start(bf16[5,4,128,128]{3,2,1,0:T(8,128)(2,1)S(1)} %get-tuple-element.85.refs_22_), channel_id=1, source_target_pairs={{0,24},{4,28},{8,0},{12,4},{16,8},{20,12},{24,16},{28,20},{1,25},{... | collective-permute-start | bytes 1966088 | tf_op jit(solution)/shard_map/along_z3/ppermute | solution.py:375
  173.4 57.3 %collective-permute-start.24 = (bf16[5,4,128,128]{3,2,1,0:T(8,128)(2,1)S(1)}, bf16[5,4,128,128]{3,2,1,0:T(8,128)(2,1)S(1)}, u32[]{:S(2)}, u32[]{:S(2)}) collective-permute-start(bf16[5,4,128,128]{3,2,1,0:T(8,128)(2,1)S(1)} %get-tuple-element.84.refs_23_), channel_id=1, source_target_pairs={{0,8},{4,12},{8,16},{12,20},{16,24},{20,28},{24,0},{28,4},{1,9},{5... | collective-permute-start | bytes 1966088 | tf_op jit(solution)/shard_map/along_z1/ppermute | solution.py:375
  216.8 13.9 %copy-start.4 = (bf16[5,4,128,128]{3,2,1,0:T(8,128)(2,1)}, bf16[5,4,128,128]{3,2,1,0:T(8,128)(2,1)S(1)}, u32[]{:S(2)}) copy-start(bf16[5,4,128,128]{3,2,1,0:T(8,128)(2,1)S(1)} %collective-permute-done.22.refs_2_.refs_1_) | copy-start | bytes 1966084
  231.6 4.5 %collective-permute-start.28 = (bf16[4,5,3,128,128]{4,3,2,1,0:T(8,128)(2,1)}, bf16[4,5,3,128,128]{4,3,2,1,0:T(8,128)(2,1)}, u32[]{:S(2)}, u32[]{:S(2)}) collective-permute-start(bf16[4,5,3,128,128]{4,3,2,1,0:T(8,128)(2,1)} %shard_map.97), channel_id=1, source_target_pairs={{0,4},{4,0},{8,12},{12,8},{16,20},{20,16},{24,28},{28,24},{1,5},{5... | collective-permute-start | bytes 5898248 | tf_op jit(solution)/shard_map/swap/ppermute | solution.py:379
  232.1 25.2 %collective-permute-start.33 = (bf16[2,128,2048]{2,1,0:T(8,128)(2,1)}, bf16[2,128,2048]{2,1,0:T(8,128)(2,1)}, u32[]{:S(2)}, u32[]{:S(2)}) collective-permute-start(bf16[2,128,2048]{2,1,0:T(8,128)(2,1)} %get-tuple-element.71), channel_id=1, source_target_pairs={{0,1},{1,0},{2,3},{3,2},{4,5},{5,4},{6,7},{7,6},{8,9},{9,8},{10,11... | collective-permute-start | bytes 3145736 | tf_op jit(solution)/shard_map/wide1/ppermute | solution.py:383
  233.4 25.9 %collective-permute-start.32 = (bf16[2,128,2048]{2,1,0:T(8,128)(2,1)}, bf16[2,128,2048]{2,1,0:T(8,128)(2,1)}, u32[]{:S(2)}, u32[]{:S(2)}) collective-permute-start(bf16[2,128,2048]{2,1,0:T(8,128)(2,1)} %get-tuple-element.69), channel_id=1, source_target_pairs={{0,2},{1,3},{2,0},{3,1},{4,6},{5,7},{6,4},{7,5},{8,10},{9,11},{10,... | collective-permute-start | bytes 3145736 | tf_op jit(solution)/shard_map/wide2/ppermute | solution.py:383
  239.3 21.9 %collective-permute-start.31 = (bf16[5,3,128,128]{3,2,1,0:T(8,128)(2,1)}, bf16[5,3,128,128]{3,2,1,0:T(8,128)(2,1)S(1)}, u32[]{:S(2)}, u32[]{:S(2)}) collective-permute-start(bf16[5,3,128,128]{3,2,1,0:T(8,128)(2,1)} %shard_map.100), channel_id=1, source_target_pairs={{0,8},{4,12},{8,16},{12,20},{16,24},{20,28},{24,0},{28,4},{1,9},{5... | collective-permute-start | bytes 1474568 | tf_op jit(solution)/shard_map/along_z1/ppermute | solution.py:375
  239.4 19.9 %copy-start.53 = (bf16[2,128,2048]{2,1,0:T(8,128)(2,1)S(1)}, bf16[2,128,2048]{2,1,0:T(8,128)(2,1)}, u32[]{:S(2)}) copy-start(bf16[2,128,2048]{2,1,0:T(8,128)(2,1)} %copy-done.52) | copy-start | bytes 3145732
  239.4 21.9 %collective-permute-start.30 = (bf16[5,3,128,128]{3,2,1,0:T(8,128)(2,1)}, bf16[5,3,128,128]{3,2,1,0:T(8,128)(2,1)S(1)}, u32[]{:S(2)}, u32[]{:S(2)}) collective-permute-start(bf16[5,3,128,128]{3,2,1,0:T(8,128)(2,1)} %shard_map.99), channel_id=1, source_target_pairs={{0,24},{4,28},{8,0},{12,4},{16,8},{20,12},{24,16},{28,20},{1,25},{... | collective-permute-start | bytes 1474568 | tf_op jit(solution)/shard_map/along_z3/ppermute | solution.py:375
  262.8 13.0 %collective-permute-start.34 = (bf16[128,2048]{1,0:T(8,128)(2,1)}, bf16[128,2048]{1,0:T(8,128)(2,1)}, u32[]{:S(2)}, u32[]{:S(2)}) collective-permute-start(bf16[128,2048]{1,0:T(8,128)(2,1)} %get-tuple-element.72.refs_2_), channel_id=1, source_target_pairs={{0,1},{1,0},{2,3},{3,2},{4,5},{5,4},{6,7},{7,6},{8,9},{9,8},{10,11... | collective-permute-start | bytes 1572872 | tf_op jit(solution)/shard_map/wide1/ppermute | solution.py:383
  264.0 36.4 %collective-permute-start.29 = (bf16[5,3,128,128]{3,2,1,0:T(8,128)(2,1)}, bf16[5,3,128,128]{3,2,1,0:T(8,128)(2,1)S(1)}, u32[]{:S(2)}, u32[]{:S(2)}) collective-permute-start(bf16[5,3,128,128]{3,2,1,0:T(8,128)(2,1)} %shard_map.98), channel_id=1, source_target_pairs={{0,16},{4,20},{8,24},{12,28},{16,0},{20,4},{24,8},{28,12},{1,17},{... | collective-permute-start | bytes 1474568 | tf_op jit(solution)/shard_map/along_z2/ppermute | solution.py:375
  264.1 13.3 %collective-permute-start.35 = (bf16[128,2048]{1,0:T(8,128)(2,1)S(1)}, bf16[128,2048]{1,0:T(8,128)(2,1)}, u32[]{:S(2)}, u32[]{:S(2)}) collective-permute-start(bf16[128,2048]{1,0:T(8,128)(2,1)S(1)} %copy-done.77), channel_id=1, source_target_pairs={{0,2},{1,3},{2,0},{3,1},{4,6},{5,7},{6,4},{7,5},{8,10},{9,11},{10,... | collective-permute-start | bytes 1572872 | tf_op jit(solution)/shard_map/wide2/ppermute | solution.py:383
  264.1 11.7 %copy-start.54 = (bf16[2,128,2048]{2,1,0:T(8,128)(2,1)S(1)}, bf16[2,128,2048]{2,1,0:T(8,128)(2,1)}, u32[]{:S(2)}) copy-start(bf16[2,128,2048]{2,1,0:T(8,128)(2,1)} %copy-done.52) | copy-start | bytes 3145732
  264.2 34.0 %collective-permute-start.39 = (bf16[2,128,2048]{2,1,0:T(8,128)(2,1)}, bf16[2,128,2048]{2,1,0:T(8,128)(2,1)S(1)}, u32[]{:S(2)}, u32[]{:S(2)}) collective-permute-start(bf16[2,128,2048]{2,1,0:T(8,128)(2,1)} %get-tuple-element.79), channel_id=1, source_target_pairs={{0,1},{1,0},{2,3},{3,2},{4,5},{5,4},{6,7},{7,6},{8,9},{9,8},{10,11... | collective-permute-start | bytes 3145736 | tf_op jit(solution)/shard_map/wide1/ppermute | solution.py:383
  265.2 34.1 %collective-permute-start.38 = (bf16[2,128,2048]{2,1,0:T(8,128)(2,1)}, bf16[2,128,2048]{2,1,0:T(8,128)(2,1)S(1)}, u32[]{:S(2)}, u32[]{:S(2)}) collective-permute-start(bf16[2,128,2048]{2,1,0:T(8,128)(2,1)} %get-tuple-element.77), channel_id=1, source_target_pairs={{0,2},{1,3},{2,0},{3,1},{4,6},{5,7},{6,4},{7,5},{8,10},{9,11},{10,... | collective-permute-start | bytes 3145736 | tf_op jit(solution)/shard_map/wide2/ppermute | solution.py:383
  277.2 20.9 %copy-start.81 = (bf16[2,128,2048]{2,1,0:T(8,128)(2,1)S(1)}, bf16[2,128,2048]{2,1,0:T(8,128)(2,1)}, u32[]{:S(2)}) copy-start(bf16[2,128,2048]{2,1,0:T(8,128)(2,1)} %get-tuple-element.78) | copy-start | bytes 3145732
  277.3 21.9 %copy-start.83 = (bf16[2,128,2048]{2,1,0:T(8,128)(2,1)S(1)}, bf16[2,128,2048]{2,1,0:T(8,128)(2,1)}, u32[]{:S(2)}) copy-start(bf16[2,128,2048]{2,1,0:T(8,128)(2,1)} %get-tuple-element.74) | copy-start | bytes 3145732
  301.2 12.0 %collective-permute-start.40 = (bf16[128,2048]{1,0:T(8,128)(2,1)}, bf16[128,2048]{1,0:T(8,128)(2,1)S(1)}, u32[]{:S(2)}, u32[]{:S(2)}) collective-permute-start(bf16[128,2048]{1,0:T(8,128)(2,1)} %get-tuple-element.80), channel_id=1, source_target_pairs={{0,1},{1,0},{2,3},{3,2},{4,5},{5,4},{6,7},{7,6},{8,9},{9,8},{10,11... | collective-permute-start | bytes 1572872 | tf_op jit(solution)/shard_map/wide1/ppermute | solution.py:383
  303.3 9.9 %copy-start.84 = (bf16[2,128,2048]{2,1,0:T(8,128)(2,1)S(1)}, bf16[2,128,2048]{2,1,0:T(8,128)(2,1)}, u32[]{:S(2)}) copy-start(bf16[2,128,2048]{2,1,0:T(8,128)(2,1)} %get-tuple-element.74) | copy-start | bytes 3145732
  303.3 24.3 %collective-permute-start.36 = (bf16[128,2048]{1,0:T(8,128)(2,1)}, bf16[128,2048]{1,0:T(8,128)(2,1)}, u32[]{:S(2)}, u32[]{:S(2)}) collective-permute-start(bf16[128,2048]{1,0:T(8,128)(2,1)} %shard_map.104), channel_id=1, source_target_pairs={{0,16},{4,20},{8,24},{12,28},{16,0},{20,4},{24,8},{28,12},{1,17},{... | collective-permute-start | bytes 1572872 | tf_op jit(solution)/shard_map/along_z2/ppermute | solution.py:375
  304.1 10.7 %collective-permute-start.41 = (bf16[128,2048]{1,0:T(8,128)(2,1)S(1)}, bf16[128,2048]{1,0:T(8,128)(2,1)}, u32[]{:S(2)}, u32[]{:S(2)}) collective-permute-start(bf16[128,2048]{1,0:T(8,128)(2,1)S(1)} %copy-done.80), channel_id=1, source_target_pairs={{0,2},{1,3},{2,0},{3,1},{4,6},{5,7},{6,4},{7,5},{8,10},{9,11},{10,... | collective-permute-start | bytes 1572872 | tf_op jit(solution)/shard_map/wide2/ppermute | solution.py:383
  305.0 9.8 %copy-start.82 = (bf16[2,128,2048]{2,1,0:T(8,128)(2,1)S(1)}, bf16[2,128,2048]{2,1,0:T(8,128)(2,1)}, u32[]{:S(2)}) copy-start(bf16[2,128,2048]{2,1,0:T(8,128)(2,1)} %get-tuple-element.78) | copy-start | bytes 3145732
  305.0 9.8 %copy-start.86 = (bf16[2,128,2048]{2,1,0:T(8,128)(2,1)S(1)}, bf16[2,128,2048]{2,1,0:T(8,128)(2,1)}, u32[]{:S(2)}) copy-start(bf16[2,128,2048]{2,1,0:T(8,128)(2,1)} %copy-done.85) | copy-start | bytes 3145732
  305.1 43.9 %collective-permute-start.37 = (bf16[128,2048]{1,0:T(8,128)(2,1)}, bf16[128,2048]{1,0:T(8,128)(2,1)}, u32[]{:S(2)}, u32[]{:S(2)}) collective-permute-start(bf16[128,2048]{1,0:T(8,128)(2,1)} %shard_map.105), channel_id=1, source_target_pairs={{0,24},{4,28},{8,0},{12,4},{16,8},{20,12},{24,16},{28,20},{1,25},{... | collective-permute-start | bytes 1572872 | tf_op jit(solution)/shard_map/along_z3/ppermute | solution.py:375
  318.0 33.8 %collective-permute-start.42 = (bf16[128,2048]{1,0:T(8,128)(2,1)}, bf16[128,2048]{1,0:T(8,128)(2,1)S(1)}, u32[]{:S(2)}, u32[]{:S(2)}) collective-permute-start(bf16[128,2048]{1,0:T(8,128)(2,1)} %shard_map.108), channel_id=1, source_target_pairs={{0,8},{4,12},{8,16},{12,20},{16,24},{20,28},{24,0},{28,4},{1,9},{5... | collective-permute-start | bytes 1572872 | tf_op jit(solution)/shard_map/along_z1/ppermute | solution.py:375
  323.3 28.5 %slice-start = ((f32[128,2048]{1,0:T(8,128)}), f32[64,2048]{1,0:T(8,128)S(1)}, s32[]{:S(2)}) async-start(f32[128,2048]{1,0:T(8,128)} %copy-done.78), calls=%async_computation | async-start | bytes 1048576 | tf_op jit(solution)/shard_map/slice | solution.py:478
  323.3 28.5 %slice-start.1 = ((f32[128,2048]{1,0:T(8,128)}), f32[64,2048]{1,0:T(8,128)S(1)}, s32[]{:S(2)}) async-start(f32[128,2048]{1,0:T(8,128)} %copy-done.79), calls=%async_computation.1 | async-start | bytes 1048576 | tf_op jit(solution)/shard_map/slice | solution.py:478
  323.3 30.8 %copy-start.1 = (s32[28,16]{0,1:T(8,128)S(1)}, s32[28,16]{0,1:T(8,128)}, u32[]{:S(2)}) copy-start(s32[28,16]{0,1:T(8,128)} %param.8) | copy-start | bytes 5380
  (73 other events, 183.5 us)

commit v3 on v2

--- a/solution.py
+++ b/solution.py
@@ -403,7 +403,8 @@
     own, *messages = pack_call(nz, bounds, where, gate_blocks, up_blocks, grad_hidden)
 
     half = tokens // 2
-    x_z = {r: along_z(inputs, r) for r in reversed(shifts)}
+    x_z = {1: along_z(inputs, 1), 3: along_z(inputs, 3)}
+    x_z[2] = along_z(x_z[1], 1)
     x_parts, layout = [], []
     for group in ([0], list(range(1, nz))):
         pieces = [inputs if r == 0 else x_z[r] for r in group]
@@ -427,7 +428,7 @@
                 )
             )
 
-    earlier = [x_z[r] for r in shifts]
+    earlier = [x_z[2] for r in shifts]
     weights, other = [], None
     for lo, hi in chunks:
         now, messages = messages[: nz - 1], messages[nz - 1 :]
@@ -461,7 +462,7 @@
         back += [(r, lo, hi) for r in [0, *shifts]]
     hidden, grad_gate, grad_up = unpack_call(nz, back, where, parts, grad_hidden, gate_blocks)
 
-    total, earlier = 0, sent[0]
+    total, moved, earlier = None, [], sent[0]
     step = [a for a, r in zip(sent[-1], shifts) if 2 * r != nz]
     for group, (to_y, to_x, keep_a, keep_b) in zip(groups, dx):
         to_y, to_x = hold([to_y, to_x], *earlier)
@@ -469,19 +470,18 @@
         near_a, pass_a = (keep_a[i].astype(F32) + to_y[i].astype(F32) for i in range(2))
         near_b, pass_b = (keep_b[i].astype(F32) + to_x[i].astype(F32) for i in range(2))
         pass_a, pass_b = hold([pass_a.astype(BF16), pass_b.astype(BF16)], *step)
-        step = sent[-1]
         earlier = [pass_a, pass_b]
         pass_a, pass_b = over_wide(pass_a, 1), over_wide(pass_b, 2)
         halves = near_a + pass_a.astype(F32), near_b + pass_b.astype(F32)
         shares = []
         for i, r in enumerate(group):
             shares.append(jnp.concatenate([a[i * half : (i + 1) * half] for a in halves], axis=0))
-        away = [i for i, r in enumerate(group) if r]
-        ready = [shares[i].astype(BF16) for i in away]
-        ready = [hold([a], sent[-1][shifts.index(group[i])])[0] for a, i in zip(ready, away)]
-        for i, a in zip(away, ready):
-            shares[i] = along_z(a, nz - group[i]).astype(F32)
-        total = total + sum(shares)
+        if not moved:
+            moved = [along_z(*hold([shares[0].astype(BF16)], *sent[-1]), nz - 1)]
+            shares = [shares[1] + moved[0].astype(F32)]
+            step = moved
+        arrived = along_z(shares[0].astype(BF16), nz - (3 if total is not None else 1))
+        total = arrived.astype(F32) if total is None else total + arrived.astype(F32) + shares[1]
     return hidden, total.astype(BF16), grad_gate, grad_up
 
 
@@ -490,7 +490,7 @@
 
     def shards(inputs, gate_blocks, up_blocks, pattern, grad_hidden):
         columns = gate_blocks.shape[0]
-        if narrow % 2 == 0 and columns % (narrow // 2) == 0 and nw == 4:
+        if narrow % 2 == 0 and columns % (narrow // 2) == 0 and narrow == 8 and nw == 4:
             return moved_tokens(
                 narrow, nw, inputs, gate_blocks, up_blocks, pattern, grad_hidden
             )

time: 355 us -> 326 us (0.918)
  the two profiles are of different devices: /device:TPU:21 before, /device:TPU:0 now
where the time goes in v3:
time: 326 us; the launch traced here: 325 us
  waiting for transfers between devices  117 us (36%)
  starting transfers between devices  80.1 us (25%)
  Pallas kernels  51.3 us (16%)
  local copies, waits for them, and re-layouts  45.2 us (14%)
  other arithmetic  29.6 us (9%)
    ppermute x18, waiting for transfers between devices, along_z(): lax.ppermute(a, 'narrow', [(i, (i + 2 * s) % narrow) for i in range(narro...  71.1 us
    ppermute x18, starting transfers between devices, along_z(): lax.ppermute(a, 'narrow', [(i, (i + 2 * s) % narrow) for i in range(narro...  60.6 us
    unnamed x179, local copies, waits for them, and re-layouts  40.1 us
    ppermute x16, waiting for transfers between devices, over_wide(): return lax.ppermute(a, 'wide', [(i, i ^ m) for i in range(nw)])  39.6 us
    pallas_call x2, Pallas kernels, forward_call(): pl.pallas_call(functools.partial(forward_kernel, nz, nw, spd, len(earlier...  29.6 us
    pallas_call x1, Pallas kernels, inputs_call(): pl.pallas_call(functools.partial(inputs_kernel, nz, spd, counts, groups,...  18.7 us
    ppermute x16, starting transfers between devices, over_wide(): return lax.ppermute(a, 'wide', [(i, i ^ m) for i in range(nw)])  18.1 us
    convert_element_type x4, other arithmetic, moved_tokens(): pass_a, pass_b = hold([pass_a.astype(BF16), pass_b.astype(BF16)], *step)  8.18 us
  transfers between devices with their start and end apart: 43, of which 19 were waited for; matrix products, arithmetic and copies ran while one was open for 10% of the time, Pallas kernels for 16%

profile of v3, /device:TPU:0, one launch (start us, length us, event | category | flops | bytes accessed | tf_op | source)
XLA Modules:
  0.0 324.8 jit_solution(7552080599842120931)
XLA Ops:
  0.6 1.1 fusion.23
  1.7 3.0 collective-permute-start
  4.7 1.6 collective-permute-start.4
  6.3 1.5 collective-permute-start.1
  7.8 2.2 collective-permute-start.6
  10.1 1.5 copy-done.41
  11.6 1.5 copy-done.42
  13.1 1.2 copy-done.56
  21.7 1.1 fusion.20
  22.8 10.1 %collective-permute-done.6 = bf16[128,2048]{1,0:T(8,128)(2,1)} collective-permute-done((bf16[128,2048]{1,0:T(8,128)(2,1)}, bf16[128,2048]{1,0:T(8,128)(2,1)}, u32[]{:S(2)}, u32[]{:S(2)}) %collective-permute-start.6) | collective-permute-done | bytes 524320 | tf_op jit(solution)/shard_map/along_z3/ppermute | solution.py:375
  32.9 1.1 fusion.22
  34.0 8.8 %collective-permute-done.5.refs_1_ = bf16[128,2048]{1,0:T(8,128)(2,1)S(1)} collective-permute-done((bf16[128,2048]{1,0:T(8,128)(2,1)}, bf16[128,2048]{1,0:T(8,128)(2,1)S(1)}, u32[]{:S(2)}, u32[]{:S(2)}) %collective-permute-start.5) | collective-permute-done | bytes 524320 | tf_op jit(solution)/shard_map/along_z1/ppermute | solution.py:375
  43.6 1.2 pad_maximum_fusion.2
  45.8 1.5 collective-permute-start.8
  48.5 1.6 collective-permute-start.11
  50.1 2.2 collective-permute-start.13
  52.3 10.9 %collective-permute-done.8.refs_9_ = bf16[192,2048]{1,0:T(8,128)(2,1)S(1)} collective-permute-done((bf16[192,2048]{1,0:T(8,128)(2,1)}, bf16[192,2048]{1,0:T(8,128)(2,1)S(1)}, u32[]{:S(2)}, u32[]{:S(2)}) %collective-permute-start.8) | collective-permute-done | bytes 786464 | tf_op jit(solution)/shard_map/wide2/ppermute | solution.py:383
  63.2 1.3 pad_maximum_fusion.1
  65.1 2.4 pad_maximum_fusion
  67.5 1.5 collective-permute-start.9
  69.0 22.1 %collective-permute-done.12.refs_1_.refs_14_.refs_2_ = bf16[5,4,128,128]{3,2,1,0:T(8,128)(2,1)} collective-permute-done((bf16[5,4,128,128]{3,2,1,0:T(8,128)(2,1)}, bf16[5,4,128,128]{3,2,1,0:T(8,128)(2,1)}, u32[]{:S(2)}, u32[]{:S(2)}) %collective-permute-start.12) | collective-permute-done | bytes 655392 | tf_op jit(solution)/shard_map/along_z2/ppermute | solution.py:375
  95.3 1.6 add_select_fusion
  96.9 12.7 %collective-permute-start.19 = (bf16[5,3,128,128]{3,2,1,0:T(8,128)(2,1)}, bf16[5,3,128,128]{3,2,1,0:T(8,128)(2,1)S(1)}, u32[]{:S(2)}, u32[]{:S(2)}) collective-permute-start(bf16[5,3,128,128]{3,2,1,0:T(8,128)(2,1)} %shard_map.92), channel_id=1, source_target_pairs={{0,16},{4,20},{8,24},{12,28},{16,0},{20,4},{24,8},{28,12},{1,17},{... | collective-permute-start | bytes 1474568 | tf_op jit(solution)/shard_map/along_z2/ppermute | solution.py:375
  110.6 2.8 collective-permute-start.20
  116.3 1.0 copy-done.30
  120.3 16.1 %shard_map.90 = (bf16[5,4,128,128]{3,2,1,0:T(8,128)(2,1)S(1)}, bf16[5,4,128,128]{3,2,1,0:T(8,128)(2,1)S(1)}, bf16[5,4,128,128]{3,2,1,0:T(8,128)(2,1)S(1)}, bf16[...) custom-call(s32[4,16,2]{2,1,0:T(8,128)S(1)} %fusion.16.places, ...), custom_call_target="tpu_custom_call" | custom-call | flops 4294967296 | bytes 20000000 | tf_op jit(solution)/shard_map/pallas_call | solution.py:156
  136.4 1.5 copy-done.21
  145.4 3.6 %collective-permute-done.21 = bf16[4,5,4,128,128]{4,3,2,1,0:T(8,128)(2,1)S(1)} collective-permute-done((bf16[4,5,4,128,128]{4,3,2,1,0:T(8,128)(2,1)}, bf16[4,5,4,128,128]{4,3,2,1,0:T(8,128)(2,1)S(1)}, u32[]{:S(2)}, u32[]{:S(2)}) %collective-permute-start.21) | collective-permute-done | bytes 2621472 | tf_op jit(solution)/shard_map/swap/ppermute | solution.py:379
  149.1 2.7 fusion
  151.8 11.2 %collective-permute-start.22 = (bf16[5,4,128,128]{3,2,1,0:T(8,128)(2,1)S(1)}, bf16[5,4,128,128]{3,2,1,0:T(8,128)(2,1)S(1)}, u32[]{:S(2)}, u32[]{:S(2)}) collective-permute-start(bf16[5,4,128,128]{3,2,1,0:T(8,128)(2,1)S(1)} %get-tuple-element.86.refs_21_), channel_id=1, source_target_pairs={{0,16},{4,20},{8,24},{12,28},{16,0},{20,4},{24,8},{28,12},{1,17},{... | collective-permute-start | bytes 1966088 | tf_op jit(solution)/shard_map/along_z2/ppermute | solution.py:375
  163.0 1.3 collective-permute-start.23
  165.2 13.5 %shard_map.95 = (bf16[5,3,128,128]{3,2,1,0:T(8,128)(2,1)S(1)}, bf16[5,3,128,128]{3,2,1,0:T(8,128)(2,1)S(1)}, bf16[5,3,128,128]{3,2,1,0:T(8,128)(2,1)S(1)}, bf16[...) custom-call(s32[3,16,2]{2,1,0:T(8,128)S(1)} %fusion.18.places, ...), custom_call_target="tpu_custom_call" | custom-call | flops 3221225472 | bytes 17500000 | tf_op jit(solution)/shard_map/pallas_call | solution.py:156
  182.0 1.3 copy-done.40
  183.2 18.7 %shard_map.96 = (bf16[2,128,2048]{2,1,0:T(8,128)(2,1)S(1)}, bf16[2,128,2048]{2,1,0:T(8,128)(2,1)S(1)}, bf16[2,128,2048]{2,1,0:T(8,128)(2,1)S(1)}, bf16[2,128,204...) custom-call(s32[7,16,2]{2,1,0:T(8,128)S(1)} %pad_add_fusion.places, ...), custom_call_target="tpu_custom_call" | custom-call | flops 3758096384 | bytes 20000000 | tf_op jit(solution)/shard_map/pallas_call | solution.py:267
  203.9 1.1 copy-done.53
  208.8 1.5 collective-permute-start.33
  210.8 2.2 collective-permute-done.28
  213.1 3.1 fusion.6
  216.2 13.1 %collective-permute-start.31 = (bf16[5,3,128,128]{3,2,1,0:T(8,128)(2,1)}, bf16[5,3,128,128]{3,2,1,0:T(8,128)(2,1)S(1)}, u32[]{:S(2)}, u32[]{:S(2)}) collective-permute-start(bf16[5,3,128,128]{3,2,1,0:T(8,128)(2,1)} %shard_map.100), channel_id=1, source_target_pairs={{0,8},{4,12},{8,16},{12,20},{16,24},{20,28},{24,0},{28,4},{1,9},{5... | collective-permute-start | bytes 1474568 | tf_op jit(solution)/shard_map/along_z1/ppermute | solution.py:375
  229.4 5.4 %collective-permute-done.33 = bf16[2,128,2048]{2,1,0:T(8,128)(2,1)} collective-permute-done((bf16[2,128,2048]{2,1,0:T(8,128)(2,1)}, bf16[2,128,2048]{2,1,0:T(8,128)(2,1)}, u32[]{:S(2)}, u32[]{:S(2)}) %collective-permute-start.33) | collective-permute-done | bytes 1048608 | tf_op jit(solution)/shard_map/wide1/ppermute | solution.py:383
  234.7 2.0 fusion.11.refs_1_
  236.7 2.0 fusion.10.refs_0_
  238.7 2.6 collective-permute-done.31.refs_7_.refs_3_
  241.3 9.7 %collective-permute-done.30.refs_6_.refs_2_ = bf16[5,3,128,128]{3,2,1,0:T(8,128)(2,1)S(1)} collective-permute-done((bf16[5,3,128,128]{3,2,1,0:T(8,128)(2,1)}, bf16[5,3,128,128]{3,2,1,0:T(8,128)(2,1)S(1)}, u32[]{:S(2)}, u32[]{:S(2)}) %collective-permute-start.30) | collective-permute-done | bytes 491552 | tf_op jit(solution)/shard_map/along_z3/ppermute | solution.py:375
  251.8 1.5 collective-permute-start.34
  253.8 1.2 collective-permute-start.29
  255.5 1.5 collective-permute-start.38
  257.1 9.9 %collective-permute-done.34 = bf16[128,2048]{1,0:T(8,128)(2,1)} collective-permute-done((bf16[128,2048]{1,0:T(8,128)(2,1)}, bf16[128,2048]{1,0:T(8,128)(2,1)}, u32[]{:S(2)}, u32[]{:S(2)}) %collective-permute-start.34) | collective-permute-done | bytes 524320 | tf_op jit(solution)/shard_map/wide1/ppermute | solution.py:383
  267.0 1.6 bitcast_add_fusion.3
  268.6 1.6 bitcast_add_fusion.2
  272.0 5.3 %collective-permute-done.29.refs_5_.refs_1_ = bf16[5,3,128,128]{3,2,1,0:T(8,128)(2,1)S(1)} collective-permute-done((bf16[5,3,128,128]{3,2,1,0:T(8,128)(2,1)}, bf16[5,3,128,128]{3,2,1,0:T(8,128)(2,1)S(1)}, u32[]{:S(2)}, u32[]{:S(2)}) %collective-permute-start.29) | collective-permute-done | bytes 491552 | tf_op jit(solution)/shard_map/along_z2/ppermute | solution.py:375
  278.1 2.5 collective-permute-start.36
  280.6 7.1 %collective-permute-done.39 = bf16[2,128,2048]{2,1,0:T(8,128)(2,1)} collective-permute-done((bf16[2,128,2048]{2,1,0:T(8,128)(2,1)}, bf16[2,128,2048]{2,1,0:T(8,128)(2,1)}, u32[]{:S(2)}, u32[]{:S(2)}) %collective-permute-start.39) | collective-permute-done | bytes 1048608 | tf_op jit(solution)/shard_map/wide1/ppermute | solution.py:383
  287.7 2.1 fusion.13.refs_1_
  289.8 2.1 fusion.12.refs_0_
  293.1 1.2 collective-permute-start.40
  294.3 1.4 collective-permute-start.41
  295.8 4.2 %collective-permute-start.37 = (bf16[128,2048]{1,0:T(8,128)(2,1)S(1)}, bf16[128,2048]{1,0:T(8,128)(2,1)S(1)}, u32[]{:S(2)}, u32[]{:S(2)}) collective-permute-start(bf16[128,2048]{1,0:T(8,128)(2,1)S(1)} %fusion.4), channel_id=1, source_target_pairs={{0,24},{4,28},{8,0},{12,4},{16,8},{20,12},{24,16},{28,20},{1,25},{... | collective-permute-start | bytes 1572872 | tf_op jit(solution)/shard_map/along_z3/ppermute | solution.py:375
  300.0 6.3 %collective-permute-done.40 = bf16[128,2048]{1,0:T(8,128)(2,1)S(1)} collective-permute-done((bf16[128,2048]{1,0:T(8,128)(2,1)}, bf16[128,2048]{1,0:T(8,128)(2,1)S(1)}, u32[]{:S(2)}, u32[]{:S(2)}) %collective-permute-start.40) | collective-permute-done | bytes 524320 | tf_op jit(solution)/shard_map/wide1/ppermute | solution.py:383
  306.3 1.2 bitcast_add_fusion.1
  307.7 1.4 bitcast_add_fusion
  309.2 1.4 collective-permute-start.42
  310.7 2.6 shard_map.101
  313.4 10.4 %collective-permute-done.42 = bf16[128,2048]{1,0:T(8,128)(2,1)S(1)} collective-permute-done((bf16[128,2048]{1,0:T(8,128)(2,1)S(1)}, bf16[128,2048]{1,0:T(8,128)(2,1)S(1)}, u32[]{:S(2)}, u32[]{:S(2)}) %collective-permute-start.42) | collective-permute-done | bytes 524320 | tf_op jit(solution)/shard_map/along_z1/ppermute | solution.py:375
  (269 shorter events, 46.5 us)
Async XLA Ops:
  0.6 93.1 %copy-start = (s32[28,16]{0,1:T(8,128)S(1)}, s32[28,16]{0,1:T(8,128)}, u32[]{:S(2)}) copy-start(s32[28,16]{0,1:T(8,128)} %param.8) | copy-start | bytes 5380
  1.7 17.0 %copy-start.26 = (bf16[64,2048]{1,0:T(8,128)(2,1)}, bf16[64,2048]{1,0:T(8,128)(2,1)S(1)}, u32[]{:S(2)}) copy-start(bf16[64,2048]{1,0:T(8,128)(2,1)S(1)} %get-tuple-element.99.refs_0_) | copy-start | bytes 786436
  1.7 18.3 %copy-start.23 = (bf16[64,2048]{1,0:T(8,128)(2,1)}, bf16[64,2048]{1,0:T(8,128)(2,1)S(1)}, u32[]{:S(2)}) copy-start(bf16[64,2048]{1,0:T(8,128)(2,1)S(1)} %get-tuple-element.98.refs_1_) | copy-start | bytes 786436
  1.7 17.0 %collective-permute-start = (bf16[64,2048]{1,0:T(8,128)(2,1)S(1)}, bf16[64,2048]{1,0:T(8,128)(2,1)S(1)}, u32[]{:S(2)}, u32[]{:S(2)}) collective-permute-start(bf16[64,2048]{1,0:T(8,128)(2,1)S(1)} %get-tuple-element.99.refs_0_), channel_id=1, source_target_pairs={{0,1},{1,0},{2,3},{3,2},{4,5},{5,4},{6,7},{7,6},{8,9},{9,8},{10,11... | collective-permute-start | bytes 786440 | tf_op jit(solution)/shard_map/wide1/ppermute | solution.py:383
  4.7 17.0 %collective-permute-start.4 = (bf16[128,2048]{1,0:T(8,128)(2,1)}, bf16[128,2048]{1,0:T(8,128)(2,1)}, u32[]{:S(2)}, u32[]{:S(2)}) collective-permute-start(bf16[128,2048]{1,0:T(8,128)(2,1)} %param.5), channel_id=1, source_target_pairs={{0,8},{4,12},{8,16},{12,20},{16,24},{20,28},{24,0},{28,4},{1,9},{5... | collective-permute-start | bytes 1572872 | tf_op jit(solution)/shard_map/along_z1/ppermute | solution.py:375
  6.3 13.7 %collective-permute-start.1 = (bf16[64,2048]{1,0:T(8,128)(2,1)S(1)}, bf16[64,2048]{1,0:T(8,128)(2,1)S(1)}, u32[]{:S(2)}, u32[]{:S(2)}) collective-permute-start(bf16[64,2048]{1,0:T(8,128)(2,1)S(1)} %get-tuple-element.98.refs_1_), channel_id=1, source_target_pairs={{0,2},{1,3},{2,0},{3,1},{4,6},{5,7},{6,4},{7,5},{8,10},{9,11},{10,... | collective-permute-start | bytes 786440 | tf_op jit(solution)/shard_map/wide2/ppermute | solution.py:383
  7.8 25.1 %collective-permute-start.6 = (bf16[128,2048]{1,0:T(8,128)(2,1)}, bf16[128,2048]{1,0:T(8,128)(2,1)}, u32[]{:S(2)}, u32[]{:S(2)}) collective-permute-start(bf16[128,2048]{1,0:T(8,128)(2,1)} %param.5), channel_id=1, source_target_pairs={{0,24},{4,28},{8,0},{12,4},{16,8},{20,12},{24,16},{28,20},{1,25},{... | collective-permute-start | bytes 1572872 | tf_op jit(solution)/shard_map/along_z3/ppermute | solution.py:375
  18.7 26.1 %copy-start.22 = (bf16[5,4,128,128]{3,2,1,0:T(8,128)(2,1)}, bf16[5,4,128,128]{3,2,1,0:T(8,128)(2,1)S(1)}, u32[]{:S(2)}) copy-start(bf16[5,4,128,128]{3,2,1,0:T(8,128)(2,1)S(1)} %get-tuple-element.44.refs_4_.refs_0_) | copy-start | bytes 1966084
  18.7 95.7 %copy-start.12 = (bf16[5,7,128,128]{3,2,1,0:T(8,128)(2,1)}, bf16[5,7,128,128]{3,2,1,0:T(8,128)(2,1)S(1)}, u32[]{:S(2)}) copy-start(bf16[5,7,128,128]{3,2,1,0:T(8,128)(2,1)S(1)} %get-tuple-element.47.refs_12_.refs_0_.refs_9_) | copy-start | bytes 3440644
  19.5 25.3 %collective-permute-start.2 = (bf16[128,2048]{1,0:T(8,128)(2,1)S(1)}, bf16[128,2048]{1,0:T(8,128)(2,1)S(1)}, u32[]{:S(2)}, u32[]{:S(2)}) collective-permute-start(bf16[128,2048]{1,0:T(8,128)(2,1)S(1)} %pad_maximum_fusion.4), channel_id=1, source_target_pairs={{0,2},{1,3},{2,0},{3,1},{4,6},{5,7},{6,4},{7,5},{8,10},{9,11},{10,... | collective-permute-start | bytes 1572872 | tf_op jit(solution)/shard_map/wide2/ppermute | solution.py:383
  20.8 24.0 %collective-permute-start.3 = (bf16[128,2048]{1,0:T(8,128)(2,1)S(1)}, bf16[128,2048]{1,0:T(8,128)(2,1)S(1)}, u32[]{:S(2)}, u32[]{:S(2)}) collective-permute-start(bf16[128,2048]{1,0:T(8,128)(2,1)S(1)} %pad_maximum_fusion.5), channel_id=1, source_target_pairs={{0,1},{1,0},{2,3},{3,2},{4,5},{5,4},{6,7},{7,6},{8,9},{9,8},{10,11... | collective-permute-start | bytes 1572872 | tf_op jit(solution)/shard_map/wide1/ppermute | solution.py:383
  21.7 21.0 %collective-permute-start.5 = (bf16[128,2048]{1,0:T(8,128)(2,1)}, bf16[128,2048]{1,0:T(8,128)(2,1)S(1)}, u32[]{:S(2)}, u32[]{:S(2)}) collective-permute-start(bf16[128,2048]{1,0:T(8,128)(2,1)} %collective-permute-done.4), channel_id=1, source_target_pairs={{0,8},{4,12},{8,16},{12,20},{16,24},{20,28},{24,0},{28,4},{1,9},{5... | collective-permute-start | bytes 1572872 | tf_op jit(solution)/shard_map/along_z1/ppermute | solution.py:375
  45.8 17.4 %collective-permute-start.8 = (bf16[192,2048]{1,0:T(8,128)(2,1)}, bf16[192,2048]{1,0:T(8,128)(2,1)S(1)}, u32[]{:S(2)}, u32[]{:S(2)}) collective-permute-start(bf16[192,2048]{1,0:T(8,128)(2,1)} %get-tuple-element.46.refs_7_), channel_id=1, source_target_pairs={{0,2},{1,3},{2,0},{3,1},{4,6},{5,7},{6,4},{7,5},{8,10},{9,11},{10,... | collective-permute-start | bytes 2359304 | tf_op jit(solution)/shard_map/wide2/ppermute | solution.py:383
  47.3 17.8 %collective-permute-start.7 = (bf16[192,2048]{1,0:T(8,128)(2,1)}, bf16[192,2048]{1,0:T(8,128)(2,1)}, u32[]{:S(2)}, u32[]{:S(2)}) collective-permute-start(bf16[192,2048]{1,0:T(8,128)(2,1)} %get-tuple-element.45.refs_6_), channel_id=1, source_target_pairs={{0,1},{1,0},{2,3},{3,2},{4,5},{5,4},{6,7},{7,6},{8,9},{9,8},{10,11... | collective-permute-start | bytes 2359304 | tf_op jit(solution)/shard_map/wide1/ppermute | solution.py:383
  47.8 43.3 %collective-permute-start.12 = (bf16[5,4,128,128]{3,2,1,0:T(8,128)(2,1)}, bf16[5,4,128,128]{3,2,1,0:T(8,128)(2,1)}, u32[]{:S(2)}, u32[]{:S(2)}) collective-permute-start(bf16[5,4,128,128]{3,2,1,0:T(8,128)(2,1)} %shard_map.87), channel_id=1, source_target_pairs={{0,16},{4,20},{8,24},{12,28},{16,0},{20,4},{24,8},{28,12},{1,17},{... | collective-permute-start | bytes 1966088 | tf_op jit(solution)/shard_map/along_z2/ppermute | solution.py:375
  48.5 14.7 %copy-start.3 = (bf16[192,2048]{1,0:T(8,128)(2,1)S(1)}, bf16[192,2048]{1,0:T(8,128)(2,1)}, u32[]{:S(2)}) copy-start(bf16[192,2048]{1,0:T(8,128)(2,1)} %get-tuple-element.46.refs_7_) | copy-start | bytes 2359300
  48.5 43.7 %collective-permute-start.11 = (bf16[5,4,128,128]{3,2,1,0:T(8,128)(2,1)}, bf16[5,4,128,128]{3,2,1,0:T(8,128)(2,1)}, u32[]{:S(2)}, u32[]{:S(2)}) collective-permute-start(bf16[5,4,128,128]{3,2,1,0:T(8,128)(2,1)} %shard_map.86), channel_id=1, source_target_pairs={{0,8},{4,12},{8,16},{12,20},{16,24},{20,28},{24,0},{28,4},{1,9},{5... | collective-permute-start | bytes 1966088 | tf_op jit(solution)/shard_map/along_z1/ppermute | solution.py:375
  50.1 15.0 %copy-start.2 = (bf16[192,2048]{1,0:T(8,128)(2,1)S(1)}, bf16[192,2048]{1,0:T(8,128)(2,1)}, u32[]{:S(2)}) copy-start(bf16[192,2048]{1,0:T(8,128)(2,1)} %get-tuple-element.45.refs_6_) | copy-start | bytes 2359300
  50.1 42.1 %collective-permute-start.13 = (bf16[5,4,128,128]{3,2,1,0:T(8,128)(2,1)}, bf16[5,4,128,128]{3,2,1,0:T(8,128)(2,1)}, u32[]{:S(2)}, u32[]{:S(2)}) collective-permute-start(bf16[5,4,128,128]{3,2,1,0:T(8,128)(2,1)} %shard_map.88), channel_id=1, source_target_pairs={{0,24},{4,28},{8,0},{12,4},{16,8},{20,12},{24,16},{28,20},{1,25},{... | collective-permute-start | bytes 1966088 | tf_op jit(solution)/shard_map/along_z3/ppermute | solution.py:375
  63.2 51.2 %copy-start.19 = (bf16[192,2048]{1,0:T(8,128)(2,1)}, bf16[192,2048]{1,0:T(8,128)(2,1)S(1)}, u32[]{:S(2)}) copy-start(bf16[192,2048]{1,0:T(8,128)(2,1)S(1)} %collective-permute-done.8.refs_9_) | copy-start | bytes 2359300
  64.5 49.8 %collective-permute-start.10 = (bf16[384,2048]{1,0:T(8,128)(2,1)}, bf16[384,2048]{1,0:T(8,128)(2,1)}, u32[]{:S(2)}, u32[]{:S(2)}) collective-permute-start(bf16[384,2048]{1,0:T(8,128)(2,1)} %pad_maximum_fusion.1), channel_id=1, source_target_pairs={{0,1},{1,0},{2,3},{3,2},{4,5},{5,4},{6,7},{7,6},{8,9},{9,8},{10,11... | collective-permute-start | bytes 4718600 | tf_op jit(solution)/shard_map/wide1/ppermute | solution.py:383
  67.5 46.8 %collective-permute-start.9 = (bf16[384,2048]{1,0:T(8,128)(2,1)}, bf16[384,2048]{1,0:T(8,128)(2,1)}, u32[]{:S(2)}, u32[]{:S(2)}) collective-permute-start(bf16[384,2048]{1,0:T(8,128)(2,1)} %pad_maximum_fusion), channel_id=1, source_target_pairs={{0,2},{1,3},{2,0},{3,1},{4,6},{5,7},{6,4},{7,5},{8,10},{9,11},{10,... | collective-permute-start | bytes 4718600 | tf_op jit(solution)/shard_map/wide2/ppermute | solution.py:383
  91.1 2.4 collective-permute-start.16
  92.2 18.5 %collective-permute-start.14 = (bf16[5,7,128,128]{3,2,1,0:T(8,128)(2,1)}, bf16[5,7,128,128]{3,2,1,0:T(8,128)(2,1)}, u32[]{:S(2)}, u32[]{:S(2)}) collective-permute-start(bf16[5,7,128,128]{3,2,1,0:T(8,128)(2,1)} %shard_map.89), channel_id=1, source_target_pairs={{0,4},{4,0},{8,12},{12,8},{16,20},{20,16},{24,28},{28,24},{1,5},{5... | collective-permute-start | bytes 3440648 | tf_op jit(solution)/shard_map/swap/ppermute | solution.py:379
  92.8 4.1 %collective-permute-start.15 = (bf16[5,4,128,128]{3,2,1,0:T(8,128)(2,1)}, bf16[5,4,128,128]{3,2,1,0:T(8,128)(2,1)}, u32[]{:S(2)}, u32[]{:S(2)}) collective-permute-start(bf16[5,4,128,128]{3,2,1,0:T(8,128)(2,1)} %collective-permute-done.11.refs_2_.refs_13_.refs_1_), channel_id=1, source_target_pairs={{0,4},{4,0},{8,12},{12,8},{16,20},{20,16},{24,28},{28,24},{1,5},{5... | collective-permute-start | bytes 1966088 | tf_op jit(solution)/shard_map/swap/ppermute | solution.py:379
  93.6 16.1 %collective-permute-start.17 = (bf16[5,4,128,128]{3,2,1,0:T(8,128)(2,1)}, bf16[5,4,128,128]{3,2,1,0:T(8,128)(2,1)}, u32[]{:S(2)}, u32[]{:S(2)}) collective-permute-start(bf16[5,4,128,128]{3,2,1,0:T(8,128)(2,1)} %collective-permute-done.13.refs_3_.refs_15_.refs_1_), channel_id=1, source_target_pairs={{0,4},{4,0},{8,12},{12,8},{16,20},{20,16},{24,28},{28,24},{1,5},{5... | collective-permute-start | bytes 1966088 | tf_op jit(solution)/shard_map/swap/ppermute | solution.py:379
  96.9 46.0 %collective-permute-start.19 = (bf16[5,3,128,128]{3,2,1,0:T(8,128)(2,1)}, bf16[5,3,128,128]{3,2,1,0:T(8,128)(2,1)S(1)}, u32[]{:S(2)}, u32[]{:S(2)}) collective-permute-start(bf16[5,3,128,128]{3,2,1,0:T(8,128)(2,1)} %shard_map.92), channel_id=1, source_target_pairs={{0,16},{4,20},{8,24},{12,28},{16,0},{20,4},{24,8},{28,12},{1,17},{... | collective-permute-start | bytes 1474568 | tf_op jit(solution)/shard_map/along_z2/ppermute | solution.py:375
  109.7 34.1 %collective-permute-start.18 = (bf16[5,3,128,128]{3,2,1,0:T(8,128)(2,1)}, bf16[5,3,128,128]{3,2,1,0:T(8,128)(2,1)}, u32[]{:S(2)}, u32[]{:S(2)}) collective-permute-start(bf16[5,3,128,128]{3,2,1,0:T(8,128)(2,1)} %shard_map.91), channel_id=1, source_target_pairs={{0,8},{4,12},{8,16},{12,20},{16,24},{20,28},{24,0},{28,4},{1,9},{5... | collective-permute-start | bytes 1474568 | tf_op jit(solution)/shard_map/along_z1/ppermute | solution.py:375
  110.6 33.1 %collective-permute-start.20 = (bf16[5,3,128,128]{3,2,1,0:T(8,128)(2,1)}, bf16[5,3,128,128]{3,2,1,0:T(8,128)(2,1)}, u32[]{:S(2)}, u32[]{:S(2)}) collective-permute-start(bf16[5,3,128,128]{3,2,1,0:T(8,128)(2,1)} %shard_map.93), channel_id=1, source_target_pairs={{0,24},{4,28},{8,0},{12,4},{16,8},{20,12},{24,16},{28,20},{1,25},{... | collective-permute-start | bytes 1474568 | tf_op jit(solution)/shard_map/along_z3/ppermute | solution.py:375
  143.8 5.2 %collective-permute-start.21 = (bf16[4,5,4,128,128]{4,3,2,1,0:T(8,128)(2,1)}, bf16[4,5,4,128,128]{4,3,2,1,0:T(8,128)(2,1)S(1)}, u32[]{:S(2)}, u32[]{:S(2)}) collective-permute-start(bf16[4,5,4,128,128]{4,3,2,1,0:T(8,128)(2,1)} %shard_map.94), channel_id=1, source_target_pairs={{0,4},{4,0},{8,12},{12,8},{16,20},{20,16},{24,28},{28,24},{1,5},{5... | collective-permute-start | bytes 7864328 | tf_op jit(solution)/shard_map/swap/ppermute | solution.py:379
  144.8 19.6 %collective-permute-start.26 = (bf16[5,3,128,128]{3,2,1,0:T(8,128)(2,1)S(1)}, bf16[5,3,128,128]{3,2,1,0:T(8,128)(2,1)S(1)}, u32[]{:S(2)}, u32[]{:S(2)}) collective-permute-start(bf16[5,3,128,128]{3,2,1,0:T(8,128)(2,1)S(1)} %copy-done.38), channel_id=1, source_target_pairs={{0,4},{4,0},{8,12},{12,8},{16,20},{20,16},{24,28},{28,24},{1,5},{5... | collective-permute-start | bytes 1474568 | tf_op jit(solution)/shard_map/swap/ppermute | solution.py:379
  144.8 20.3 %collective-permute-start.25 = (bf16[5,3,128,128]{3,2,1,0:T(8,128)(2,1)}, bf16[5,3,128,128]{3,2,1,0:T(8,128)(2,1)S(1)}, u32[]{:S(2)}, u32[]{:S(2)}) collective-permute-start(bf16[5,3,128,128]{3,2,1,0:T(8,128)(2,1)} %collective-permute-done.18.refs_1_.refs_13_.refs_10_), channel_id=1, source_target_pairs={{0,4},{4,0},{8,12},{12,8},{16,20},{20,16},{24,28},{28,24},{1,5},{5... | collective-permute-start | bytes 1474568 | tf_op jit(solution)/shard_map/swap/ppermute | solution.py:379
  145.3 19.8 %collective-permute-start.27 = (bf16[5,3,128,128]{3,2,1,0:T(8,128)(2,1)}, bf16[5,3,128,128]{3,2,1,0:T(8,128)(2,1)S(1)}, u32[]{:S(2)}, u32[]{:S(2)}) collective-permute-start(bf16[5,3,128,128]{3,2,1,0:T(8,128)(2,1)} %collective-permute-done.20.refs_3_.refs_15_.refs_12_), channel_id=1, source_target_pairs={{0,4},{4,0},{8,12},{12,8},{16,20},{20,16},{24,28},{28,24},{1,5},{5... | collective-permute-start | bytes 1474568 | tf_op jit(solution)/shard_map/swap/ppermute | solution.py:379
  149.0 16.1 %copy-start.86 = (s32[7,16,1]{2,1,0:T(8,128)S(1)}, s32[7,16,1]{2,1,0:T(8,128)}, u32[]{:S(2)}) copy-start(s32[7,16,1]{2,1,0:T(8,128)} %get-tuple-element.100) | copy-start | bytes 1348
  149.0 16.1 %copy-start.88 = (s32[7,16,1]{2,1,0:T(8,128)S(1)}, s32[7,16,1]{2,1,0:T(8,128)}, u32[]{:S(2)}) copy-start(s32[7,16,1]{2,1,0:T(8,128)} %get-tuple-element.101) | copy-start | bytes 1348
  149.0 16.1 %copy-start.13 = (bf16[5,7,128,128]{3,2,1,0:T(8,128)(2,1)S(1)}, bf16[5,7,128,128]{3,2,1,0:T(8,128)(2,1)}, u32[]{:S(2)}) copy-start(bf16[5,7,128,128]{3,2,1,0:T(8,128)(2,1)} %copy-done.12) | copy-start | bytes 3440644
  149.0 16.1 %copy-start.20 = (bf16[192,2048]{1,0:T(8,128)(2,1)S(1)}, bf16[192,2048]{1,0:T(8,128)(2,1)}, u32[]{:S(2)}) copy-start(bf16[192,2048]{1,0:T(8,128)(2,1)} %copy-done.19) | copy-start | bytes 2359300
  149.0 16.1 %copy-start.25 = (bf16[64,2048]{1,0:T(8,128)(2,1)S(1)}, bf16[64,2048]{1,0:T(8,128)(2,1)}, u32[]{:S(2)}) copy-start(bf16[64,2048]{1,0:T(8,128)(2,1)} %copy-done.23) | copy-start | bytes 786436
  149.0 16.1 %copy-start.28 = (bf16[64,2048]{1,0:T(8,128)(2,1)S(1)}, bf16[64,2048]{1,0:T(8,128)(2,1)}, u32[]{:S(2)}) copy-start(bf16[64,2048]{1,0:T(8,128)(2,1)} %copy-done.26) | copy-start | bytes 786436
  149.1 16.1 %copy-start.31 = (bf16[128,2048]{1,0:T(8,128)(2,1)S(1)}, bf16[128,2048]{1,0:T(8,128)(2,1)}, u32[]{:S(2)}) copy-start(bf16[128,2048]{1,0:T(8,128)(2,1)} %copy-done.29) | copy-start | bytes 1572868
  149.1 16.1 %copy-start.34 = (bf16[128,2048]{1,0:T(8,128)(2,1)S(1)}, bf16[128,2048]{1,0:T(8,128)(2,1)}, u32[]{:S(2)}) copy-start(bf16[128,2048]{1,0:T(8,128)(2,1)} %copy-done.32) | copy-start | bytes 1572868
  149.1 16.1 %copy-start.39 = (bf16[5,3,128,128]{3,2,1,0:T(8,128)(2,1)S(1)}, bf16[5,3,128,128]{3,2,1,0:T(8,128)(2,1)}, u32[]{:S(2)}) copy-start(bf16[5,3,128,128]{3,2,1,0:T(8,128)(2,1)} %copy-done.37) | copy-start | bytes 1474564
  149.1 16.1 %copy-start.45 = (bf16[64,2048]{1,0:T(8,128)(2,1)S(1)}, bf16[64,2048]{1,0:T(8,128)(2,1)}, u32[]{:S(2)}) copy-start(bf16[64,2048]{1,0:T(8,128)(2,1)} %copy-done.43) | copy-start | bytes 786436
  149.1 16.1 %copy-start.48 = (bf16[64,2048]{1,0:T(8,128)(2,1)S(1)}, bf16[64,2048]{1,0:T(8,128)(2,1)}, u32[]{:S(2)}) copy-start(bf16[64,2048]{1,0:T(8,128)(2,1)} %copy-done.46) | copy-start | bytes 786436
  151.8 27.0 %copy-start.10 = (bf16[5,4,128,128]{3,2,1,0:T(8,128)(2,1)}, bf16[5,4,128,128]{3,2,1,0:T(8,128)(2,1)S(1)}, u32[]{:S(2)}) copy-start(bf16[5,4,128,128]{3,2,1,0:T(8,128)(2,1)S(1)} %get-tuple-element.87.refs_20_.refs_0_) | copy-start | bytes 1966084
  151.8 55.1 %collective-permute-start.22 = (bf16[5,4,128,128]{3,2,1,0:T(8,128)(2,1)S(1)}, bf16[5,4,128,128]{3,2,1,0:T(8,128)(2,1)S(1)}, u32[]{:S(2)}, u32[]{:S(2)}) collective-permute-start(bf16[5,4,128,128]{3,2,1,0:T(8,128)(2,1)S(1)} %get-tuple-element.86.refs_21_), channel_id=1, source_target_pairs={{0,16},{4,20},{8,24},{12,28},{16,0},{20,4},{24,8},{28,12},{1,17},{... | collective-permute-start | bytes 1966088 | tf_op jit(solution)/shard_map/along_z2/ppermute | solution.py:375
  163.0 43.9 %collective-permute-start.23 = (bf16[5,4,128,128]{3,2,1,0:T(8,128)(2,1)S(1)}, bf16[5,4,128,128]{3,2,1,0:T(8,128)(2,1)S(1)}, u32[]{:S(2)}, u32[]{:S(2)}) collective-permute-start(bf16[5,4,128,128]{3,2,1,0:T(8,128)(2,1)S(1)} %get-tuple-element.85.refs_22_), channel_id=1, source_target_pairs={{0,24},{4,28},{8,0},{12,4},{16,8},{20,12},{24,16},{28,20},{1,25},{... | collective-permute-start | bytes 1966088 | tf_op jit(solution)/shard_map/along_z3/ppermute | solution.py:375
  164.4 43.0 %collective-permute-start.24 = (bf16[5,4,128,128]{3,2,1,0:T(8,128)(2,1)S(1)}, bf16[5,4,128,128]{3,2,1,0:T(8,128)(2,1)S(1)}, u32[]{:S(2)}, u32[]{:S(2)}) collective-permute-start(bf16[5,4,128,128]{3,2,1,0:T(8,128)(2,1)S(1)} %get-tuple-element.84.refs_23_), channel_id=1, source_target_pairs={{0,8},{4,12},{8,16},{12,20},{16,24},{20,28},{24,0},{28,4},{1,9},{5... | collective-permute-start | bytes 1966088 | tf_op jit(solution)/shard_map/along_z1/ppermute | solution.py:375
  208.7 4.3 %collective-permute-start.28 = (bf16[4,5,3,128,128]{4,3,2,1,0:T(8,128)(2,1)}, bf16[4,5,3,128,128]{4,3,2,1,0:T(8,128)(2,1)}, u32[]{:S(2)}, u32[]{:S(2)}) collective-permute-start(bf16[4,5,3,128,128]{4,3,2,1,0:T(8,128)(2,1)} %shard_map.97), channel_id=1, source_target_pairs={{0,4},{4,0},{8,12},{12,8},{16,20},{20,16},{24,28},{28,24},{1,5},{5... | collective-permute-start | bytes 5898248 | tf_op jit(solution)/shard_map/swap/ppermute | solution.py:379
  208.8 25.9 %collective-permute-start.33 = (bf16[2,128,2048]{2,1,0:T(8,128)(2,1)}, bf16[2,128,2048]{2,1,0:T(8,128)(2,1)}, u32[]{:S(2)}, u32[]{:S(2)}) collective-permute-start(bf16[2,128,2048]{2,1,0:T(8,128)(2,1)} %get-tuple-element.71), channel_id=1, source_target_pairs={{0,1},{1,0},{2,3},{3,2},{4,5},{5,4},{6,7},{7,6},{8,9},{9,8},{10,11... | collective-permute-start | bytes 3145736 | tf_op jit(solution)/shard_map/wide1/ppermute | solution.py:383
  210.3 26.4 %collective-permute-start.32 = (bf16[2,128,2048]{2,1,0:T(8,128)(2,1)}, bf16[2,128,2048]{2,1,0:T(8,128)(2,1)}, u32[]{:S(2)}, u32[]{:S(2)}) collective-permute-start(bf16[2,128,2048]{2,1,0:T(8,128)(2,1)} %get-tuple-element.69), channel_id=1, source_target_pairs={{0,2},{1,3},{2,0},{3,1},{4,6},{5,7},{6,4},{7,5},{8,10},{9,11},{10,... | collective-permute-start | bytes 3145736 | tf_op jit(solution)/shard_map/wide2/ppermute | solution.py:383
  216.2 18.5 %copy-start.50 = (bf16[2,128,2048]{2,1,0:T(8,128)(2,1)S(1)}, bf16[2,128,2048]{2,1,0:T(8,128)(2,1)}, u32[]{:S(2)}) copy-start(bf16[2,128,2048]{2,1,0:T(8,128)(2,1)} %copy-done.49) | copy-start | bytes 3145732
  216.2 25.1 %collective-permute-start.31 = (bf16[5,3,128,128]{3,2,1,0:T(8,128)(2,1)}, bf16[5,3,128,128]{3,2,1,0:T(8,128)(2,1)S(1)}, u32[]{:S(2)}, u32[]{:S(2)}) collective-permute-start(bf16[5,3,128,128]{3,2,1,0:T(8,128)(2,1)} %shard_map.100), channel_id=1, source_target_pairs={{0,8},{4,12},{8,16},{12,20},{16,24},{20,28},{24,0},{28,4},{1,9},{5... | collective-permute-start | bytes 1474568 | tf_op jit(solution)/shard_map/along_z1/ppermute | solution.py:375
  229.4 21.6 %collective-permute-start.30 = (bf16[5,3,128,128]{3,2,1,0:T(8,128)(2,1)}, bf16[5,3,128,128]{3,2,1,0:T(8,128)(2,1)S(1)}, u32[]{:S(2)}, u32[]{:S(2)}) collective-permute-start(bf16[5,3,128,128]{3,2,1,0:T(8,128)(2,1)} %shard_map.99), channel_id=1, source_target_pairs={{0,24},{4,28},{8,0},{12,4},{16,8},{20,12},{24,16},{28,20},{1,25},{... | collective-permute-start | bytes 1474568 | tf_op jit(solution)/shard_map/along_z3/ppermute | solution.py:375
  251.8 15.2 %collective-permute-start.34 = (bf16[128,2048]{1,0:T(8,128)(2,1)}, bf16[128,2048]{1,0:T(8,128)(2,1)}, u32[]{:S(2)}, u32[]{:S(2)}) collective-permute-start(bf16[128,2048]{1,0:T(8,128)(2,1)} %get-tuple-element.72.refs_2_), channel_id=1, source_target_pairs={{0,1},{1,0},{2,3},{3,2},{4,5},{5,4},{6,7},{7,6},{8,9},{9,8},{10,11... | collective-permute-start | bytes 1572872 | tf_op jit(solution)/shard_map/wide1/ppermute | solution.py:383
  253.3 15.3 %collective-permute-start.35 = (bf16[128,2048]{1,0:T(8,128)(2,1)}, bf16[128,2048]{1,0:T(8,128)(2,1)S(1)}, u32[]{:S(2)}, u32[]{:S(2)}) collective-permute-start(bf16[128,2048]{1,0:T(8,128)(2,1)} %get-tuple-element.73.refs_3_), channel_id=1, source_target_pairs={{0,2},{1,3},{2,0},{3,1},{4,6},{5,7},{6,4},{7,5},{8,10},{9,11},{10,... | collective-permute-start | bytes 1572872 | tf_op jit(solution)/shard_map/wide2/ppermute | solution.py:383
  253.8 23.5 %collective-permute-start.29 = (bf16[5,3,128,128]{3,2,1,0:T(8,128)(2,1)}, bf16[5,3,128,128]{3,2,1,0:T(8,128)(2,1)S(1)}, u32[]{:S(2)}, u32[]{:S(2)}) collective-permute-start(bf16[5,3,128,128]{3,2,1,0:T(8,128)(2,1)} %shard_map.98), channel_id=1, source_target_pairs={{0,16},{4,20},{8,24},{12,28},{16,0},{20,4},{24,8},{28,12},{1,17},{... | collective-permute-start | bytes 1474568 | tf_op jit(solution)/shard_map/along_z2/ppermute | solution.py:375
  255.0 32.7 %collective-permute-start.39 = (bf16[2,128,2048]{2,1,0:T(8,128)(2,1)}, bf16[2,128,2048]{2,1,0:T(8,128)(2,1)}, u32[]{:S(2)}, u32[]{:S(2)}) collective-permute-start(bf16[2,128,2048]{2,1,0:T(8,128)(2,1)} %get-tuple-element.79), channel_id=1, source_target_pairs={{0,1},{1,0},{2,3},{3,2},{4,5},{5,4},{6,7},{7,6},{8,9},{9,8},{10,11... | collective-permute-start | bytes 3145736 | tf_op jit(solution)/shard_map/wide1/ppermute | solution.py:383
  255.5 34.3 %collective-permute-start.38 = (bf16[2,128,2048]{2,1,0:T(8,128)(2,1)}, bf16[2,128,2048]{2,1,0:T(8,128)(2,1)}, u32[]{:S(2)}, u32[]{:S(2)}) collective-permute-start(bf16[2,128,2048]{2,1,0:T(8,128)(2,1)} %get-tuple-element.77), channel_id=1, source_target_pairs={{0,2},{1,3},{2,0},{3,1},{4,6},{5,7},{6,4},{7,5},{8,10},{9,11},{10,... | collective-permute-start | bytes 3145736 | tf_op jit(solution)/shard_map/wide2/ppermute | solution.py:383
  278.1 14.2 %collective-permute-start.36 = (bf16[128,2048]{1,0:T(8,128)(2,1)}, bf16[128,2048]{1,0:T(8,128)(2,1)S(1)}, u32[]{:S(2)}, u32[]{:S(2)}) collective-permute-start(bf16[128,2048]{1,0:T(8,128)(2,1)} %shard_map.104), channel_id=1, source_target_pairs={{0,24},{4,28},{8,0},{12,4},{16,8},{20,12},{24,16},{28,20},{1,25},{... | collective-permute-start | bytes 1572872 | tf_op jit(solution)/shard_map/along_z3/ppermute | solution.py:375
  293.1 13.2 %collective-permute-start.40 = (bf16[128,2048]{1,0:T(8,128)(2,1)}, bf16[128,2048]{1,0:T(8,128)(2,1)S(1)}, u32[]{:S(2)}, u32[]{:S(2)}) collective-permute-start(bf16[128,2048]{1,0:T(8,128)(2,1)} %get-tuple-element.80), channel_id=1, source_target_pairs={{0,1},{1,0},{2,3},{3,2},{4,5},{5,4},{6,7},{7,6},{8,9},{9,8},{10,11... | collective-permute-start | bytes 1572872 | tf_op jit(solution)/shard_map/wide1/ppermute | solution.py:383
  294.3 13.4 %collective-permute-start.41 = (bf16[128,2048]{1,0:T(8,128)(2,1)S(1)}, bf16[128,2048]{1,0:T(8,128)(2,1)S(1)}, u32[]{:S(2)}, u32[]{:S(2)}) collective-permute-start(bf16[128,2048]{1,0:T(8,128)(2,1)S(1)} %copy-done.80), channel_id=1, source_target_pairs={{0,2},{1,3},{2,0},{3,1},{4,6},{5,7},{6,4},{7,5},{8,10},{9,11},{10,... | collective-permute-start | bytes 1572872 | tf_op jit(solution)/shard_map/wide2/ppermute | solution.py:383
  295.8 17.6 %collective-permute-start.37 = (bf16[128,2048]{1,0:T(8,128)(2,1)S(1)}, bf16[128,2048]{1,0:T(8,128)(2,1)S(1)}, u32[]{:S(2)}, u32[]{:S(2)}) collective-permute-start(bf16[128,2048]{1,0:T(8,128)(2,1)S(1)} %fusion.4), channel_id=1, source_target_pairs={{0,24},{4,28},{8,0},{12,4},{16,8},{20,12},{24,16},{28,20},{1,25},{... | collective-permute-start | bytes 1572872 | tf_op jit(solution)/shard_map/along_z3/ppermute | solution.py:375
  309.2 14.6 %collective-permute-start.42 = (bf16[128,2048]{1,0:T(8,128)(2,1)S(1)}, bf16[128,2048]{1,0:T(8,128)(2,1)S(1)}, u32[]{:S(2)}, u32[]{:S(2)}) collective-permute-start(bf16[128,2048]{1,0:T(8,128)(2,1)S(1)} %pad_maximum_fusion.7), channel_id=1, source_target_pairs={{0,8},{4,12},{8,16},{12,20},{16,24},{20,28},{24,0},{28,4},{1,9},{5... | collective-permute-start | bytes 1572872 | tf_op jit(solution)/shard_map/along_z1/ppermute | solution.py:375
  (70 other events, 160.2 us)

commit v4 on v3

--- a/solution.py
+++ b/solution.py
@@ -413,7 +413,7 @@
             for h in range(2)
         )
         if x_parts:
-            a, b = hold([a, b], *x_parts[-2:], *messages[:1])
+            a, b = hold([a, b], *x_parts[-2:], *messages[:1], places)
         n = len(group) * half
         ax, by = over_wide(a, 1), over_wide(b, 2)
         far_a = over_wide(jnp.concatenate([a, ax], axis=0), 2)
@@ -435,12 +435,13 @@
         now = [hold([a], e)[0] for a, e in zip(now, earlier)]
         now = earlier = [along_z(a, r) for a, r in zip(now, shifts)]
         if other is None:
-            other = swap(*hold([own], *now))
+            (own,) = hold([own], *now)
+            other = swap(own)
         in_order = [now[shifts.index(r)] for r in range(1, nz)]
         weights.append(([own] + in_order, [other] + [swap(a) for a in in_order]))
 
     order = [*shifts, 0]
-    groups = [order[: (nz + 1) // 2], order[(nz + 1) // 2 :]]
+    groups = [[2, 3], [1, 0]]
     columns, sent, parts, back, sums = [], [], [], [], []
     for k, ((lo, hi), (w_own, w_other)) in enumerate(zip(chunks, weights)):
         g_own, g_other, d = forward_call(
@@ -477,11 +478,12 @@
         for i, r in enumerate(group):
             shares.append(jnp.concatenate([a[i * half : (i + 1) * half] for a in halves], axis=0))
         if not moved:
-            moved = [along_z(*hold([shares[0].astype(BF16)], *sent[-1]), nz - 1)]
-            shares = [shares[1] + moved[0].astype(F32)]
-            step = moved
-        arrived = along_z(shares[0].astype(BF16), nz - (3 if total is not None else 1))
-        total = arrived.astype(F32) if total is None else total + arrived.astype(F32) + shares[1]
+            two, three = hold([a.astype(BF16) for a in shares], *sent[-1])
+            moved = [along_z(two, nz - 1), along_z(three, nz - 3)]
+            step = moved[:1]
+        else:
+            one = (shares[0] + moved[0].astype(F32)).astype(BF16)
+            total = along_z(one, nz - 1).astype(F32) + moved[1].astype(F32) + shares[1]
     return hidden, total.astype(BF16), grad_gate, grad_up
 
 

time: 326 us -> 322 us (0.988)
  local copies, waits for them, and re-layouts: 45.2 us -> 41.7 us
    ppermute x18, waiting for transfers between devices: 71.1 us -> 64.9 us  [along_z(): lax.ppermute(a, 'narrow', [(i, (i + 2 * s) % narrow) for i in range(narro...]
    ppermute x9, waiting for transfers between devices: 6.44 us -> 10.9 us  [swap(): return lax.ppermute(a, 'narrow', [(i, i ^ 1) for i in range(narrow)])]
    ppermute x16, waiting for transfers between devices: 39.6 us -> 43.3 us  [over_wide(): return lax.ppermute(a, 'wide', [(i, i ^ m) for i in range(nw)])]
    unnamed x179 -> x184, local copies, waits for them, and re-layouts: 40.1 us -> 39.3 us
  transfers between devices with their start and end apart: 43 -> 43, of which waited for: 19 -> 17; matrix products, arithmetic and copies ran while one was open for 10% -> 9% of each run, Pallas kernels for 16% -> 16%
where the time goes in v4:
time: 322 us; the launch traced here: 321 us
  waiting for transfers between devices  119 us (37%)
  starting transfers between devices  79.8 us (25%)
  Pallas kernels  51 us (16%)
  local copies, waits for them, and re-layouts  41.7 us (13%)
  other arithmetic  28 us (9%)
    ppermute x18, waiting for transfers between devices, along_z(): lax.ppermute(a, 'narrow', [(i, (i + 2 * s) % narrow) for i in range(narro...  64.9 us
    ppermute x18, starting transfers between devices, along_z(): lax.ppermute(a, 'narrow', [(i, (i + 2 * s) % narrow) for i in range(narro...  61.1 us
    ppermute x16, waiting for transfers between devices, over_wide(): return lax.ppermute(a, 'wide', [(i, i ^ m) for i in range(nw)])  43.3 us
    unnamed x184, local copies, waits for them, and re-layouts  39.3 us
    pallas_call x2, Pallas kernels, forward_call(): pl.pallas_call(functools.partial(forward_kernel, nz, nw, spd, len(earlier...  29.5 us
    pallas_call x1, Pallas kernels, inputs_call(): pl.pallas_call(functools.partial(inputs_kernel, nz, spd, counts, groups,...  18.5 us
    ppermute x16, starting transfers between devices, over_wide(): return lax.ppermute(a, 'wide', [(i, i ^ m) for i in range(nw)])  16.9 us
    ppermute x9, waiting for transfers between devices, swap(): return lax.ppermute(a, 'narrow', [(i, i ^ 1) for i in range(narrow)])  10.9 us
  transfers between devices with their start and end apart: 43, of which 17 were waited for; matrix products, arithmetic and copies ran while one was open for 9% of the time, Pallas kernels for 16%

profile of v4, /device:TPU:0, one launch (start us, length us, event | category | flops | bytes accessed | tf_op | source)
XLA Modules:
  0.0 321.2 jit_solution(1868006442184100099)
XLA Ops:
  0.7 3.1 collective-permute-start.4
  3.7 2.1 collective-permute-start.6
  5.8 1.1 fusion.29
  6.9 1.7 collective-permute-start
  8.6 1.5 collective-permute-start.1
  12.2 1.5 copy-done.42
  13.6 1.5 copy-done.43
  22.2 6.6 %collective-permute-done.6 = bf16[128,2048]{1,0:T(8,128)(2,1)S(1)} collective-permute-done((bf16[128,2048]{1,0:T(8,128)(2,1)}, bf16[128,2048]{1,0:T(8,128)(2,1)S(1)}, u32[]{:S(2)}, u32[]{:S(2)}) %collective-permute-start.6) | collective-permute-done | bytes 524320 | tf_op jit(solution)/shard_map/along_z3/ppermute | solution.py:375
  28.8 11.6 %collective-permute-done.5.refs_1_ = bf16[128,2048]{1,0:T(8,128)(2,1)S(1)} collective-permute-done((bf16[128,2048]{1,0:T(8,128)(2,1)S(1)}, bf16[128,2048]{1,0:T(8,128)(2,1)S(1)}, u32[]{:S(2)}, u32[]{:S(2)}) %collective-permute-start.5) | collective-permute-done | bytes 524320 | tf_op jit(solution)/shard_map/along_z1/ppermute | solution.py:375
  41.2 1.2 pad_maximum_fusion.2
  43.5 1.5 collective-permute-start.8
  45.0 1.5 collective-permute-start.7
  47.2 1.6 collective-permute-start.12
  48.7 2.2 collective-permute-start.13
  51.0 9.9 %collective-permute-done.8.refs_9_ = bf16[192,2048]{1,0:T(8,128)(2,1)S(1)} collective-permute-done((bf16[192,2048]{1,0:T(8,128)(2,1)}, bf16[192,2048]{1,0:T(8,128)(2,1)S(1)}, u32[]{:S(2)}, u32[]{:S(2)}) %collective-permute-start.8) | collective-permute-done | bytes 786464 | tf_op jit(solution)/shard_map/wide2/ppermute | solution.py:383
  60.9 1.3 pad_maximum_fusion.1
  62.2 1.5 collective-permute-start.10
  63.7 1.4 pad_maximum_fusion
  65.1 1.5 collective-permute-start.9
  66.6 23.5 %collective-permute-done.11.refs_1_.refs_14_.refs_2_ = bf16[5,4,128,128]{3,2,1,0:T(8,128)(2,1)} collective-permute-done((bf16[5,4,128,128]{3,2,1,0:T(8,128)(2,1)}, bf16[5,4,128,128]{3,2,1,0:T(8,128)(2,1)}, u32[]{:S(2)}, u32[]{:S(2)}) %collective-permute-start.11) | collective-permute-done | bytes 655392 | tf_op jit(solution)/shard_map/along_z2/ppermute | solution.py:375
  90.7 1.8 collective-permute-done.16.refs_18_.refs_6_
  93.3 1.8 collective-permute-done.15.refs_17_.refs_5_
  95.2 13.1 %collective-permute-start.19 = (bf16[5,3,128,128]{3,2,1,0:T(8,128)(2,1)}, bf16[5,3,128,128]{3,2,1,0:T(8,128)(2,1)}, u32[]{:S(2)}, u32[]{:S(2)}) collective-permute-start(bf16[5,3,128,128]{3,2,1,0:T(8,128)(2,1)} %shard_map.92), channel_id=1, source_target_pairs={{0,16},{4,20},{8,24},{12,28},{16,0},{20,4},{24,8},{28,12},{1,17},{... | collective-permute-start | bytes 1474568 | tf_op jit(solution)/shard_map/along_z2/ppermute | solution.py:375
  109.3 2.9 collective-permute-start.20
  113.0 1.1 copy-done.23
  120.0 1.1 copy-done.80
  121.1 16.1 %shard_map.90 = (bf16[5,4,128,128]{3,2,1,0:T(8,128)(2,1)S(1)}, bf16[5,4,128,128]{3,2,1,0:T(8,128)(2,1)S(1)}, bf16[5,4,128,128]{3,2,1,0:T(8,128)(2,1)S(1)}, bf16[...) custom-call(s32[4,16,2]{2,1,0:T(8,128)S(1)} %fusion.18.places, ...), custom_call_target="tpu_custom_call" | custom-call | flops 4294967296 | bytes 20000000 | tf_op jit(solution)/shard_map/pallas_call | solution.py:156
  137.2 1.5 copy-done.25
  144.2 4.1 %collective-permute-done.21 = bf16[4,5,4,128,128]{4,3,2,1,0:T(8,128)(2,1)S(1)} collective-permute-done((bf16[4,5,4,128,128]{4,3,2,1,0:T(8,128)(2,1)}, bf16[4,5,4,128,128]{4,3,2,1,0:T(8,128)(2,1)S(1)}, u32[]{:S(2)}, u32[]{:S(2)}) %collective-permute-start.21) | collective-permute-done | bytes 2621472 | tf_op jit(solution)/shard_map/swap/ppermute | solution.py:379
  148.5 2.4 fusion
  150.9 10.2 %collective-permute-start.22 = (bf16[5,4,128,128]{3,2,1,0:T(8,128)(2,1)S(1)}, bf16[5,4,128,128]{3,2,1,0:T(8,128)(2,1)S(1)}, u32[]{:S(2)}, u32[]{:S(2)}) collective-permute-start(bf16[5,4,128,128]{3,2,1,0:T(8,128)(2,1)S(1)} %get-tuple-element.90.refs_21_), channel_id=1, source_target_pairs={{0,16},{4,20},{8,24},{12,28},{16,0},{20,4},{24,8},{28,12},{1,17},{... | collective-permute-start | bytes 1966088 | tf_op jit(solution)/shard_map/along_z2/ppermute | solution.py:375
  161.1 1.4 collective-permute-start.23
  163.3 13.4 %shard_map.95 = (bf16[5,3,128,128]{3,2,1,0:T(8,128)(2,1)S(1)}, bf16[5,3,128,128]{3,2,1,0:T(8,128)(2,1)S(1)}, bf16[5,3,128,128]{3,2,1,0:T(8,128)(2,1)S(1)}, bf16[...) custom-call(s32[3,16,2]{2,1,0:T(8,128)S(1)} %fusion.20.places, ...), custom_call_target="tpu_custom_call" | custom-call | flops 3221225472 | bytes 17500000 | tf_op jit(solution)/shard_map/pallas_call | solution.py:156
  176.8 1.3 copy-done.41
  181.2 18.5 %shard_map.96 = (bf16[2,128,2048]{2,1,0:T(8,128)(2,1)S(1)}, bf16[2,128,2048]{2,1,0:T(8,128)(2,1)S(1)}, bf16[2,128,2048]{2,1,0:T(8,128)(2,1)S(1)}, bf16[2,128,204...) custom-call(s32[7,16,2]{2,1,0:T(8,128)S(1)} %copy-done.78, ...), custom_call_target="tpu_custom_call" | custom-call | flops 3758096384 | bytes 20000000 | tf_op jit(solution)/shard_map/pallas_call | solution.py:267
  200.6 1.1 copy-done.50
  202.6 1.1 copy-done.52
  208.1 3.2 collective-permute-done.28
  211.3 3.1 fusion.8
  214.4 13.0 %collective-permute-start.31 = (bf16[5,3,128,128]{3,2,1,0:T(8,128)(2,1)}, bf16[5,3,128,128]{3,2,1,0:T(8,128)(2,1)S(1)}, u32[]{:S(2)}, u32[]{:S(2)}) collective-permute-start(bf16[5,3,128,128]{3,2,1,0:T(8,128)(2,1)} %shard_map.100), channel_id=1, source_target_pairs={{0,8},{4,12},{8,16},{12,20},{16,24},{20,28},{24,0},{28,4},{1,9},{5... | collective-permute-start | bytes 1474568 | tf_op jit(solution)/shard_map/along_z1/ppermute | solution.py:375
  227.4 5.5 %collective-permute-done.33 = bf16[2,128,2048]{2,1,0:T(8,128)(2,1)} collective-permute-done((bf16[2,128,2048]{2,1,0:T(8,128)(2,1)}, bf16[2,128,2048]{2,1,0:T(8,128)(2,1)}, u32[]{:S(2)}, u32[]{:S(2)}) %collective-permute-start.33) | collective-permute-done | bytes 1048608 | tf_op jit(solution)/shard_map/wide1/ppermute | solution.py:383
  232.9 2.0 fusion.13.refs_1_
  235.0 2.0 fusion.12.refs_0_
  237.0 2.4 collective-permute-done.31.refs_7_.refs_3_.refs_4_
  239.3 9.7 %collective-permute-done.30.refs_6_.refs_2_.refs_3_ = bf16[5,3,128,128]{3,2,1,0:T(8,128)(2,1)S(1)} collective-permute-done((bf16[5,3,128,128]{3,2,1,0:T(8,128)(2,1)}, bf16[5,3,128,128]{3,2,1,0:T(8,128)(2,1)S(1)}, u32[]{:S(2)}, u32[]{:S(2)}) %collective-permute-start.30) | collective-permute-done | bytes 491552 | tf_op jit(solution)/shard_map/along_z3/ppermute | solution.py:375
  250.9 1.4 collective-permute-start.29
  252.3 1.5 collective-permute-start.35
  253.8 1.5 collective-permute-start.34
  255.3 9.7 %collective-permute-done.36 = bf16[128,2048]{1,0:T(8,128)(2,1)} collective-permute-done((bf16[128,2048]{1,0:T(8,128)(2,1)}, bf16[128,2048]{1,0:T(8,128)(2,1)}, u32[]{:S(2)}, u32[]{:S(2)}) %collective-permute-start.36) | collective-permute-done | bytes 524320 | tf_op jit(solution)/shard_map/wide1/ppermute | solution.py:383
  265.0 1.6 fusion.7
  266.6 1.3 fusion.6
  269.7 4.7 %collective-permute-done.29.refs_5_.refs_2_ = bf16[5,3,128,128]{3,2,1,0:T(8,128)(2,1)S(1)} collective-permute-done((bf16[5,3,128,128]{3,2,1,0:T(8,128)(2,1)}, bf16[5,3,128,128]{3,2,1,0:T(8,128)(2,1)S(1)}, u32[]{:S(2)}, u32[]{:S(2)}) %collective-permute-start.29) | collective-permute-done | bytes 491552 | tf_op jit(solution)/shard_map/along_z2/ppermute | solution.py:375
  275.2 2.7 collective-permute-start.38
  277.9 7.9 %collective-permute-done.35 = bf16[2,128,2048]{2,1,0:T(8,128)(2,1)} collective-permute-done((bf16[2,128,2048]{2,1,0:T(8,128)(2,1)}, bf16[2,128,2048]{2,1,0:T(8,128)(2,1)}, u32[]{:S(2)}, u32[]{:S(2)}) %collective-permute-start.35) | collective-permute-done | bytes 1048608 | tf_op jit(solution)/shard_map/wide1/ppermute | solution.py:383
  285.8 2.0 fusion.15.refs_1_
  287.8 2.2 fusion.14.refs_0_
  290.8 1.1 collective-permute-start.39
  291.9 1.6 collective-permute-start.42
  294.0 9.6 %collective-permute-done.39 = bf16[128,2048]{1,0:T(8,128)(2,1)S(1)} collective-permute-done((bf16[128,2048]{1,0:T(8,128)(2,1)}, bf16[128,2048]{1,0:T(8,128)(2,1)S(1)}, u32[]{:S(2)}, u32[]{:S(2)}) %collective-permute-start.39) | collective-permute-done | bytes 524320 | tf_op jit(solution)/shard_map/wide1/ppermute | solution.py:383
  303.6 1.4 bitcast_add_fusion.3
  305.8 1.3 bitcast_add_fusion
  307.4 3.6 %collective-permute-start.41 = (bf16[128,2048]{1,0:T(8,128)(2,1)S(1)}, bf16[128,2048]{1,0:T(8,128)(2,1)S(1)}, u32[]{:S(2)}, u32[]{:S(2)}) collective-permute-start(bf16[128,2048]{1,0:T(8,128)(2,1)S(1)} %fusion.4), channel_id=1, source_target_pairs={{0,24},{4,28},{8,0},{12,4},{16,8},{20,12},{24,16},{28,20},{1,25},{... | collective-permute-start | bytes 1572872 | tf_op jit(solution)/shard_map/along_z3/ppermute | solution.py:375
  311.0 2.6 shard_map.101
  313.7 6.5 %collective-permute-done.41 = bf16[128,2048]{1,0:T(8,128)(2,1)S(1)} collective-permute-done((bf16[128,2048]{1,0:T(8,128)(2,1)S(1)}, bf16[128,2048]{1,0:T(8,128)(2,1)S(1)}, u32[]{:S(2)}, u32[]{:S(2)}) %collective-permute-start.41) | collective-permute-done | bytes 524320 | tf_op jit(solution)/shard_map/along_z3/ppermute | solution.py:375
  (268 shorter events, 43.9 us)
Async XLA Ops:
  0.7 21.5 %collective-permute-start.4 = (bf16[128,2048]{1,0:T(8,128)(2,1)}, bf16[128,2048]{1,0:T(8,128)(2,1)S(1)}, u32[]{:S(2)}, u32[]{:S(2)}) collective-permute-start(bf16[128,2048]{1,0:T(8,128)(2,1)} %param.5), channel_id=1, source_target_pairs={{0,8},{4,12},{8,16},{12,20},{16,24},{20,28},{24,0},{28,4},{1,9},{5... | collective-permute-start | bytes 1572872 | tf_op jit(solution)/shard_map/along_z1/ppermute | solution.py:375
  3.7 25.0 %collective-permute-start.6 = (bf16[128,2048]{1,0:T(8,128)(2,1)}, bf16[128,2048]{1,0:T(8,128)(2,1)S(1)}, u32[]{:S(2)}, u32[]{:S(2)}) collective-permute-start(bf16[128,2048]{1,0:T(8,128)(2,1)} %param.5), channel_id=1, source_target_pairs={{0,24},{4,28},{8,0},{12,4},{16,8},{20,12},{24,16},{28,20},{1,25},{... | collective-permute-start | bytes 1572872 | tf_op jit(solution)/shard_map/along_z3/ppermute | solution.py:375
  6.9 14.1 %copy-start.27 = (bf16[64,2048]{1,0:T(8,128)(2,1)}, bf16[64,2048]{1,0:T(8,128)(2,1)S(1)}, u32[]{:S(2)}) copy-start(bf16[64,2048]{1,0:T(8,128)(2,1)S(1)} %get-tuple-element.110.refs_1_) | copy-start | bytes 786436
  6.9 12.7 %collective-permute-start = (bf16[64,2048]{1,0:T(8,128)(2,1)S(1)}, bf16[64,2048]{1,0:T(8,128)(2,1)S(1)}, u32[]{:S(2)}, u32[]{:S(2)}) collective-permute-start(bf16[64,2048]{1,0:T(8,128)(2,1)S(1)} %get-tuple-element.111.refs_0_), channel_id=1, source_target_pairs={{0,1},{1,0},{2,3},{3,2},{4,5},{5,4},{6,7},{7,6},{8,9},{9,8},{10,11... | collective-permute-start | bytes 786440 | tf_op jit(solution)/shard_map/wide1/ppermute | solution.py:383
  8.6 12.4 %collective-permute-start.1 = (bf16[64,2048]{1,0:T(8,128)(2,1)S(1)}, bf16[64,2048]{1,0:T(8,128)(2,1)S(1)}, u32[]{:S(2)}, u32[]{:S(2)}) collective-permute-start(bf16[64,2048]{1,0:T(8,128)(2,1)S(1)} %get-tuple-element.110.refs_1_), channel_id=1, source_target_pairs={{0,2},{1,3},{2,0},{3,1},{4,6},{5,7},{6,4},{7,5},{8,10},{9,11},{10,... | collective-permute-start | bytes 786440 | tf_op jit(solution)/shard_map/wide2/ppermute | solution.py:383
  20.5 22.0 %collective-permute-start.2 = (bf16[128,2048]{1,0:T(8,128)(2,1)S(1)}, bf16[128,2048]{1,0:T(8,128)(2,1)S(1)}, u32[]{:S(2)}, u32[]{:S(2)}) collective-permute-start(bf16[128,2048]{1,0:T(8,128)(2,1)S(1)} %pad_maximum_fusion.4), channel_id=1, source_target_pairs={{0,2},{1,3},{2,0},{3,1},{4,6},{5,7},{6,4},{7,5},{8,10},{9,11},{10,... | collective-permute-start | bytes 1572872 | tf_op jit(solution)/shard_map/wide2/ppermute | solution.py:383
  21.7 20.8 %collective-permute-start.3 = (bf16[128,2048]{1,0:T(8,128)(2,1)S(1)}, bf16[128,2048]{1,0:T(8,128)(2,1)S(1)}, u32[]{:S(2)}, u32[]{:S(2)}) collective-permute-start(bf16[128,2048]{1,0:T(8,128)(2,1)S(1)} %pad_maximum_fusion.5), channel_id=1, source_target_pairs={{0,1},{1,0},{2,3},{3,2},{4,5},{5,4},{6,7},{7,6},{8,9},{9,8},{10,11... | collective-permute-start | bytes 1572872 | tf_op jit(solution)/shard_map/wide1/ppermute | solution.py:383
  22.1 18.3 %collective-permute-start.5 = (bf16[128,2048]{1,0:T(8,128)(2,1)S(1)}, bf16[128,2048]{1,0:T(8,128)(2,1)S(1)}, u32[]{:S(2)}, u32[]{:S(2)}) collective-permute-start(bf16[128,2048]{1,0:T(8,128)(2,1)S(1)} %collective-permute-done.4), channel_id=1, source_target_pairs={{0,8},{4,12},{8,16},{12,20},{16,24},{20,28},{24,0},{28,4},{1,9},{5... | collective-permute-start | bytes 1572872 | tf_op jit(solution)/shard_map/along_z1/ppermute | solution.py:375
  43.5 17.4 %collective-permute-start.8 = (bf16[192,2048]{1,0:T(8,128)(2,1)}, bf16[192,2048]{1,0:T(8,128)(2,1)S(1)}, u32[]{:S(2)}, u32[]{:S(2)}) collective-permute-start(bf16[192,2048]{1,0:T(8,128)(2,1)} %get-tuple-element.48.refs_7_), channel_id=1, source_target_pairs={{0,2},{1,3},{2,0},{3,1},{4,6},{5,7},{6,4},{7,5},{8,10},{9,11},{10,... | collective-permute-start | bytes 2359304 | tf_op jit(solution)/shard_map/wide2/ppermute | solution.py:383
  45.0 18.7 %collective-permute-start.7 = (bf16[192,2048]{1,0:T(8,128)(2,1)}, bf16[192,2048]{1,0:T(8,128)(2,1)S(1)}, u32[]{:S(2)}, u32[]{:S(2)}) collective-permute-start(bf16[192,2048]{1,0:T(8,128)(2,1)} %get-tuple-element.47.refs_6_), channel_id=1, source_target_pairs={{0,1},{1,0},{2,3},{3,2},{4,5},{5,4},{6,7},{7,6},{8,9},{9,8},{10,11... | collective-permute-start | bytes 2359304 | tf_op jit(solution)/shard_map/wide1/ppermute | solution.py:383
  46.5 43.7 %collective-permute-start.11 = (bf16[5,4,128,128]{3,2,1,0:T(8,128)(2,1)}, bf16[5,4,128,128]{3,2,1,0:T(8,128)(2,1)}, u32[]{:S(2)}, u32[]{:S(2)}) collective-permute-start(bf16[5,4,128,128]{3,2,1,0:T(8,128)(2,1)} %shard_map.86), channel_id=1, source_target_pairs={{0,16},{4,20},{8,24},{12,28},{16,0},{20,4},{24,8},{28,12},{1,17},{... | collective-permute-start | bytes 1966088 | tf_op jit(solution)/shard_map/along_z2/ppermute | solution.py:375
  47.2 13.7 %copy-start.3 = (bf16[192,2048]{1,0:T(8,128)(2,1)S(1)}, bf16[192,2048]{1,0:T(8,128)(2,1)}, u32[]{:S(2)}) copy-start(bf16[192,2048]{1,0:T(8,128)(2,1)} %get-tuple-element.48.refs_7_) | copy-start | bytes 2359300
  47.2 43.0 %collective-permute-start.12 = (bf16[5,4,128,128]{3,2,1,0:T(8,128)(2,1)}, bf16[5,4,128,128]{3,2,1,0:T(8,128)(2,1)}, u32[]{:S(2)}, u32[]{:S(2)}) collective-permute-start(bf16[5,4,128,128]{3,2,1,0:T(8,128)(2,1)} %shard_map.87), channel_id=1, source_target_pairs={{0,8},{4,12},{8,16},{12,20},{16,24},{20,28},{24,0},{28,4},{1,9},{5... | collective-permute-start | bytes 1966088 | tf_op jit(solution)/shard_map/along_z1/ppermute | solution.py:375
  48.7 15.0 %copy-start.2 = (bf16[192,2048]{1,0:T(8,128)(2,1)S(1)}, bf16[192,2048]{1,0:T(8,128)(2,1)}, u32[]{:S(2)}) copy-start(bf16[192,2048]{1,0:T(8,128)(2,1)} %get-tuple-element.47.refs_6_) | copy-start | bytes 2359300
  48.7 41.4 %collective-permute-start.13 = (bf16[5,4,128,128]{3,2,1,0:T(8,128)(2,1)}, bf16[5,4,128,128]{3,2,1,0:T(8,128)(2,1)}, u32[]{:S(2)}, u32[]{:S(2)}) collective-permute-start(bf16[5,4,128,128]{3,2,1,0:T(8,128)(2,1)} %shard_map.88), channel_id=1, source_target_pairs={{0,24},{4,28},{8,0},{12,4},{16,8},{20,12},{24,16},{28,20},{1,25},{... | collective-permute-start | bytes 1966088 | tf_op jit(solution)/shard_map/along_z3/ppermute | solution.py:375
  60.9 52.1 %copy-start.20 = (bf16[192,2048]{1,0:T(8,128)(2,1)}, bf16[192,2048]{1,0:T(8,128)(2,1)S(1)}, u32[]{:S(2)}) copy-start(bf16[192,2048]{1,0:T(8,128)(2,1)S(1)} %collective-permute-done.8.refs_9_) | copy-start | bytes 2359300
  62.2 50.7 %collective-permute-start.10 = (bf16[384,2048]{1,0:T(8,128)(2,1)}, bf16[384,2048]{1,0:T(8,128)(2,1)}, u32[]{:S(2)}, u32[]{:S(2)}) collective-permute-start(bf16[384,2048]{1,0:T(8,128)(2,1)} %pad_maximum_fusion.1), channel_id=1, source_target_pairs={{0,1},{1,0},{2,3},{3,2},{4,5},{5,4},{6,7},{7,6},{8,9},{9,8},{10,11... | collective-permute-start | bytes 4718600 | tf_op jit(solution)/shard_map/wide1/ppermute | solution.py:383
  65.1 47.8 %collective-permute-start.9 = (bf16[384,2048]{1,0:T(8,128)(2,1)}, bf16[384,2048]{1,0:T(8,128)(2,1)}, u32[]{:S(2)}, u32[]{:S(2)}) collective-permute-start(bf16[384,2048]{1,0:T(8,128)(2,1)} %pad_maximum_fusion), channel_id=1, source_target_pairs={{0,2},{1,3},{2,0},{3,1},{4,6},{5,7},{6,4},{7,5},{8,10},{9,11},{10,... | collective-permute-start | bytes 4718600 | tf_op jit(solution)/shard_map/wide2/ppermute | solution.py:383
  90.1 2.4 collective-permute-start.16
  90.2 19.1 %collective-permute-start.14 = (bf16[5,7,128,128]{3,2,1,0:T(8,128)(2,1)}, bf16[5,7,128,128]{3,2,1,0:T(8,128)(2,1)}, u32[]{:S(2)}, u32[]{:S(2)}) collective-permute-start(bf16[5,7,128,128]{3,2,1,0:T(8,128)(2,1)} %shard_map.89.refs_12_.refs_0_.refs_9_), channel_id=1, source_target_pairs={{0,4},{4,0},{8,12},{12,8},{16,20},{20,16},{24,28},{28,24},{1,5},{5... | collective-permute-start | bytes 3440648 | tf_op jit(solution)/shard_map/swap/ppermute | solution.py:379
  90.7 4.5 %collective-permute-start.15 = (bf16[5,4,128,128]{3,2,1,0:T(8,128)(2,1)}, bf16[5,4,128,128]{3,2,1,0:T(8,128)(2,1)}, u32[]{:S(2)}, u32[]{:S(2)}) collective-permute-start(bf16[5,4,128,128]{3,2,1,0:T(8,128)(2,1)} %collective-permute-done.12.refs_2_.refs_13_.refs_1_), channel_id=1, source_target_pairs={{0,4},{4,0},{8,12},{12,8},{16,20},{20,16},{24,28},{28,24},{1,5},{5... | collective-permute-start | bytes 1966088 | tf_op jit(solution)/shard_map/swap/ppermute | solution.py:379
  92.5 15.8 %collective-permute-start.17 = (bf16[5,4,128,128]{3,2,1,0:T(8,128)(2,1)}, bf16[5,4,128,128]{3,2,1,0:T(8,128)(2,1)}, u32[]{:S(2)}, u32[]{:S(2)}) collective-permute-start(bf16[5,4,128,128]{3,2,1,0:T(8,128)(2,1)} %collective-permute-done.13.refs_3_.refs_15_.refs_1_), channel_id=1, source_target_pairs={{0,4},{4,0},{8,12},{12,8},{16,20},{20,16},{24,28},{28,24},{1,5},{5... | collective-permute-start | bytes 1966088 | tf_op jit(solution)/shard_map/swap/ppermute | solution.py:379
  93.3 19.6 %copy-start.13 = (bf16[5,7,128,128]{3,2,1,0:T(8,128)(2,1)S(1)}, bf16[5,7,128,128]{3,2,1,0:T(8,128)(2,1)}, u32[]{:S(2)}) copy-start(bf16[5,7,128,128]{3,2,1,0:T(8,128)(2,1)} %shard_map.89.refs_12_.refs_0_.refs_9_) | copy-start | bytes 3440644
  95.2 47.9 %collective-permute-start.19 = (bf16[5,3,128,128]{3,2,1,0:T(8,128)(2,1)}, bf16[5,3,128,128]{3,2,1,0:T(8,128)(2,1)}, u32[]{:S(2)}, u32[]{:S(2)}) collective-permute-start(bf16[5,3,128,128]{3,2,1,0:T(8,128)(2,1)} %shard_map.92), channel_id=1, source_target_pairs={{0,16},{4,20},{8,24},{12,28},{16,0},{20,4},{24,8},{28,12},{1,17},{... | collective-permute-start | bytes 1474568 | tf_op jit(solution)/shard_map/along_z2/ppermute | solution.py:375
  108.3 34.8 %collective-permute-start.18 = (bf16[5,3,128,128]{3,2,1,0:T(8,128)(2,1)}, bf16[5,3,128,128]{3,2,1,0:T(8,128)(2,1)}, u32[]{:S(2)}, u32[]{:S(2)}) collective-permute-start(bf16[5,3,128,128]{3,2,1,0:T(8,128)(2,1)} %shard_map.91), channel_id=1, source_target_pairs={{0,8},{4,12},{8,16},{12,20},{16,24},{20,28},{24,0},{28,4},{1,9},{5... | collective-permute-start | bytes 1474568 | tf_op jit(solution)/shard_map/along_z1/ppermute | solution.py:375
  109.3 33.8 %collective-permute-start.20 = (bf16[5,3,128,128]{3,2,1,0:T(8,128)(2,1)}, bf16[5,3,128,128]{3,2,1,0:T(8,128)(2,1)}, u32[]{:S(2)}, u32[]{:S(2)}) collective-permute-start(bf16[5,3,128,128]{3,2,1,0:T(8,128)(2,1)} %shard_map.93), channel_id=1, source_target_pairs={{0,24},{4,28},{8,0},{12,4},{16,8},{20,12},{24,16},{28,20},{1,25},{... | collective-permute-start | bytes 1474568 | tf_op jit(solution)/shard_map/along_z3/ppermute | solution.py:375
  143.1 5.2 %collective-permute-start.21 = (bf16[4,5,4,128,128]{4,3,2,1,0:T(8,128)(2,1)}, bf16[4,5,4,128,128]{4,3,2,1,0:T(8,128)(2,1)S(1)}, u32[]{:S(2)}, u32[]{:S(2)}) collective-permute-start(bf16[4,5,4,128,128]{4,3,2,1,0:T(8,128)(2,1)} %shard_map.94), channel_id=1, source_target_pairs={{0,4},{4,0},{8,12},{12,8},{16,20},{20,16},{24,28},{28,24},{1,5},{5... | collective-permute-start | bytes 7864328 | tf_op jit(solution)/shard_map/swap/ppermute | solution.py:379
  143.2 19.3 %collective-permute-start.26 = (bf16[5,3,128,128]{3,2,1,0:T(8,128)(2,1)}, bf16[5,3,128,128]{3,2,1,0:T(8,128)(2,1)S(1)}, u32[]{:S(2)}, u32[]{:S(2)}) collective-permute-start(bf16[5,3,128,128]{3,2,1,0:T(8,128)(2,1)} %collective-permute-done.19.refs_2_.refs_14_.refs_11_), channel_id=1, source_target_pairs={{0,4},{4,0},{8,12},{12,8},{16,20},{20,16},{24,28},{28,24},{1,5},{5... | collective-permute-start | bytes 1474568 | tf_op jit(solution)/shard_map/swap/ppermute | solution.py:379
  143.7 19.5 %collective-permute-start.25 = (bf16[5,3,128,128]{3,2,1,0:T(8,128)(2,1)}, bf16[5,3,128,128]{3,2,1,0:T(8,128)(2,1)S(1)}, u32[]{:S(2)}, u32[]{:S(2)}) collective-permute-start(bf16[5,3,128,128]{3,2,1,0:T(8,128)(2,1)} %collective-permute-done.18.refs_1_.refs_13_.refs_10_), channel_id=1, source_target_pairs={{0,4},{4,0},{8,12},{12,8},{16,20},{20,16},{24,28},{28,24},{1,5},{5... | collective-permute-start | bytes 1474568 | tf_op jit(solution)/shard_map/swap/ppermute | solution.py:379
  143.8 19.4 %collective-permute-start.27 = (bf16[5,3,128,128]{3,2,1,0:T(8,128)(2,1)}, bf16[5,3,128,128]{3,2,1,0:T(8,128)(2,1)S(1)}, u32[]{:S(2)}, u32[]{:S(2)}) collective-permute-start(bf16[5,3,128,128]{3,2,1,0:T(8,128)(2,1)} %collective-permute-done.20.refs_3_.refs_15_.refs_12_), channel_id=1, source_target_pairs={{0,4},{4,0},{8,12},{12,8},{16,20},{20,16},{24,28},{28,24},{1,5},{5... | collective-permute-start | bytes 1474568 | tf_op jit(solution)/shard_map/swap/ppermute | solution.py:379
  148.3 14.8 %copy-start.89 = (s32[7,16,1]{2,1,0:T(8,128)S(1)}, s32[7,16,1]{2,1,0:T(8,128)}, u32[]{:S(2)}) copy-start(s32[7,16,1]{2,1,0:T(8,128)} %copy-done.88) | copy-start | bytes 1348
  148.3 14.8 %copy-start.91 = (s32[7,16,1]{2,1,0:T(8,128)S(1)}, s32[7,16,1]{2,1,0:T(8,128)}, u32[]{:S(2)}) copy-start(s32[7,16,1]{2,1,0:T(8,128)} %copy-done.90) | copy-start | bytes 1348
  148.4 14.9 %copy-start.14 = (bf16[5,7,128,128]{3,2,1,0:T(8,128)(2,1)S(1)}, bf16[5,7,128,128]{3,2,1,0:T(8,128)(2,1)}, u32[]{:S(2)}) copy-start(bf16[5,7,128,128]{3,2,1,0:T(8,128)(2,1)} %shard_map.89.refs_12_.refs_0_.refs_9_) | copy-start | bytes 3440644
  148.4 14.9 %copy-start.21 = (bf16[192,2048]{1,0:T(8,128)(2,1)S(1)}, bf16[192,2048]{1,0:T(8,128)(2,1)}, u32[]{:S(2)}) copy-start(bf16[192,2048]{1,0:T(8,128)(2,1)} %copy-done.20) | copy-start | bytes 2359300
  148.4 14.9 %copy-start.24 = (bf16[192,2048]{1,0:T(8,128)(2,1)S(1)}, bf16[192,2048]{1,0:T(8,128)(2,1)}, u32[]{:S(2)}) copy-start(bf16[192,2048]{1,0:T(8,128)(2,1)} %copy-done.22) | copy-start | bytes 2359300
  148.4 14.9 %copy-start.29 = (bf16[64,2048]{1,0:T(8,128)(2,1)S(1)}, bf16[64,2048]{1,0:T(8,128)(2,1)}, u32[]{:S(2)}) copy-start(bf16[64,2048]{1,0:T(8,128)(2,1)} %copy-done.27) | copy-start | bytes 786436
  148.4 14.9 %copy-start.32 = (bf16[64,2048]{1,0:T(8,128)(2,1)S(1)}, bf16[64,2048]{1,0:T(8,128)(2,1)}, u32[]{:S(2)}) copy-start(bf16[64,2048]{1,0:T(8,128)(2,1)} %copy-done.30) | copy-start | bytes 786436
  148.4 14.9 %copy-start.35 = (bf16[128,2048]{1,0:T(8,128)(2,1)S(1)}, bf16[128,2048]{1,0:T(8,128)(2,1)}, u32[]{:S(2)}) copy-start(bf16[128,2048]{1,0:T(8,128)(2,1)} %copy-done.33) | copy-start | bytes 1572868
  148.4 14.9 %copy-start.38 = (bf16[128,2048]{1,0:T(8,128)(2,1)S(1)}, bf16[128,2048]{1,0:T(8,128)(2,1)}, u32[]{:S(2)}) copy-start(bf16[128,2048]{1,0:T(8,128)(2,1)} %copy-done.36) | copy-start | bytes 1572868
  148.4 14.9 %copy-start.46 = (bf16[64,2048]{1,0:T(8,128)(2,1)S(1)}, bf16[64,2048]{1,0:T(8,128)(2,1)}, u32[]{:S(2)}) copy-start(bf16[64,2048]{1,0:T(8,128)(2,1)} %copy-done.44) | copy-start | bytes 786436
  148.4 14.9 %copy-start.49 = (bf16[64,2048]{1,0:T(8,128)(2,1)S(1)}, bf16[64,2048]{1,0:T(8,128)(2,1)}, u32[]{:S(2)}) copy-start(bf16[64,2048]{1,0:T(8,128)(2,1)} %copy-done.47) | copy-start | bytes 786436
  150.9 25.9 %copy-start.10 = (bf16[5,4,128,128]{3,2,1,0:T(8,128)(2,1)}, bf16[5,4,128,128]{3,2,1,0:T(8,128)(2,1)S(1)}, u32[]{:S(2)}) copy-start(bf16[5,4,128,128]{3,2,1,0:T(8,128)(2,1)S(1)} %get-tuple-element.91.refs_20_.refs_0_) | copy-start | bytes 1966084
  150.9 54.8 %collective-permute-start.22 = (bf16[5,4,128,128]{3,2,1,0:T(8,128)(2,1)S(1)}, bf16[5,4,128,128]{3,2,1,0:T(8,128)(2,1)S(1)}, u32[]{:S(2)}, u32[]{:S(2)}) collective-permute-start(bf16[5,4,128,128]{3,2,1,0:T(8,128)(2,1)S(1)} %get-tuple-element.90.refs_21_), channel_id=1, source_target_pairs={{0,16},{4,20},{8,24},{12,28},{16,0},{20,4},{24,8},{28,12},{1,17},{... | collective-permute-start | bytes 1966088 | tf_op jit(solution)/shard_map/along_z2/ppermute | solution.py:375
  161.1 44.6 %collective-permute-start.23 = (bf16[5,4,128,128]{3,2,1,0:T(8,128)(2,1)S(1)}, bf16[5,4,128,128]{3,2,1,0:T(8,128)(2,1)S(1)}, u32[]{:S(2)}, u32[]{:S(2)}) collective-permute-start(bf16[5,4,128,128]{3,2,1,0:T(8,128)(2,1)S(1)} %get-tuple-element.89.refs_22_), channel_id=1, source_target_pairs={{0,24},{4,28},{8,0},{12,4},{16,8},{20,12},{24,16},{28,20},{1,25},{... | collective-permute-start | bytes 1966088 | tf_op jit(solution)/shard_map/along_z3/ppermute | solution.py:375
  162.5 43.2 %collective-permute-start.24 = (bf16[5,4,128,128]{3,2,1,0:T(8,128)(2,1)S(1)}, bf16[5,4,128,128]{3,2,1,0:T(8,128)(2,1)S(1)}, u32[]{:S(2)}, u32[]{:S(2)}) collective-permute-start(bf16[5,4,128,128]{3,2,1,0:T(8,128)(2,1)S(1)} %get-tuple-element.88.refs_23_), channel_id=1, source_target_pairs={{0,8},{4,12},{8,16},{12,20},{16,24},{20,28},{24,0},{28,4},{1,9},{5... | collective-permute-start | bytes 1966088 | tf_op jit(solution)/shard_map/along_z1/ppermute | solution.py:375
  163.3 17.9 %copy-start.78 = (s32[7,16,2]{2,1,0:T(8,128)S(1)}, s32[7,16,2]{2,1,0:T(8,128)}, u32[]{:S(2)}) copy-start(s32[7,16,2]{2,1,0:T(8,128)} %pad_add_fusion.refs_5_.places) | copy-start | bytes 2692
  163.3 17.8 %copy-start.81 = (bf16[5,4,128,128]{3,2,1,0:T(8,128)(2,1)S(1)}, bf16[5,4,128,128]{3,2,1,0:T(8,128)(2,1)}, u32[]{:S(2)}) copy-start(bf16[5,4,128,128]{3,2,1,0:T(8,128)(2,1)} %copy-done.79) | copy-start | bytes 1966084
  206.9 4.3 %collective-permute-start.28 = (bf16[4,5,3,128,128]{4,3,2,1,0:T(8,128)(2,1)}, bf16[4,5,3,128,128]{4,3,2,1,0:T(8,128)(2,1)}, u32[]{:S(2)}, u32[]{:S(2)}) collective-permute-start(bf16[4,5,3,128,128]{4,3,2,1,0:T(8,128)(2,1)} %shard_map.97), channel_id=1, source_target_pairs={{0,4},{4,0},{8,12},{12,8},{16,20},{20,16},{24,28},{28,24},{1,5},{5... | collective-permute-start | bytes 5898248 | tf_op jit(solution)/shard_map/swap/ppermute | solution.py:379
  207.0 25.9 %collective-permute-start.33 = (bf16[2,128,2048]{2,1,0:T(8,128)(2,1)}, bf16[2,128,2048]{2,1,0:T(8,128)(2,1)}, u32[]{:S(2)}, u32[]{:S(2)}) collective-permute-start(bf16[2,128,2048]{2,1,0:T(8,128)(2,1)} %get-tuple-element.76), channel_id=1, source_target_pairs={{0,1},{1,0},{2,3},{3,2},{4,5},{5,4},{6,7},{7,6},{8,9},{9,8},{10,11... | collective-permute-start | bytes 3145736 | tf_op jit(solution)/shard_map/wide1/ppermute | solution.py:383
  207.6 27.4 %collective-permute-start.32 = (bf16[2,128,2048]{2,1,0:T(8,128)(2,1)}, bf16[2,128,2048]{2,1,0:T(8,128)(2,1)}, u32[]{:S(2)}, u32[]{:S(2)}) collective-permute-start(bf16[2,128,2048]{2,1,0:T(8,128)(2,1)} %get-tuple-element.74), channel_id=1, source_target_pairs={{0,2},{1,3},{2,0},{3,1},{4,6},{5,7},{6,4},{7,5},{8,10},{9,11},{10,... | collective-permute-start | bytes 3145736 | tf_op jit(solution)/shard_map/wide2/ppermute | solution.py:383
  214.4 18.5 %copy-start.53 = (bf16[2,128,2048]{2,1,0:T(8,128)(2,1)S(1)}, bf16[2,128,2048]{2,1,0:T(8,128)(2,1)}, u32[]{:S(2)}) copy-start(bf16[2,128,2048]{2,1,0:T(8,128)(2,1)} %copy-done.52) | copy-start | bytes 3145732
  214.4 24.9 %collective-permute-start.31 = (bf16[5,3,128,128]{3,2,1,0:T(8,128)(2,1)}, bf16[5,3,128,128]{3,2,1,0:T(8,128)(2,1)S(1)}, u32[]{:S(2)}, u32[]{:S(2)}) collective-permute-start(bf16[5,3,128,128]{3,2,1,0:T(8,128)(2,1)} %shard_map.100), channel_id=1, source_target_pairs={{0,8},{4,12},{8,16},{12,20},{16,24},{20,28},{24,0},{28,4},{1,9},{5... | collective-permute-start | bytes 1474568 | tf_op jit(solution)/shard_map/along_z1/ppermute | solution.py:375
  227.4 21.6 %collective-permute-start.30 = (bf16[5,3,128,128]{3,2,1,0:T(8,128)(2,1)}, bf16[5,3,128,128]{3,2,1,0:T(8,128)(2,1)S(1)}, u32[]{:S(2)}, u32[]{:S(2)}) collective-permute-start(bf16[5,3,128,128]{3,2,1,0:T(8,128)(2,1)} %shard_map.99), channel_id=1, source_target_pairs={{0,24},{4,28},{8,0},{12,4},{16,8},{20,12},{24,16},{28,20},{1,25},{... | collective-permute-start | bytes 1474568 | tf_op jit(solution)/shard_map/along_z3/ppermute | solution.py:375
  249.8 15.2 %collective-permute-start.36 = (bf16[128,2048]{1,0:T(8,128)(2,1)}, bf16[128,2048]{1,0:T(8,128)(2,1)}, u32[]{:S(2)}, u32[]{:S(2)}) collective-permute-start(bf16[128,2048]{1,0:T(8,128)(2,1)} %get-tuple-element.77.refs_2_), channel_id=1, source_target_pairs={{0,1},{1,0},{2,3},{3,2},{4,5},{5,4},{6,7},{7,6},{8,9},{9,8},{10,11... | collective-permute-start | bytes 1572872 | tf_op jit(solution)/shard_map/wide1/ppermute | solution.py:383
  250.4 16.2 %collective-permute-start.37 = (bf16[128,2048]{1,0:T(8,128)(2,1)}, bf16[128,2048]{1,0:T(8,128)(2,1)S(1)}, u32[]{:S(2)}, u32[]{:S(2)}) collective-permute-start(bf16[128,2048]{1,0:T(8,128)(2,1)} %get-tuple-element.78.refs_3_), channel_id=1, source_target_pairs={{0,2},{1,3},{2,0},{3,1},{4,6},{5,7},{6,4},{7,5},{8,10},{9,11},{10,... | collective-permute-start | bytes 1572872 | tf_op jit(solution)/shard_map/wide2/ppermute | solution.py:383
  250.9 23.5 %collective-permute-start.29 = (bf16[5,3,128,128]{3,2,1,0:T(8,128)(2,1)}, bf16[5,3,128,128]{3,2,1,0:T(8,128)(2,1)S(1)}, u32[]{:S(2)}, u32[]{:S(2)}) collective-permute-start(bf16[5,3,128,128]{3,2,1,0:T(8,128)(2,1)} %shard_map.98), channel_id=1, source_target_pairs={{0,16},{4,20},{8,24},{12,28},{16,0},{20,4},{24,8},{28,12},{1,17},{... | collective-permute-start | bytes 1474568 | tf_op jit(solution)/shard_map/along_z2/ppermute | solution.py:375
  252.3 33.5 %collective-permute-start.35 = (bf16[2,128,2048]{2,1,0:T(8,128)(2,1)}, bf16[2,128,2048]{2,1,0:T(8,128)(2,1)}, u32[]{:S(2)}, u32[]{:S(2)}) collective-permute-start(bf16[2,128,2048]{2,1,0:T(8,128)(2,1)} %get-tuple-element.81), channel_id=1, source_target_pairs={{0,1},{1,0},{2,3},{3,2},{4,5},{5,4},{6,7},{7,6},{8,9},{9,8},{10,11... | collective-permute-start | bytes 3145736 | tf_op jit(solution)/shard_map/wide1/ppermute | solution.py:383
  253.8 34.0 %collective-permute-start.34 = (bf16[2,128,2048]{2,1,0:T(8,128)(2,1)}, bf16[2,128,2048]{2,1,0:T(8,128)(2,1)}, u32[]{:S(2)}, u32[]{:S(2)}) collective-permute-start(bf16[2,128,2048]{2,1,0:T(8,128)(2,1)} %get-tuple-element.79), channel_id=1, source_target_pairs={{0,2},{1,3},{2,0},{3,1},{4,6},{5,7},{6,4},{7,5},{8,10},{9,11},{10,... | collective-permute-start | bytes 3145736 | tf_op jit(solution)/shard_map/wide2/ppermute | solution.py:383
  268.9 16.8 %copy-start.87 = (bf16[2,128,2048]{2,1,0:T(8,128)(2,1)S(1)}, bf16[2,128,2048]{2,1,0:T(8,128)(2,1)}, u32[]{:S(2)}) copy-start(bf16[2,128,2048]{2,1,0:T(8,128)(2,1)} %get-tuple-element.80) | copy-start | bytes 3145732
  275.2 14.8 %collective-permute-start.38 = (bf16[128,2048]{1,0:T(8,128)(2,1)}, bf16[128,2048]{1,0:T(8,128)(2,1)S(1)}, u32[]{:S(2)}, u32[]{:S(2)}) collective-permute-start(bf16[128,2048]{1,0:T(8,128)(2,1)} %get-tuple-element.82), channel_id=1, source_target_pairs={{0,24},{4,28},{8,0},{12,4},{16,8},{20,12},{24,16},{28,20},{1,25},{... | collective-permute-start | bytes 1572872 | tf_op jit(solution)/shard_map/along_z3/ppermute | solution.py:375
  290.8 12.8 %collective-permute-start.39 = (bf16[128,2048]{1,0:T(8,128)(2,1)}, bf16[128,2048]{1,0:T(8,128)(2,1)S(1)}, u32[]{:S(2)}, u32[]{:S(2)}) collective-permute-start(bf16[128,2048]{1,0:T(8,128)(2,1)} %get-tuple-element.83), channel_id=1, source_target_pairs={{0,1},{1,0},{2,3},{3,2},{4,5},{5,4},{6,7},{7,6},{8,9},{9,8},{10,11... | collective-permute-start | bytes 1572872 | tf_op jit(solution)/shard_map/wide1/ppermute | solution.py:383
  291.9 21.8 %collective-permute-start.42 = (bf16[128,2048]{1,0:T(8,128)(2,1)S(1)}, bf16[128,2048]{1,0:T(8,128)(2,1)S(1)}, u32[]{:S(2)}, u32[]{:S(2)}) collective-permute-start(bf16[128,2048]{1,0:T(8,128)(2,1)S(1)} %copy-done.84), channel_id=1, source_target_pairs={{0,8},{4,12},{8,16},{12,20},{16,24},{20,28},{24,0},{28,4},{1,9},{5... | collective-permute-start | bytes 1572872 | tf_op jit(solution)/shard_map/along_z1/ppermute | solution.py:375
  293.4 12.3 %collective-permute-start.40 = (bf16[128,2048]{1,0:T(8,128)(2,1)}, bf16[128,2048]{1,0:T(8,128)(2,1)S(1)}, u32[]{:S(2)}, u32[]{:S(2)}) collective-permute-start(bf16[128,2048]{1,0:T(8,128)(2,1)} %get-tuple-element.84), channel_id=1, source_target_pairs={{0,2},{1,3},{2,0},{3,1},{4,6},{5,7},{6,4},{7,5},{8,10},{9,11},{10,... | collective-permute-start | bytes 1572872 | tf_op jit(solution)/shard_map/wide2/ppermute | solution.py:383
  307.4 12.8 %collective-permute-start.41 = (bf16[128,2048]{1,0:T(8,128)(2,1)S(1)}, bf16[128,2048]{1,0:T(8,128)(2,1)S(1)}, u32[]{:S(2)}, u32[]{:S(2)}) collective-permute-start(bf16[128,2048]{1,0:T(8,128)(2,1)S(1)} %fusion.4), channel_id=1, source_target_pairs={{0,24},{4,28},{8,0},{12,4},{16,8},{20,12},{24,16},{28,20},{1,25},{... | collective-permute-start | bytes 1572872 | tf_op jit(solution)/shard_map/along_z3/ppermute | solution.py:375
  (71 other events, 176.5 us)

commit v5 on v4

--- a/solution.py
+++ b/solution.py
@@ -480,7 +480,7 @@
         if not moved:
             two, three = hold([a.astype(BF16) for a in shares], *sent[-1])
             moved = [along_z(two, nz - 1), along_z(three, nz - 3)]
-            step = moved[:1]
+            step = moved[1:]
         else:
             one = (shares[0] + moved[0].astype(F32)).astype(BF16)
             total = along_z(one, nz - 1).astype(F32) + moved[1].astype(F32) + shares[1]

time: 322 us -> 321 us (level)
  no operation moved by 1% of the time
where the time goes in v5:
time: 321 us; the launch traced here: 320 us
  waiting for transfers between devices  119 us (37%)
  starting transfers between devices  79.6 us (25%)
  Pallas kernels  50.9 us (16%)
  local copies, waits for them, and re-layouts  41.7 us (13%)
  other arithmetic  28 us (9%)
    ppermute x18, waiting for transfers between devices, along_z(): lax.ppermute(a, 'narrow', [(i, (i + 2 * s) % narrow) for i in range(narro...  64.8 us
    ppermute x18, starting transfers between devices, along_z(): lax.ppermute(a, 'narrow', [(i, (i + 2 * s) % narrow) for i in range(narro...  59.5 us
    ppermute x16, waiting for transfers between devices, over_wide(): return lax.ppermute(a, 'wide', [(i, i ^ m) for i in range(nw)])  43 us
    unnamed x184, local copies, waits for them, and re-layouts  39.3 us
    pallas_call x2, Pallas kernels, forward_call(): pl.pallas_call(functools.partial(forward_kernel, nz, nw, spd, len(earlier...  29.5 us
    pallas_call x1, Pallas kernels, inputs_call(): pl.pallas_call(functools.partial(inputs_kernel, nz, spd, counts, groups,...  18.4 us
    ppermute x16, starting transfers between devices, over_wide(): return lax.ppermute(a, 'wide', [(i, i ^ m) for i in range(nw)])  18.4 us
    ppermute x9, waiting for transfers between devices, swap(): return lax.ppermute(a, 'narrow', [(i, i ^ 1) for i in range(narrow)])  10.8 us
  transfers between devices with their start and end apart: 43, of which 17 were waited for; matrix products, arithmetic and copies ran while one was open for 9% of the time, Pallas kernels for 16%

profile of v5, /device:TPU:0, one launch (start us, length us, event | category | flops | bytes accessed | tf_op | source)
XLA Modules:
  0.0 320.3 jit_solution(2472818310986187693)
XLA Ops:
  0.7 3.1 collective-permute-start.4
  3.7 2.1 collective-permute-start.6
  5.8 1.1 fusion.29
  6.9 1.7 collective-permute-start
  8.6 1.5 collective-permute-start.1
  12.2 1.5 copy-done.42
  13.6 1.5 copy-done.43
  22.2 6.6 %collective-permute-done.6 = bf16[128,2048]{1,0:T(8,128)(2,1)S(1)} collective-permute-done((bf16[128,2048]{1,0:T(8,128)(2,1)}, bf16[128,2048]{1,0:T(8,128)(2,1)S(1)}, u32[]{:S(2)}, u32[]{:S(2)}) %collective-permute-start.6) | collective-permute-done | bytes 524320 | tf_op jit(solution)/shard_map/along_z3/ppermute | solution.py:375
  28.8 11.6 %collective-permute-done.5.refs_1_ = bf16[128,2048]{1,0:T(8,128)(2,1)S(1)} collective-permute-done((bf16[128,2048]{1,0:T(8,128)(2,1)S(1)}, bf16[128,2048]{1,0:T(8,128)(2,1)S(1)}, u32[]{:S(2)}, u32[]{:S(2)}) %collective-permute-start.5) | collective-permute-done | bytes 524320 | tf_op jit(solution)/shard_map/along_z1/ppermute | solution.py:375
  41.2 1.2 pad_maximum_fusion.2
  43.5 1.5 collective-permute-start.8
  45.0 1.5 collective-permute-start.7
  47.2 1.6 collective-permute-start.12
  48.7 2.2 collective-permute-start.13
  51.0 9.9 %collective-permute-done.8.refs_9_ = bf16[192,2048]{1,0:T(8,128)(2,1)S(1)} collective-permute-done((bf16[192,2048]{1,0:T(8,128)(2,1)}, bf16[192,2048]{1,0:T(8,128)(2,1)S(1)}, u32[]{:S(2)}, u32[]{:S(2)}) %collective-permute-start.8) | collective-permute-done | bytes 786464 | tf_op jit(solution)/shard_map/wide2/ppermute | solution.py:383
  60.9 1.3 pad_maximum_fusion.1
  62.2 1.5 collective-permute-start.10
  63.7 1.4 pad_maximum_fusion
  65.1 1.5 collective-permute-start.9
  66.6 23.5 %collective-permute-done.11.refs_1_.refs_14_.refs_2_ = bf16[5,4,128,128]{3,2,1,0:T(8,128)(2,1)} collective-permute-done((bf16[5,4,128,128]{3,2,1,0:T(8,128)(2,1)}, bf16[5,4,128,128]{3,2,1,0:T(8,128)(2,1)}, u32[]{:S(2)}, u32[]{:S(2)}) %collective-permute-start.11) | collective-permute-done | bytes 655392 | tf_op jit(solution)/shard_map/along_z2/ppermute | solution.py:375
  90.7 1.8 collective-permute-done.16.refs_18_.refs_6_
  93.3 1.8 collective-permute-done.15.refs_17_.refs_5_
  95.2 13.1 %collective-permute-start.19 = (bf16[5,3,128,128]{3,2,1,0:T(8,128)(2,1)}, bf16[5,3,128,128]{3,2,1,0:T(8,128)(2,1)}, u32[]{:S(2)}, u32[]{:S(2)}) collective-permute-start(bf16[5,3,128,128]{3,2,1,0:T(8,128)(2,1)} %shard_map.92), channel_id=1, source_target_pairs={{0,16},{4,20},{8,24},{12,28},{16,0},{20,4},{24,8},{28,12},{1,17},{... | collective-permute-start | bytes 1474568 | tf_op jit(solution)/shard_map/along_z2/ppermute | solution.py:375
  109.3 2.9 collective-permute-start.20
  113.0 1.1 copy-done.23
  120.0 1.1 copy-done.80
  121.1 16.0 %shard_map.90 = (bf16[5,4,128,128]{3,2,1,0:T(8,128)(2,1)S(1)}, bf16[5,4,128,128]{3,2,1,0:T(8,128)(2,1)S(1)}, bf16[5,4,128,128]{3,2,1,0:T(8,128)(2,1)S(1)}, bf16[...) custom-call(s32[4,16,2]{2,1,0:T(8,128)S(1)} %fusion.18.places, ...), custom_call_target="tpu_custom_call" | custom-call | flops 4294967296 | bytes 20000000 | tf_op jit(solution)/shard_map/pallas_call | solution.py:156
  137.2 1.5 copy-done.25
  144.2 4.1 %collective-permute-done.21 = bf16[4,5,4,128,128]{4,3,2,1,0:T(8,128)(2,1)S(1)} collective-permute-done((bf16[4,5,4,128,128]{4,3,2,1,0:T(8,128)(2,1)}, bf16[4,5,4,128,128]{4,3,2,1,0:T(8,128)(2,1)S(1)}, u32[]{:S(2)}, u32[]{:S(2)}) %collective-permute-start.21) | collective-permute-done | bytes 2621472 | tf_op jit(solution)/shard_map/swap/ppermute | solution.py:379
  148.4 2.4 fusion
  150.8 10.2 %collective-permute-start.22 = (bf16[5,4,128,128]{3,2,1,0:T(8,128)(2,1)S(1)}, bf16[5,4,128,128]{3,2,1,0:T(8,128)(2,1)S(1)}, u32[]{:S(2)}, u32[]{:S(2)}) collective-permute-start(bf16[5,4,128,128]{3,2,1,0:T(8,128)(2,1)S(1)} %get-tuple-element.90.refs_21_), channel_id=1, source_target_pairs={{0,16},{4,20},{8,24},{12,28},{16,0},{20,4},{24,8},{28,12},{1,17},{... | collective-permute-start | bytes 1966088 | tf_op jit(solution)/shard_map/along_z2/ppermute | solution.py:375
  161.1 1.4 collective-permute-start.23
  163.3 13.4 %shard_map.95 = (bf16[5,3,128,128]{3,2,1,0:T(8,128)(2,1)S(1)}, bf16[5,3,128,128]{3,2,1,0:T(8,128)(2,1)S(1)}, bf16[5,3,128,128]{3,2,1,0:T(8,128)(2,1)S(1)}, bf16[...) custom-call(s32[3,16,2]{2,1,0:T(8,128)S(1)} %fusion.20.places, ...), custom_call_target="tpu_custom_call" | custom-call | flops 3221225472 | bytes 17500000 | tf_op jit(solution)/shard_map/pallas_call | solution.py:156
  176.8 1.3 copy-done.41
  181.2 18.4 %shard_map.96 = (bf16[2,128,2048]{2,1,0:T(8,128)(2,1)S(1)}, bf16[2,128,2048]{2,1,0:T(8,128)(2,1)S(1)}, bf16[2,128,2048]{2,1,0:T(8,128)(2,1)S(1)}, bf16[2,128,204...) custom-call(s32[7,16,2]{2,1,0:T(8,128)S(1)} %copy-done.78, ...), custom_call_target="tpu_custom_call" | custom-call | flops 3758096384 | bytes 20000000 | tf_op jit(solution)/shard_map/pallas_call | solution.py:267
  200.5 1.1 copy-done.50
  202.5 1.1 copy-done.52
  208.1 3.1 collective-permute-done.28
  211.2 3.1 fusion.8
  214.3 13.1 %collective-permute-start.31 = (bf16[5,3,128,128]{3,2,1,0:T(8,128)(2,1)}, bf16[5,3,128,128]{3,2,1,0:T(8,128)(2,1)S(1)}, u32[]{:S(2)}, u32[]{:S(2)}) collective-permute-start(bf16[5,3,128,128]{3,2,1,0:T(8,128)(2,1)} %shard_map.100), channel_id=1, source_target_pairs={{0,8},{4,12},{8,16},{12,20},{16,24},{20,28},{24,0},{28,4},{1,9},{5... | collective-permute-start | bytes 1474568 | tf_op jit(solution)/shard_map/along_z1/ppermute | solution.py:375
  227.4 5.4 %collective-permute-done.33 = bf16[2,128,2048]{2,1,0:T(8,128)(2,1)} collective-permute-done((bf16[2,128,2048]{2,1,0:T(8,128)(2,1)}, bf16[2,128,2048]{2,1,0:T(8,128)(2,1)}, u32[]{:S(2)}, u32[]{:S(2)}) %collective-permute-start.33) | collective-permute-done | bytes 1048608 | tf_op jit(solution)/shard_map/wide1/ppermute | solution.py:383
  232.9 2.0 fusion.13.refs_1_
  234.9 2.0 fusion.12.refs_0_
  236.9 2.4 collective-permute-done.31.refs_7_.refs_3_.refs_4_
  239.3 9.7 %collective-permute-done.30.refs_6_.refs_2_.refs_3_ = bf16[5,3,128,128]{3,2,1,0:T(8,128)(2,1)S(1)} collective-permute-done((bf16[5,3,128,128]{3,2,1,0:T(8,128)(2,1)}, bf16[5,3,128,128]{3,2,1,0:T(8,128)(2,1)S(1)}, u32[]{:S(2)}, u32[]{:S(2)}) %collective-permute-start.30) | collective-permute-done | bytes 491552 | tf_op jit(solution)/shard_map/along_z3/ppermute | solution.py:375
  250.9 1.4 collective-permute-start.29
  252.3 1.5 collective-permute-start.35
  253.8 1.5 collective-permute-start.34
  255.3 9.7 %collective-permute-done.36 = bf16[128,2048]{1,0:T(8,128)(2,1)} collective-permute-done((bf16[128,2048]{1,0:T(8,128)(2,1)}, bf16[128,2048]{1,0:T(8,128)(2,1)}, u32[]{:S(2)}, u32[]{:S(2)}) %collective-permute-start.36) | collective-permute-done | bytes 524320 | tf_op jit(solution)/shard_map/wide1/ppermute | solution.py:383
  265.0 1.6 fusion.7
  266.6 1.3 fusion.6
  269.7 4.7 %collective-permute-done.29.refs_5_.refs_2_ = bf16[5,3,128,128]{3,2,1,0:T(8,128)(2,1)S(1)} collective-permute-done((bf16[5,3,128,128]{3,2,1,0:T(8,128)(2,1)}, bf16[5,3,128,128]{3,2,1,0:T(8,128)(2,1)S(1)}, u32[]{:S(2)}, u32[]{:S(2)}) %collective-permute-start.29) | collective-permute-done | bytes 491552 | tf_op jit(solution)/shard_map/along_z2/ppermute | solution.py:375
  275.2 10.6 %collective-permute-done.35 = bf16[2,128,2048]{2,1,0:T(8,128)(2,1)} collective-permute-done((bf16[2,128,2048]{2,1,0:T(8,128)(2,1)}, bf16[2,128,2048]{2,1,0:T(8,128)(2,1)}, u32[]{:S(2)}, u32[]{:S(2)}) %collective-permute-start.35) | collective-permute-done | bytes 1048608 | tf_op jit(solution)/shard_map/wide1/ppermute | solution.py:383
  285.8 2.0 fusion.15.refs_1_
  287.8 2.2 fusion.14.refs_0_
  291.0 1.5 collective-permute-start.39
  292.5 1.5 collective-permute-start.40
  294.0 2.0 collective-permute-start.41
  296.0 7.3 %collective-permute-done.39 = bf16[128,2048]{1,0:T(8,128)(2,1)S(1)} collective-permute-done((bf16[128,2048]{1,0:T(8,128)(2,1)}, bf16[128,2048]{1,0:T(8,128)(2,1)S(1)}, u32[]{:S(2)}, u32[]{:S(2)}) %collective-permute-start.39) | collective-permute-done | bytes 524320 | tf_op jit(solution)/shard_map/wide1/ppermute | solution.py:383
  303.3 1.4 bitcast_add_fusion.3
  304.7 1.3 bitcast_add_fusion
  306.4 4.1 %collective-permute-start.42 = (bf16[128,2048]{1,0:T(8,128)(2,1)S(1)}, bf16[128,2048]{1,0:T(8,128)(2,1)S(1)}, u32[]{:S(2)}, u32[]{:S(2)}) collective-permute-start(bf16[128,2048]{1,0:T(8,128)(2,1)S(1)} %fusion.4), channel_id=1, source_target_pairs={{0,24},{4,28},{8,0},{12,4},{16,8},{20,12},{24,16},{28,20},{1,25},{... | collective-permute-start | bytes 1572872 | tf_op jit(solution)/shard_map/along_z3/ppermute | solution.py:375
  310.6 2.6 shard_map.101
  313.2 6.1 %collective-permute-done.42 = bf16[128,2048]{1,0:T(8,128)(2,1)S(1)} collective-permute-done((bf16[128,2048]{1,0:T(8,128)(2,1)S(1)}, bf16[128,2048]{1,0:T(8,128)(2,1)S(1)}, u32[]{:S(2)}, u32[]{:S(2)}) %collective-permute-start.42) | collective-permute-done | bytes 524320 | tf_op jit(solution)/shard_map/along_z3/ppermute | solution.py:375
  (268 shorter events, 43.1 us)
Async XLA Ops:
  0.7 21.5 %collective-permute-start.4 = (bf16[128,2048]{1,0:T(8,128)(2,1)}, bf16[128,2048]{1,0:T(8,128)(2,1)S(1)}, u32[]{:S(2)}, u32[]{:S(2)}) collective-permute-start(bf16[128,2048]{1,0:T(8,128)(2,1)} %param.5), channel_id=1, source_target_pairs={{0,8},{4,12},{8,16},{12,20},{16,24},{20,28},{24,0},{28,4},{1,9},{5... | collective-permute-start | bytes 1572872 | tf_op jit(solution)/shard_map/along_z1/ppermute | solution.py:375
  3.7 25.0 %collective-permute-start.6 = (bf16[128,2048]{1,0:T(8,128)(2,1)}, bf16[128,2048]{1,0:T(8,128)(2,1)S(1)}, u32[]{:S(2)}, u32[]{:S(2)}) collective-permute-start(bf16[128,2048]{1,0:T(8,128)(2,1)} %param.5), channel_id=1, source_target_pairs={{0,24},{4,28},{8,0},{12,4},{16,8},{20,12},{24,16},{28,20},{1,25},{... | collective-permute-start | bytes 1572872 | tf_op jit(solution)/shard_map/along_z3/ppermute | solution.py:375
  6.9 14.1 %copy-start.27 = (bf16[64,2048]{1,0:T(8,128)(2,1)}, bf16[64,2048]{1,0:T(8,128)(2,1)S(1)}, u32[]{:S(2)}) copy-start(bf16[64,2048]{1,0:T(8,128)(2,1)S(1)} %get-tuple-element.110.refs_1_) | copy-start | bytes 786436
  6.9 12.7 %collective-permute-start = (bf16[64,2048]{1,0:T(8,128)(2,1)S(1)}, bf16[64,2048]{1,0:T(8,128)(2,1)S(1)}, u32[]{:S(2)}, u32[]{:S(2)}) collective-permute-start(bf16[64,2048]{1,0:T(8,128)(2,1)S(1)} %get-tuple-element.111.refs_0_), channel_id=1, source_target_pairs={{0,1},{1,0},{2,3},{3,2},{4,5},{5,4},{6,7},{7,6},{8,9},{9,8},{10,11... | collective-permute-start | bytes 786440 | tf_op jit(solution)/shard_map/wide1/ppermute | solution.py:383
  8.6 12.4 %collective-permute-start.1 = (bf16[64,2048]{1,0:T(8,128)(2,1)S(1)}, bf16[64,2048]{1,0:T(8,128)(2,1)S(1)}, u32[]{:S(2)}, u32[]{:S(2)}) collective-permute-start(bf16[64,2048]{1,0:T(8,128)(2,1)S(1)} %get-tuple-element.110.refs_1_), channel_id=1, source_target_pairs={{0,2},{1,3},{2,0},{3,1},{4,6},{5,7},{6,4},{7,5},{8,10},{9,11},{10,... | collective-permute-start | bytes 786440 | tf_op jit(solution)/shard_map/wide2/ppermute | solution.py:383
  20.5 22.0 %collective-permute-start.2 = (bf16[128,2048]{1,0:T(8,128)(2,1)S(1)}, bf16[128,2048]{1,0:T(8,128)(2,1)S(1)}, u32[]{:S(2)}, u32[]{:S(2)}) collective-permute-start(bf16[128,2048]{1,0:T(8,128)(2,1)S(1)} %pad_maximum_fusion.4), channel_id=1, source_target_pairs={{0,2},{1,3},{2,0},{3,1},{4,6},{5,7},{6,4},{7,5},{8,10},{9,11},{10,... | collective-permute-start | bytes 1572872 | tf_op jit(solution)/shard_map/wide2/ppermute | solution.py:383
  21.7 20.8 %collective-permute-start.3 = (bf16[128,2048]{1,0:T(8,128)(2,1)S(1)}, bf16[128,2048]{1,0:T(8,128)(2,1)S(1)}, u32[]{:S(2)}, u32[]{:S(2)}) collective-permute-start(bf16[128,2048]{1,0:T(8,128)(2,1)S(1)} %pad_maximum_fusion.5), channel_id=1, source_target_pairs={{0,1},{1,0},{2,3},{3,2},{4,5},{5,4},{6,7},{7,6},{8,9},{9,8},{10,11... | collective-permute-start | bytes 1572872 | tf_op jit(solution)/shard_map/wide1/ppermute | solution.py:383
  22.1 18.3 %collective-permute-start.5 = (bf16[128,2048]{1,0:T(8,128)(2,1)S(1)}, bf16[128,2048]{1,0:T(8,128)(2,1)S(1)}, u32[]{:S(2)}, u32[]{:S(2)}) collective-permute-start(bf16[128,2048]{1,0:T(8,128)(2,1)S(1)} %collective-permute-done.4), channel_id=1, source_target_pairs={{0,8},{4,12},{8,16},{12,20},{16,24},{20,28},{24,0},{28,4},{1,9},{5... | collective-permute-start | bytes 1572872 | tf_op jit(solution)/shard_map/along_z1/ppermute | solution.py:375
  43.5 17.4 %collective-permute-start.8 = (bf16[192,2048]{1,0:T(8,128)(2,1)}, bf16[192,2048]{1,0:T(8,128)(2,1)S(1)}, u32[]{:S(2)}, u32[]{:S(2)}) collective-permute-start(bf16[192,2048]{1,0:T(8,128)(2,1)} %get-tuple-element.48.refs_7_), channel_id=1, source_target_pairs={{0,2},{1,3},{2,0},{3,1},{4,6},{5,7},{6,4},{7,5},{8,10},{9,11},{10,... | collective-permute-start | bytes 2359304 | tf_op jit(solution)/shard_map/wide2/ppermute | solution.py:383
  45.0 18.7 %collective-permute-start.7 = (bf16[192,2048]{1,0:T(8,128)(2,1)}, bf16[192,2048]{1,0:T(8,128)(2,1)S(1)}, u32[]{:S(2)}, u32[]{:S(2)}) collective-permute-start(bf16[192,2048]{1,0:T(8,128)(2,1)} %get-tuple-element.47.refs_6_), channel_id=1, source_target_pairs={{0,1},{1,0},{2,3},{3,2},{4,5},{5,4},{6,7},{7,6},{8,9},{9,8},{10,11... | collective-permute-start | bytes 2359304 | tf_op jit(solution)/shard_map/wide1/ppermute | solution.py:383
  46.5 43.7 %collective-permute-start.11 = (bf16[5,4,128,128]{3,2,1,0:T(8,128)(2,1)}, bf16[5,4,128,128]{3,2,1,0:T(8,128)(2,1)}, u32[]{:S(2)}, u32[]{:S(2)}) collective-permute-start(bf16[5,4,128,128]{3,2,1,0:T(8,128)(2,1)} %shard_map.86), channel_id=1, source_target_pairs={{0,16},{4,20},{8,24},{12,28},{16,0},{20,4},{24,8},{28,12},{1,17},{... | collective-permute-start | bytes 1966088 | tf_op jit(solution)/shard_map/along_z2/ppermute | solution.py:375
  47.2 13.7 %copy-start.3 = (bf16[192,2048]{1,0:T(8,128)(2,1)S(1)}, bf16[192,2048]{1,0:T(8,128)(2,1)}, u32[]{:S(2)}) copy-start(bf16[192,2048]{1,0:T(8,128)(2,1)} %get-tuple-element.48.refs_7_) | copy-start | bytes 2359300
  47.2 43.0 %collective-permute-start.12 = (bf16[5,4,128,128]{3,2,1,0:T(8,128)(2,1)}, bf16[5,4,128,128]{3,2,1,0:T(8,128)(2,1)}, u32[]{:S(2)}, u32[]{:S(2)}) collective-permute-start(bf16[5,4,128,128]{3,2,1,0:T(8,128)(2,1)} %shard_map.87), channel_id=1, source_target_pairs={{0,8},{4,12},{8,16},{12,20},{16,24},{20,28},{24,0},{28,4},{1,9},{5... | collective-permute-start | bytes 1966088 | tf_op jit(solution)/shard_map/along_z1/ppermute | solution.py:375
  48.7 15.0 %copy-start.2 = (bf16[192,2048]{1,0:T(8,128)(2,1)S(1)}, bf16[192,2048]{1,0:T(8,128)(2,1)}, u32[]{:S(2)}) copy-start(bf16[192,2048]{1,0:T(8,128)(2,1)} %get-tuple-element.47.refs_6_) | copy-start | bytes 2359300
  48.7 41.4 %collective-permute-start.13 = (bf16[5,4,128,128]{3,2,1,0:T(8,128)(2,1)}, bf16[5,4,128,128]{3,2,1,0:T(8,128)(2,1)}, u32[]{:S(2)}, u32[]{:S(2)}) collective-permute-start(bf16[5,4,128,128]{3,2,1,0:T(8,128)(2,1)} %shard_map.88), channel_id=1, source_target_pairs={{0,24},{4,28},{8,0},{12,4},{16,8},{20,12},{24,16},{28,20},{1,25},{... | collective-permute-start | bytes 1966088 | tf_op jit(solution)/shard_map/along_z3/ppermute | solution.py:375
  60.9 52.1 %copy-start.20 = (bf16[192,2048]{1,0:T(8,128)(2,1)}, bf16[192,2048]{1,0:T(8,128)(2,1)S(1)}, u32[]{:S(2)}) copy-start(bf16[192,2048]{1,0:T(8,128)(2,1)S(1)} %collective-permute-done.8.refs_9_) | copy-start | bytes 2359300
  62.2 50.7 %collective-permute-start.10 = (bf16[384,2048]{1,0:T(8,128)(2,1)}, bf16[384,2048]{1,0:T(8,128)(2,1)}, u32[]{:S(2)}, u32[]{:S(2)}) collective-permute-start(bf16[384,2048]{1,0:T(8,128)(2,1)} %pad_maximum_fusion.1), channel_id=1, source_target_pairs={{0,1},{1,0},{2,3},{3,2},{4,5},{5,4},{6,7},{7,6},{8,9},{9,8},{10,11... | collective-permute-start | bytes 4718600 | tf_op jit(solution)/shard_map/wide1/ppermute | solution.py:383
  65.1 47.8 %collective-permute-start.9 = (bf16[384,2048]{1,0:T(8,128)(2,1)}, bf16[384,2048]{1,0:T(8,128)(2,1)}, u32[]{:S(2)}, u32[]{:S(2)}) collective-permute-start(bf16[384,2048]{1,0:T(8,128)(2,1)} %pad_maximum_fusion), channel_id=1, source_target_pairs={{0,2},{1,3},{2,0},{3,1},{4,6},{5,7},{6,4},{7,5},{8,10},{9,11},{10,... | collective-permute-start | bytes 4718600 | tf_op jit(solution)/shard_map/wide2/ppermute | solution.py:383
  90.1 2.4 collective-permute-start.16
  90.2 19.1 %collective-permute-start.14 = (bf16[5,7,128,128]{3,2,1,0:T(8,128)(2,1)}, bf16[5,7,128,128]{3,2,1,0:T(8,128)(2,1)}, u32[]{:S(2)}, u32[]{:S(2)}) collective-permute-start(bf16[5,7,128,128]{3,2,1,0:T(8,128)(2,1)} %shard_map.89.refs_12_.refs_0_.refs_9_), channel_id=1, source_target_pairs={{0,4},{4,0},{8,12},{12,8},{16,20},{20,16},{24,28},{28,24},{1,5},{5... | collective-permute-start | bytes 3440648 | tf_op jit(solution)/shard_map/swap/ppermute | solution.py:379
  90.7 4.5 %collective-permute-start.15 = (bf16[5,4,128,128]{3,2,1,0:T(8,128)(2,1)}, bf16[5,4,128,128]{3,2,1,0:T(8,128)(2,1)}, u32[]{:S(2)}, u32[]{:S(2)}) collective-permute-start(bf16[5,4,128,128]{3,2,1,0:T(8,128)(2,1)} %collective-permute-done.12.refs_2_.refs_13_.refs_1_), channel_id=1, source_target_pairs={{0,4},{4,0},{8,12},{12,8},{16,20},{20,16},{24,28},{28,24},{1,5},{5... | collective-permute-start | bytes 1966088 | tf_op jit(solution)/shard_map/swap/ppermute | solution.py:379
  92.5 15.8 %collective-permute-start.17 = (bf16[5,4,128,128]{3,2,1,0:T(8,128)(2,1)}, bf16[5,4,128,128]{3,2,1,0:T(8,128)(2,1)}, u32[]{:S(2)}, u32[]{:S(2)}) collective-permute-start(bf16[5,4,128,128]{3,2,1,0:T(8,128)(2,1)} %collective-permute-done.13.refs_3_.refs_15_.refs_1_), channel_id=1, source_target_pairs={{0,4},{4,0},{8,12},{12,8},{16,20},{20,16},{24,28},{28,24},{1,5},{5... | collective-permute-start | bytes 1966088 | tf_op jit(solution)/shard_map/swap/ppermute | solution.py:379
  93.3 19.6 %copy-start.13 = (bf16[5,7,128,128]{3,2,1,0:T(8,128)(2,1)S(1)}, bf16[5,7,128,128]{3,2,1,0:T(8,128)(2,1)}, u32[]{:S(2)}) copy-start(bf16[5,7,128,128]{3,2,1,0:T(8,128)(2,1)} %shard_map.89.refs_12_.refs_0_.refs_9_) | copy-start | bytes 3440644
  95.2 47.9 %collective-permute-start.19 = (bf16[5,3,128,128]{3,2,1,0:T(8,128)(2,1)}, bf16[5,3,128,128]{3,2,1,0:T(8,128)(2,1)}, u32[]{:S(2)}, u32[]{:S(2)}) collective-permute-start(bf16[5,3,128,128]{3,2,1,0:T(8,128)(2,1)} %shard_map.92), channel_id=1, source_target_pairs={{0,16},{4,20},{8,24},{12,28},{16,0},{20,4},{24,8},{28,12},{1,17},{... | collective-permute-start | bytes 1474568 | tf_op jit(solution)/shard_map/along_z2/ppermute | solution.py:375
  108.3 34.8 %collective-permute-start.18 = (bf16[5,3,128,128]{3,2,1,0:T(8,128)(2,1)}, bf16[5,3,128,128]{3,2,1,0:T(8,128)(2,1)}, u32[]{:S(2)}, u32[]{:S(2)}) collective-permute-start(bf16[5,3,128,128]{3,2,1,0:T(8,128)(2,1)} %shard_map.91), channel_id=1, source_target_pairs={{0,8},{4,12},{8,16},{12,20},{16,24},{20,28},{24,0},{28,4},{1,9},{5... | collective-permute-start | bytes 1474568 | tf_op jit(solution)/shard_map/along_z1/ppermute | solution.py:375
  109.3 33.8 %collective-permute-start.20 = (bf16[5,3,128,128]{3,2,1,0:T(8,128)(2,1)}, bf16[5,3,128,128]{3,2,1,0:T(8,128)(2,1)}, u32[]{:S(2)}, u32[]{:S(2)}) collective-permute-start(bf16[5,3,128,128]{3,2,1,0:T(8,128)(2,1)} %shard_map.93), channel_id=1, source_target_pairs={{0,24},{4,28},{8,0},{12,4},{16,8},{20,12},{24,16},{28,20},{1,25},{... | collective-permute-start | bytes 1474568 | tf_op jit(solution)/shard_map/along_z3/ppermute | solution.py:375
  143.1 5.2 %collective-permute-start.21 = (bf16[4,5,4,128,128]{4,3,2,1,0:T(8,128)(2,1)}, bf16[4,5,4,128,128]{4,3,2,1,0:T(8,128)(2,1)S(1)}, u32[]{:S(2)}, u32[]{:S(2)}) collective-permute-start(bf16[4,5,4,128,128]{4,3,2,1,0:T(8,128)(2,1)} %shard_map.94), channel_id=1, source_target_pairs={{0,4},{4,0},{8,12},{12,8},{16,20},{20,16},{24,28},{28,24},{1,5},{5... | collective-permute-start | bytes 7864328 | tf_op jit(solution)/shard_map/swap/ppermute | solution.py:379
  143.2 19.3 %collective-permute-start.26 = (bf16[5,3,128,128]{3,2,1,0:T(8,128)(2,1)}, bf16[5,3,128,128]{3,2,1,0:T(8,128)(2,1)S(1)}, u32[]{:S(2)}, u32[]{:S(2)}) collective-permute-start(bf16[5,3,128,128]{3,2,1,0:T(8,128)(2,1)} %collective-permute-done.19.refs_2_.refs_14_.refs_11_), channel_id=1, source_target_pairs={{0,4},{4,0},{8,12},{12,8},{16,20},{20,16},{24,28},{28,24},{1,5},{5... | collective-permute-start | bytes 1474568 | tf_op jit(solution)/shard_map/swap/ppermute | solution.py:379
  143.7 19.5 %collective-permute-start.25 = (bf16[5,3,128,128]{3,2,1,0:T(8,128)(2,1)}, bf16[5,3,128,128]{3,2,1,0:T(8,128)(2,1)S(1)}, u32[]{:S(2)}, u32[]{:S(2)}) collective-permute-start(bf16[5,3,128,128]{3,2,1,0:T(8,128)(2,1)} %collective-permute-done.18.refs_1_.refs_13_.refs_10_), channel_id=1, source_target_pairs={{0,4},{4,0},{8,12},{12,8},{16,20},{20,16},{24,28},{28,24},{1,5},{5... | collective-permute-start | bytes 1474568 | tf_op jit(solution)/shard_map/swap/ppermute | solution.py:379
  143.8 19.4 %collective-permute-start.27 = (bf16[5,3,128,128]{3,2,1,0:T(8,128)(2,1)}, bf16[5,3,128,128]{3,2,1,0:T(8,128)(2,1)S(1)}, u32[]{:S(2)}, u32[]{:S(2)}) collective-permute-start(bf16[5,3,128,128]{3,2,1,0:T(8,128)(2,1)} %collective-permute-done.20.refs_3_.refs_15_.refs_12_), channel_id=1, source_target_pairs={{0,4},{4,0},{8,12},{12,8},{16,20},{20,16},{24,28},{28,24},{1,5},{5... | collective-permute-start | bytes 1474568 | tf_op jit(solution)/shard_map/swap/ppermute | solution.py:379
  148.3 14.8 %copy-start.89 = (s32[7,16,1]{2,1,0:T(8,128)S(1)}, s32[7,16,1]{2,1,0:T(8,128)}, u32[]{:S(2)}) copy-start(s32[7,16,1]{2,1,0:T(8,128)} %copy-done.88) | copy-start | bytes 1348
  148.3 14.8 %copy-start.91 = (s32[7,16,1]{2,1,0:T(8,128)S(1)}, s32[7,16,1]{2,1,0:T(8,128)}, u32[]{:S(2)}) copy-start(s32[7,16,1]{2,1,0:T(8,128)} %copy-done.90) | copy-start | bytes 1348
  148.3 14.9 %copy-start.14 = (bf16[5,7,128,128]{3,2,1,0:T(8,128)(2,1)S(1)}, bf16[5,7,128,128]{3,2,1,0:T(8,128)(2,1)}, u32[]{:S(2)}) copy-start(bf16[5,7,128,128]{3,2,1,0:T(8,128)(2,1)} %shard_map.89.refs_12_.refs_0_.refs_9_) | copy-start | bytes 3440644
  148.3 14.9 %copy-start.21 = (bf16[192,2048]{1,0:T(8,128)(2,1)S(1)}, bf16[192,2048]{1,0:T(8,128)(2,1)}, u32[]{:S(2)}) copy-start(bf16[192,2048]{1,0:T(8,128)(2,1)} %copy-done.20) | copy-start | bytes 2359300
  148.3 14.9 %copy-start.24 = (bf16[192,2048]{1,0:T(8,128)(2,1)S(1)}, bf16[192,2048]{1,0:T(8,128)(2,1)}, u32[]{:S(2)}) copy-start(bf16[192,2048]{1,0:T(8,128)(2,1)} %copy-done.22) | copy-start | bytes 2359300
  148.4 14.9 %copy-start.29 = (bf16[64,2048]{1,0:T(8,128)(2,1)S(1)}, bf16[64,2048]{1,0:T(8,128)(2,1)}, u32[]{:S(2)}) copy-start(bf16[64,2048]{1,0:T(8,128)(2,1)} %copy-done.27) | copy-start | bytes 786436
  148.4 14.9 %copy-start.32 = (bf16[64,2048]{1,0:T(8,128)(2,1)S(1)}, bf16[64,2048]{1,0:T(8,128)(2,1)}, u32[]{:S(2)}) copy-start(bf16[64,2048]{1,0:T(8,128)(2,1)} %copy-done.30) | copy-start | bytes 786436
  148.4 14.9 %copy-start.35 = (bf16[128,2048]{1,0:T(8,128)(2,1)S(1)}, bf16[128,2048]{1,0:T(8,128)(2,1)}, u32[]{:S(2)}) copy-start(bf16[128,2048]{1,0:T(8,128)(2,1)} %copy-done.33) | copy-start | bytes 1572868
  148.4 14.9 %copy-start.38 = (bf16[128,2048]{1,0:T(8,128)(2,1)S(1)}, bf16[128,2048]{1,0:T(8,128)(2,1)}, u32[]{:S(2)}) copy-start(bf16[128,2048]{1,0:T(8,128)(2,1)} %copy-done.36) | copy-start | bytes 1572868
  148.4 14.9 %copy-start.46 = (bf16[64,2048]{1,0:T(8,128)(2,1)S(1)}, bf16[64,2048]{1,0:T(8,128)(2,1)}, u32[]{:S(2)}) copy-start(bf16[64,2048]{1,0:T(8,128)(2,1)} %copy-done.44) | copy-start | bytes 786436
  148.4 14.9 %copy-start.49 = (bf16[64,2048]{1,0:T(8,128)(2,1)S(1)}, bf16[64,2048]{1,0:T(8,128)(2,1)}, u32[]{:S(2)}) copy-start(bf16[64,2048]{1,0:T(8,128)(2,1)} %copy-done.47) | copy-start | bytes 786436
  150.8 25.9 %copy-start.10 = (bf16[5,4,128,128]{3,2,1,0:T(8,128)(2,1)}, bf16[5,4,128,128]{3,2,1,0:T(8,128)(2,1)S(1)}, u32[]{:S(2)}) copy-start(bf16[5,4,128,128]{3,2,1,0:T(8,128)(2,1)S(1)} %get-tuple-element.91.refs_20_.refs_0_) | copy-start | bytes 1966084
  150.8 54.8 %collective-permute-start.22 = (bf16[5,4,128,128]{3,2,1,0:T(8,128)(2,1)S(1)}, bf16[5,4,128,128]{3,2,1,0:T(8,128)(2,1)S(1)}, u32[]{:S(2)}, u32[]{:S(2)}) collective-permute-start(bf16[5,4,128,128]{3,2,1,0:T(8,128)(2,1)S(1)} %get-tuple-element.90.refs_21_), channel_id=1, source_target_pairs={{0,16},{4,20},{8,24},{12,28},{16,0},{20,4},{24,8},{28,12},{1,17},{... | collective-permute-start | bytes 1966088 | tf_op jit(solution)/shard_map/along_z2/ppermute | solution.py:375
  161.1 44.5 %collective-permute-start.23 = (bf16[5,4,128,128]{3,2,1,0:T(8,128)(2,1)S(1)}, bf16[5,4,128,128]{3,2,1,0:T(8,128)(2,1)S(1)}, u32[]{:S(2)}, u32[]{:S(2)}) collective-permute-start(bf16[5,4,128,128]{3,2,1,0:T(8,128)(2,1)S(1)} %get-tuple-element.89.refs_22_), channel_id=1, source_target_pairs={{0,24},{4,28},{8,0},{12,4},{16,8},{20,12},{24,16},{28,20},{1,25},{... | collective-permute-start | bytes 1966088 | tf_op jit(solution)/shard_map/along_z3/ppermute | solution.py:375
  162.5 43.1 %collective-permute-start.24 = (bf16[5,4,128,128]{3,2,1,0:T(8,128)(2,1)S(1)}, bf16[5,4,128,128]{3,2,1,0:T(8,128)(2,1)S(1)}, u32[]{:S(2)}, u32[]{:S(2)}) collective-permute-start(bf16[5,4,128,128]{3,2,1,0:T(8,128)(2,1)S(1)} %get-tuple-element.88.refs_23_), channel_id=1, source_target_pairs={{0,8},{4,12},{8,16},{12,20},{16,24},{20,28},{24,0},{28,4},{1,9},{5... | collective-permute-start | bytes 1966088 | tf_op jit(solution)/shard_map/along_z1/ppermute | solution.py:375
  163.3 17.8 %copy-start.78 = (s32[7,16,2]{2,1,0:T(8,128)S(1)}, s32[7,16,2]{2,1,0:T(8,128)}, u32[]{:S(2)}) copy-start(s32[7,16,2]{2,1,0:T(8,128)} %pad_add_fusion.refs_5_.places) | copy-start | bytes 2692
  163.3 17.8 %copy-start.81 = (bf16[5,4,128,128]{3,2,1,0:T(8,128)(2,1)S(1)}, bf16[5,4,128,128]{3,2,1,0:T(8,128)(2,1)}, u32[]{:S(2)}) copy-start(bf16[5,4,128,128]{3,2,1,0:T(8,128)(2,1)} %copy-done.79) | copy-start | bytes 1966084
  206.9 4.3 %collective-permute-start.28 = (bf16[4,5,3,128,128]{4,3,2,1,0:T(8,128)(2,1)}, bf16[4,5,3,128,128]{4,3,2,1,0:T(8,128)(2,1)}, u32[]{:S(2)}, u32[]{:S(2)}) collective-permute-start(bf16[4,5,3,128,128]{4,3,2,1,0:T(8,128)(2,1)} %shard_map.97), channel_id=1, source_target_pairs={{0,4},{4,0},{8,12},{12,8},{16,20},{20,16},{24,28},{28,24},{1,5},{5... | collective-permute-start | bytes 5898248 | tf_op jit(solution)/shard_map/swap/ppermute | solution.py:379
  206.9 25.9 %collective-permute-start.33 = (bf16[2,128,2048]{2,1,0:T(8,128)(2,1)}, bf16[2,128,2048]{2,1,0:T(8,128)(2,1)}, u32[]{:S(2)}, u32[]{:S(2)}) collective-permute-start(bf16[2,128,2048]{2,1,0:T(8,128)(2,1)} %get-tuple-element.76), channel_id=1, source_target_pairs={{0,1},{1,0},{2,3},{3,2},{4,5},{5,4},{6,7},{7,6},{8,9},{9,8},{10,11... | collective-permute-start | bytes 3145736 | tf_op jit(solution)/shard_map/wide1/ppermute | solution.py:383
  207.6 27.3 %collective-permute-start.32 = (bf16[2,128,2048]{2,1,0:T(8,128)(2,1)}, bf16[2,128,2048]{2,1,0:T(8,128)(2,1)}, u32[]{:S(2)}, u32[]{:S(2)}) collective-permute-start(bf16[2,128,2048]{2,1,0:T(8,128)(2,1)} %get-tuple-element.74), channel_id=1, source_target_pairs={{0,2},{1,3},{2,0},{3,1},{4,6},{5,7},{6,4},{7,5},{8,10},{9,11},{10,... | collective-permute-start | bytes 3145736 | tf_op jit(solution)/shard_map/wide2/ppermute | solution.py:383
  214.3 18.5 %copy-start.53 = (bf16[2,128,2048]{2,1,0:T(8,128)(2,1)S(1)}, bf16[2,128,2048]{2,1,0:T(8,128)(2,1)}, u32[]{:S(2)}) copy-start(bf16[2,128,2048]{2,1,0:T(8,128)(2,1)} %copy-done.52) | copy-start | bytes 3145732
  214.3 25.0 %collective-permute-start.31 = (bf16[5,3,128,128]{3,2,1,0:T(8,128)(2,1)}, bf16[5,3,128,128]{3,2,1,0:T(8,128)(2,1)S(1)}, u32[]{:S(2)}, u32[]{:S(2)}) collective-permute-start(bf16[5,3,128,128]{3,2,1,0:T(8,128)(2,1)} %shard_map.100), channel_id=1, source_target_pairs={{0,8},{4,12},{8,16},{12,20},{16,24},{20,28},{24,0},{28,4},{1,9},{5... | collective-permute-start | bytes 1474568 | tf_op jit(solution)/shard_map/along_z1/ppermute | solution.py:375
  227.4 21.6 %collective-permute-start.30 = (bf16[5,3,128,128]{3,2,1,0:T(8,128)(2,1)}, bf16[5,3,128,128]{3,2,1,0:T(8,128)(2,1)S(1)}, u32[]{:S(2)}, u32[]{:S(2)}) collective-permute-start(bf16[5,3,128,128]{3,2,1,0:T(8,128)(2,1)} %shard_map.99), channel_id=1, source_target_pairs={{0,24},{4,28},{8,0},{12,4},{16,8},{20,12},{24,16},{28,20},{1,25},{... | collective-permute-start | bytes 1474568 | tf_op jit(solution)/shard_map/along_z3/ppermute | solution.py:375
  249.8 15.2 %collective-permute-start.36 = (bf16[128,2048]{1,0:T(8,128)(2,1)}, bf16[128,2048]{1,0:T(8,128)(2,1)}, u32[]{:S(2)}, u32[]{:S(2)}) collective-permute-start(bf16[128,2048]{1,0:T(8,128)(2,1)} %get-tuple-element.77.refs_2_), channel_id=1, source_target_pairs={{0,1},{1,0},{2,3},{3,2},{4,5},{5,4},{6,7},{7,6},{8,9},{9,8},{10,11... | collective-permute-start | bytes 1572872 | tf_op jit(solution)/shard_map/wide1/ppermute | solution.py:383
  250.4 16.2 %collective-permute-start.37 = (bf16[128,2048]{1,0:T(8,128)(2,1)}, bf16[128,2048]{1,0:T(8,128)(2,1)S(1)}, u32[]{:S(2)}, u32[]{:S(2)}) collective-permute-start(bf16[128,2048]{1,0:T(8,128)(2,1)} %get-tuple-element.78.refs_3_), channel_id=1, source_target_pairs={{0,2},{1,3},{2,0},{3,1},{4,6},{5,7},{6,4},{7,5},{8,10},{9,11},{10,... | collective-permute-start | bytes 1572872 | tf_op jit(solution)/shard_map/wide2/ppermute | solution.py:383
  250.9 23.5 %collective-permute-start.29 = (bf16[5,3,128,128]{3,2,1,0:T(8,128)(2,1)}, bf16[5,3,128,128]{3,2,1,0:T(8,128)(2,1)S(1)}, u32[]{:S(2)}, u32[]{:S(2)}) collective-permute-start(bf16[5,3,128,128]{3,2,1,0:T(8,128)(2,1)} %shard_map.98), channel_id=1, source_target_pairs={{0,16},{4,20},{8,24},{12,28},{16,0},{20,4},{24,8},{28,12},{1,17},{... | collective-permute-start | bytes 1474568 | tf_op jit(solution)/shard_map/along_z2/ppermute | solution.py:375
  252.3 33.5 %collective-permute-start.35 = (bf16[2,128,2048]{2,1,0:T(8,128)(2,1)}, bf16[2,128,2048]{2,1,0:T(8,128)(2,1)}, u32[]{:S(2)}, u32[]{:S(2)}) collective-permute-start(bf16[2,128,2048]{2,1,0:T(8,128)(2,1)} %get-tuple-element.81), channel_id=1, source_target_pairs={{0,1},{1,0},{2,3},{3,2},{4,5},{5,4},{6,7},{7,6},{8,9},{9,8},{10,11... | collective-permute-start | bytes 3145736 | tf_op jit(solution)/shard_map/wide1/ppermute | solution.py:383
  253.8 34.0 %collective-permute-start.34 = (bf16[2,128,2048]{2,1,0:T(8,128)(2,1)}, bf16[2,128,2048]{2,1,0:T(8,128)(2,1)}, u32[]{:S(2)}, u32[]{:S(2)}) collective-permute-start(bf16[2,128,2048]{2,1,0:T(8,128)(2,1)} %get-tuple-element.79), channel_id=1, source_target_pairs={{0,2},{1,3},{2,0},{3,1},{4,6},{5,7},{6,4},{7,5},{8,10},{9,11},{10,... | collective-permute-start | bytes 3145736 | tf_op jit(solution)/shard_map/wide2/ppermute | solution.py:383
  268.9 16.8 %copy-start.87 = (bf16[2,128,2048]{2,1,0:T(8,128)(2,1)S(1)}, bf16[2,128,2048]{2,1,0:T(8,128)(2,1)}, u32[]{:S(2)}) copy-start(bf16[2,128,2048]{2,1,0:T(8,128)(2,1)} %get-tuple-element.80) | copy-start | bytes 3145732
  275.2 15.0 %collective-permute-start.38 = (bf16[128,2048]{1,0:T(8,128)(2,1)}, bf16[128,2048]{1,0:T(8,128)(2,1)S(1)}, u32[]{:S(2)}, u32[]{:S(2)}) collective-permute-start(bf16[128,2048]{1,0:T(8,128)(2,1)} %get-tuple-element.82), channel_id=1, source_target_pairs={{0,8},{4,12},{8,16},{12,20},{16,24},{20,28},{24,0},{28,4},{1,9},{5... | collective-permute-start | bytes 1572872 | tf_op jit(solution)/shard_map/along_z1/ppermute | solution.py:375
  291.0 12.3 %collective-permute-start.39 = (bf16[128,2048]{1,0:T(8,128)(2,1)}, bf16[128,2048]{1,0:T(8,128)(2,1)S(1)}, u32[]{:S(2)}, u32[]{:S(2)}) collective-permute-start(bf16[128,2048]{1,0:T(8,128)(2,1)} %get-tuple-element.83), channel_id=1, source_target_pairs={{0,1},{1,0},{2,3},{3,2},{4,5},{5,4},{6,7},{7,6},{8,9},{9,8},{10,11... | collective-permute-start | bytes 1572872 | tf_op jit(solution)/shard_map/wide1/ppermute | solution.py:383
  292.5 12.2 %collective-permute-start.40 = (bf16[128,2048]{1,0:T(8,128)(2,1)}, bf16[128,2048]{1,0:T(8,128)(2,1)S(1)}, u32[]{:S(2)}, u32[]{:S(2)}) collective-permute-start(bf16[128,2048]{1,0:T(8,128)(2,1)} %get-tuple-element.84), channel_id=1, source_target_pairs={{0,2},{1,3},{2,0},{3,1},{4,6},{5,7},{6,4},{7,5},{8,10},{9,11},{10,... | collective-permute-start | bytes 1572872 | tf_op jit(solution)/shard_map/wide2/ppermute | solution.py:383
  294.0 12.3 %collective-permute-start.41 = (bf16[128,2048]{1,0:T(8,128)(2,1)S(1)}, bf16[128,2048]{1,0:T(8,128)(2,1)S(1)}, u32[]{:S(2)}, u32[]{:S(2)}) collective-permute-start(bf16[128,2048]{1,0:T(8,128)(2,1)S(1)} %copy-done.86), channel_id=1, source_target_pairs={{0,24},{4,28},{8,0},{12,4},{16,8},{20,12},{24,16},{28,20},{1,25},{... | collective-permute-start | bytes 1572872 | tf_op jit(solution)/shard_map/along_z3/ppermute | solution.py:375
  306.4 12.9 %collective-permute-start.42 = (bf16[128,2048]{1,0:T(8,128)(2,1)S(1)}, bf16[128,2048]{1,0:T(8,128)(2,1)S(1)}, u32[]{:S(2)}, u32[]{:S(2)}) collective-permute-start(bf16[128,2048]{1,0:T(8,128)(2,1)S(1)} %fusion.4), channel_id=1, source_target_pairs={{0,24},{4,28},{8,0},{12,4},{16,8},{20,12},{24,16},{28,20},{1,25},{... | collective-permute-start | bytes 1572872 | tf_op jit(solution)/shard_map/along_z3/ppermute | solution.py:375
  (71 other events, 189.2 us)
